TPU v7x, 32 devices: a whole 2x2x4 slice. The times are simulated.
32 devices in a mesh: seq: 4 (over y, x), mp: 8 (over z, core).
Axes of the slice: x: 2, y: 2, z: 4, core: 2. Of those that a mesh axis runs over, the one named last changes fastest.
Arguments:
- layer_in: bfloat16 [8, 1536, 1024], P('mp', 'seq'), may hold values from -6 to 6
- out_grad: bfloat16 [8, 1536, 1024], P('mp', 'seq'), may hold values from -6 to 6
- seq_lengths: int32 [8, 3], P('mp'), may hold values from 1 to 1248, 1536 in all within a row
- dealing: int32 [8, 1536], P('mp'), may hold values from 0 to 1535, each once within a row
- log_decay: float32 [8, 1536, 8], P('mp', 'seq'), may hold values from -0.75 to 0
- w_qkv: bfloat16 [1024, 4096], P(('seq', 'mp')), may hold values from -0.1875 to 0.1875
- w_out_gate: bfloat16 [1024, 2048], P(('seq', 'mp')), may hold values from -0.1875 to 0.1875
- w_beta: bfloat16 [1024, 8], P(('seq', 'mp')), may hold values from -0.1875 to 0.1875
- conv_w: bfloat16 [4096, 4], P(('seq', 'mp')), may hold values from -3 to 3
- gain_in: bfloat16 [1024], P(('seq', 'mp')), may hold values from 0.099609375 to 1.8984375
- gain_o: bfloat16 [256], P(('seq', 'mp')), may hold values from 0.099609375 to 1.8984375
- w_out: bfloat16 [2048, 1024], P(None, ('seq', 'mp')), may hold values from -0.125 to 0.125
- gain_mid: bfloat16 [1024], P(('seq', 'mp')), may hold values from 0.099609375 to 1.8984375
- w_gate_up: bfloat16 [1024, 5632], P(('seq', 'mp')), may hold values from -0.1875 to 0.1875
- w_down: bfloat16 [2816, 1024], P(None, ('seq', 'mp')), may hold values from -0.109375 to 0.109375
Outputs:
- mixed_out: bfloat16 [8, 1536, 1024], P('mp', 'seq')
- input_grad: bfloat16 [8, 1536, 1024], P('mp', 'seq')
- grad_w_qkv: float32 [1024, 4096], P(('seq', 'mp'))
- grad_w_out_gate: float32 [1024, 2048], P(('seq', 'mp'))
- grad_w_beta: float32 [1024, 8], P(('seq', 'mp'))
- grad_conv_w: float32 [4096, 4], P(('seq', 'mp'))
- grad_gain_in: float32 [1024], P(('seq', 'mp'))
- grad_gain_o: float32 [256], P(('seq', 'mp'))
- grad_w_out: float32 [2048, 1024], P(None, ('seq', 'mp'))
- grad_gain_mid: float32 [1024], P(('seq', 'mp'))
- grad_w_gate_up: float32 [1024, 5632], P(('seq', 'mp'))
- grad_w_down: float32 [2816, 1024], P(None, ('seq', 'mp'))
Inputs may be any that keep to these rules, and one draw needn't show every extreme that they name: `seq_lengths`: each row holds the lengths of 3 sequences packed in this order, summing to 1536; the largest is exactly 1248. `dealing`: each row is a permutation of the group's rows.
All inputs are finite; a program needn't handle non-finite values.
Results may differ from a plain program's by a relative error of at most 0.012.
The roundings to bfloat16 on the way count: a program that leaves them out, or rounds other values in their place, can miss the bound.
Values may be sent and summed in bfloat16 or wider, within the bound.
No kernel may reach another device: no remote copies, remote signals or barrier semaphores. Data moves between devices by JAX's collectives and lax.ppermute only.
A program may use at most 320 MiB of HBM per device.

v0:
```python
import functools

import jax
import jax.numpy as jnp
from jax import lax
from jax.experimental import pallas as pl
from jax.experimental.pallas import tpu as pltpu
from jax.sharding import PartitionSpec as P

HEAD_COUNT = 8
DK = 128
DV = 256
BLOCK = 128
FORWARD_STEP = 6
BACKWARD_STEP = 2
F32 = jnp.float32
BF16 = jnp.bfloat16


def mm(left, right):
    return jnp.dot(left.astype(BF16), right.astype(BF16), preferred_element_type=F32)


def mm_nt(left, right):
    return lax.dot_general(
        left.astype(BF16),
        right.astype(BF16),
        (((1,), (1,)), ((), ())),
        preferred_element_type=F32,
    )


def mm_tn(left, right):
    return lax.dot_general(
        left.astype(BF16),
        right.astype(BF16),
        (((0,), (0,)), ((), ())),
        preferred_element_type=F32,
    )


def masks():
    rows = lax.broadcasted_iota(jnp.int32, (BLOCK, BLOCK), 0)
    cols = lax.broadcasted_iota(jnp.int32, (BLOCK, BLOCK), 1)
    return rows, cols


def unit_inverses(mats, rows, cols):
    ident = (rows == cols).astype(F32)
    near = (rows // 16) == (cols // 16)
    power = [jnp.where(near, a, 0.0) for a in mats]
    result = [ident - p for p in power]
    span = 2
    while span < 16:
        power = [mm(p, p) for p in power]
        result = [t + mm(t, p) for t, p in zip(result, power)]
        span *= 2
    size = 16
    while size < BLOCK:
        off = ((rows // (2 * size)) == (cols // (2 * size))) & ((rows // size) != (cols // size))
        reach = [mm(jnp.where(off, a, 0.0), t) for a, t in zip(mats, result)]
        result = [t - mm(t, x) for t, x in zip(result, reach)]
        size *= 2
    return result


def convolve(ext_ref, conv_ref, col_ref, start, first, width):
    cols = pl.ds(first, width)
    total = ext_ref[pl.ds(16 + start, BLOCK), cols] * conv_ref[3:4, cols]
    for tap in range(3):
        keep = col_ref[pl.ds(start, BLOCK), tap : tap + 1]
        total += ext_ref[pl.ds(13 + tap + start, BLOCK), cols] * keep * conv_ref[tap : tap + 1, cols]
    return total


def column(col_ref, start, index):
    return col_ref[pl.ds(start, BLOCK), index : index + 1]


def strength(logit_ref, start, head, heads):
    return jax.nn.sigmoid(column(logit_ref, start, head))


def exact_nt(left, right):
    left_high, right_high = left.astype(BF16), right.astype(BF16)
    left_low = left - left_high.astype(F32)
    right_low = right - right_high.astype(F32)
    return mm_nt(left_high, right_high) + (mm_nt(left_high, right_low) + mm_nt(left_low, right_high))


def decay_matrix(col_ref, row_ref, start, head, heads, rows, cols):
    cum_i = column(col_ref, start, 5 + head)
    cum_j = row_ref[head : head + 1, pl.ds(start, BLOCK)]
    seg_i = column(col_ref, start, 3)
    seg_j = row_ref[heads : heads + 1, pl.ds(start, BLOCK)]
    within = (rows >= cols) & (seg_i == seg_j)
    return jnp.where(within, jnp.exp(jnp.where(within, cum_i - cum_j, 0.0)), 0.0)


def silu(values):
    return values * jax.nn.sigmoid(values)


def forward_kernel(
    heads, edge_ref, proj_ref, conv_ref, col_ref, row_ref, logit_ref, *refs,
):
    o_ref, s_ref, n_ref, t_ref, w_ref, p_ref, pre_ref, ext_ref, state_ref = refs[-9:]
    steps = proj_ref.shape[0] // BLOCK

    @pl.when(pl.program_id(0) == 0)
    def _():
        state_ref[...] = jnp.zeros_like(state_ref)

    ext_ref[:16, :] = edge_ref[...].astype(F32)
    ext_ref[16:, :] = proj_ref[...].astype(F32)
    rows, cols = masks()
    strict = rows > cols
    units = [(g, h) for g in range(steps) for h in range(heads)]
    queries, keys, values, mats, decays, betas = {}, {}, {}, [], {}, {}
    for g, h in units:
        start = g * BLOCK

        def taken(first, width):
            value = convolve(ext_ref, conv_ref, col_ref, start, first, width)
            pre_ref[pl.ds(start, BLOCK), first : first + width] = value
            return value

        queries[g, h] = silu(taken(h * DK, DK))
        raw = silu(taken((heads + h) * DK, DK))
        keys[g, h] = raw * lax.rsqrt(jnp.sum(raw * raw, axis=1, keepdims=True) + 1e-06)
        values[g, h] = silu(taken(2 * heads * DK + h * DV, DV))
        decays[g, h] = decay_matrix(col_ref, row_ref, start, h, heads, rows, cols)
        betas[g, h] = strength(logit_ref, start, h, heads)
        beta = betas[g, h]
        inner = mm_nt(keys[g, h], keys[g, h])
        mats.append(jnp.where(strict, beta * inner * decays[g, h], 0.0))
    inverses = unit_inverses(mats, rows, cols)
    umats, wmats, pmats, boundary, reads = {}, {}, {}, {}, {}
    for (g, h), inverse in zip(units, inverses):
        start = g * BLOCK
        beta = betas[g, h]
        elog = column(col_ref, start, 5 + heads + h)
        flog = column(col_ref, start, 5 + 2 * heads + h)
        inverse = inverse.astype(BF16)
        t_ref[g, h] = inverse
        umats[g, h] = mm(inverse, beta * values[g, h])
        wmats[g, h] = mm(inverse, (beta * elog) * keys[g, h]).astype(BF16)
        w_ref[g, h] = wmats[g, h]
        pmats[g, h] = (exact_nt(queries[g, h], keys[g, h]) * decays[g, h]).astype(BF16)
        p_ref[g, h] = pmats[g, h]
        boundary[g, h] = (keys[g, h] * flog).T.astype(BF16)
        reads[g, h] = (queries[g, h] * elog).astype(BF16)
    for g in range(steps):
        start = g * BLOCK
        for h in range(heads):
            state = state_ref[h]
            low = state.astype(BF16)
            s_ref[g, h] = low
            news = (umats[g, h] - mm(wmats[g, h], low)).astype(BF16)
            n_ref[g, h] = news
            carried = col_ref[pl.ds(start + BLOCK - 1, 1), 5 + heads + h : 6 + heads + h]
            state_ref[h] = carried * state + mm(boundary[g, h], news)
            output = mm(reads[g, h], low) + mm(pmats[g, h], news)
            o_ref[pl.ds(start, BLOCK), h * DV : (h + 1) * DV] = output.astype(BF16)


def backward_kernel(
    heads, edge_ref, proj_ref, conv_ref, col_ref, row_ref, logit_ref,
    s_ref, n_ref, t_ref, w_ref, p_ref, pre_ref, do_ref, *refs,
):
    grad_ref, gconv_ref, ext_ref, shift_ref, dstate_ref, head_ref = refs[-6:]
    count = proj_ref.shape[0]
    steps = count // BLOCK
    channels = proj_ref.shape[1]

    @pl.when(pl.program_id(0) == 0)
    def _():
        dstate_ref[...] = jnp.zeros_like(dstate_ref)
        head_ref[...] = jnp.zeros_like(head_ref)
        gconv_ref[...] = jnp.zeros_like(gconv_ref)

    ext_ref[:16, :] = edge_ref[...].astype(F32)
    ext_ref[16:, :] = proj_ref[...].astype(F32)
    for tap in range(3):
        shift_ref[tap, count : count + 8, :] = head_ref[tap]
    rows, cols = masks()
    strict = rows > cols
    units = [(g, h) for g in reversed(range(steps)) for h in range(heads)]
    queries, keys, pre, reads, first, gains = {}, {}, {}, {}, {}, {}
    for g, h in units:
        start = g * BLOCK

        def taken(first, width):
            return pre_ref[pl.ds(start, BLOCK), first : first + width]

        elog = column(col_ref, start, 5 + heads + h)
        out_grad = do_ref[pl.ds(start, BLOCK), h * DV : (h + 1) * DV]
        queries[g, h] = silu(taken(h * DK, DK))
        raw = silu(taken((heads + h) * DK, DK))
        scale = lax.rsqrt(jnp.sum(raw * raw, axis=1, keepdims=True) + 1e-06)
        keys[g, h] = (raw * scale, scale)
        first[g, h] = mm_tn(p_ref[g, h], out_grad)
        gains[g, h] = mm_tn(queries[g, h] * elog, out_grad)
    news_grads, state_grads = {}, {}
    for g in reversed(range(steps)):
        start = g * BLOCK
        for h in range(heads):
            flog = column(col_ref, start, 5 + 2 * heads + h)
            dstate = dstate_ref[h]
            low = dstate.astype(BF16)
            state_grads[g, h] = low
            news_grad = (first[g, h] + mm(keys[g, h][0] * flog, low)).astype(BF16)
            news_grads[g, h] = news_grad
            carried = col_ref[pl.ds(start + BLOCK - 1, 1), 5 + heads + h : 6 + heads + h]
            dstate_ref[h] = gains[g, h] + carried * dstate - mm_tn(w_ref[g, h], news_grad)
    lane = lax.broadcasted_iota(jnp.int32, (BLOCK, 128), 1)

    def through_conv(g, first_col, width, grad):
        start = g * BLOCK
        cols_ = pl.ds(first_col, width)
        value = pre_ref[pl.ds(start, BLOCK), first_col : first_col + width]
        gate = jax.nn.sigmoid(value)
        grad = grad * (gate * (1.0 + value * (1.0 - gate)))
        shift_ref[3, pl.ds(start, BLOCK), cols_] = grad * conv_ref[3:4, cols_]
        sums = []
        for tap in range(3):
            kept = grad * col_ref[pl.ds(start, BLOCK), tap : tap + 1]
            shift_ref[tap, pl.ds(start, BLOCK), cols_] = kept * conv_ref[tap : tap + 1, cols_]
            sums.append(
                jnp.sum(kept * ext_ref[pl.ds(13 + tap + start, BLOCK), cols_], axis=0, keepdims=True)
            )
        sums.append(
            jnp.sum(grad * ext_ref[pl.ds(16 + start, BLOCK), cols_], axis=0, keepdims=True)
        )
        for tap in range(4):
            gconv_ref[tap : tap + 1, cols_] += sums[tap]

    logit_grads = {}
    for g, h in units:
        start = g * BLOCK
        beta = strength(logit_ref, start, h, heads)
        elog = column(col_ref, start, 5 + heads + h)
        flog = column(col_ref, start, 5 + 2 * heads + h)
        key, scale = keys[g, h]
        query = queries[g, h]
        out_grad = do_ref[pl.ds(start, BLOCK), h * DV : (h + 1) * DV]
        decay = decay_matrix(col_ref, row_ref, start, h, heads, rows, cols)
        key_low = key.astype(BF16)
        inner = mm_nt(key_low, key_low) * decay
        news, state, dstate = n_ref[g, h], s_ref[g, h], state_grads[g, h]
        rhs_grad = mm_tn(t_ref[g, h], news_grads[g, h])
        rhs_low = rhs_grad.astype(BF16)
        within = (mm_nt(out_grad, news) * decay).astype(BF16)
        mat_grad = jnp.where(strict, -mm_nt(rhs_low, news), 0.0)
        pair = (mat_grad * beta * decay).astype(BF16)
        back = mm_nt(rhs_low, state)
        q_grad = mm(within, key_low) + elog * mm_nt(out_grad, state)
        k_grad = (
            mm_tn(within, query)
            + mm(pair, key_low)
            + mm_tn(pair, key_low)
            + flog * mm_nt(news, dstate)
            - (beta * elog) * back
        )
        value = silu(pre_ref[pl.ds(start, BLOCK), pl.ds(2 * heads * DK + h * DV, DV)])
        beta_grad = (
            jnp.sum(mat_grad * inner - elog * (key * back), axis=1, keepdims=True)
            + jnp.sum(rhs_grad * value, axis=1, keepdims=True)
        )
        logit_grads[g, h] = beta_grad * beta * (1.0 - beta)
        raw_grad = scale * (k_grad - key * jnp.sum(k_grad * key, axis=1, keepdims=True))
        through_conv(g, h * DK, DK, q_grad)
        through_conv(g, (heads + h) * DK, DK, raw_grad)
        through_conv(g, 2 * heads * DK + h * DV, DV, beta * rhs_grad)
    for g in range(steps):
        total = jnp.zeros((BLOCK, 128), F32)
        for h in range(heads):
            total = jnp.where(lane == h, logit_grads[g, h], total)
        grad_ref[pl.ds(g * BLOCK, BLOCK), channels : channels + 128] = total.astype(BF16)
        grad_ref[pl.ds(g * BLOCK, BLOCK), channels + 128 :] = jnp.zeros((BLOCK, 128), BF16)
    total = shift_ref[3, :count, :]
    for tap in range(3):
        total += shift_ref[tap, pl.ds(3 - tap, count), :]
    grad_ref[:, :channels] = total.astype(BF16)
    for tap in range(3):
        head_ref[tap] = shift_ref[tap, :8, :]


def saved_shapes(blocks, heads):
    return (
        jax.ShapeDtypeStruct((blocks, heads, DK, DV), BF16),
        jax.ShapeDtypeStruct((blocks, heads, BLOCK, DV), BF16),
        jax.ShapeDtypeStruct((blocks, heads, BLOCK, BLOCK), BF16),
        jax.ShapeDtypeStruct((blocks, heads, BLOCK, DK), BF16),
        jax.ShapeDtypeStruct((blocks, heads, BLOCK, BLOCK), BF16),
        jax.ShapeDtypeStruct((blocks * BLOCK, heads * (2 * DK + DV)), F32),
    )


def saved_specs(shapes, per_step, index):
    return [
        pl.BlockSpec((per_step,) + shape.shape[1:], lambda i: (index(i), 0, 0, 0))
        for shape in shapes[:-1]
    ] + [pl.BlockSpec((per_step * BLOCK, shapes[-1].shape[1]), lambda i: (index(i), 0))]


def common_specs(step, channels, logits, index):
    return [
        pl.BlockSpec((16, channels), lambda i: (jnp.maximum(index(i) * (step // 16) - 1, 0), 0)),
        pl.BlockSpec((step, channels), lambda i: (index(i), 0)),
        pl.BlockSpec((8, channels), lambda i: (0, 0)),
        pl.BlockSpec((step, 128), lambda i: (index(i), 0)),
        pl.BlockSpec((8, step), lambda i: (0, index(i))),
        pl.BlockSpec((step, logits), lambda i: (index(i), 0)),
    ]


MIB = 1024 * 1024
VMEM_BYTES = 24 * MIB
SMALL_COST = pl.CostEstimate(flops=10**6, bytes_accessed=10**6, transcendentals=0)
ANYWHERE = pl.BlockSpec(memory_space=pl.ANY)
WHOLE = pl.BlockSpec(memory_space=pltpu.VMEM)
SCALAR = pl.BlockSpec(memory_space=pltpu.SMEM)


def params(limit=VMEM_BYTES):
    return pltpu.CompilerParams(dimension_semantics=("arbitrary",), vmem_limit_bytes=limit)


def forward_recurrence(proj, conv, cols, rows, logits, heads, tokens):
    count, channels = proj.shape
    step = BLOCK * FORWARD_STEP
    shapes = saved_shapes(count // BLOCK, heads)
    index = lambda i: i
    return pl.pallas_call(
        functools.partial(forward_kernel, heads),
        grid=(count // step,),
        in_specs=common_specs(step, channels, 128, index) + [ANYWHERE] * len(tokens),
        out_specs=[pl.BlockSpec((step, heads * DV), lambda i: (i, 0))] + saved_specs(shapes, FORWARD_STEP, index),
        out_shape=(jax.ShapeDtypeStruct((count, heads * DV), BF16),) + shapes,
        scratch_shapes=[
            pltpu.VMEM((step + 16, channels), F32),
            pltpu.VMEM((heads, DK, DV), F32),
        ],
        compiler_params=params(56 * MIB),
        cost_estimate=SMALL_COST,
        name="recurrence_forward",
    )(proj, proj, conv, cols, rows, logits, *tokens)


def backward_recurrence(proj, conv, cols, rows, logits, saved, out_grad, heads, tokens):
    count, channels = proj.shape
    step = BLOCK * BACKWARD_STEP
    last = count // step - 1
    index = lambda i: last - i
    return pl.pallas_call(
        functools.partial(backward_kernel, heads),
        grid=(count // step,),
        in_specs=common_specs(step, channels, 128, index)
        + saved_specs(saved, BACKWARD_STEP, index)
        + [pl.BlockSpec((step, heads * DV), lambda i: (index(i), 0))]
        + [ANYWHERE] * len(tokens),
        out_specs=[
            pl.BlockSpec((step, channels + 256), lambda i: (index(i), 0)),
            pl.BlockSpec((8, channels), lambda i: (0, 0)),
        ],
        out_shape=(
            jax.ShapeDtypeStruct((count, channels + 256), BF16),
            jax.ShapeDtypeStruct((8, channels), F32),
        ),
        scratch_shapes=[
            pltpu.VMEM((step + 16, channels), F32),
            pltpu.VMEM((4, step + 8, channels), F32),
            pltpu.VMEM((heads, DK, DV), F32),
            pltpu.VMEM((3, 8, channels), F32),
        ],
        compiler_params=params(56 * MIB),
        cost_estimate=SMALL_COST,
        name="recurrence_backward",
    )(proj, proj, conv, cols, rows, logits, *saved, out_grad, *tokens)


def project_kernel(
    channels, chunks, handed, rank_ref, gain_ref, w_ref, col_ref, *refs
):
    x_refs = refs[:chunks]
    normed_ref, gate_ref, proj_ref, logit_ref, all_ref = refs[chunks + handed : chunks + handed + 5]
    rows_ref = refs[-1]
    step = pl.program_id(0)
    count = x_refs[0].shape[0]

    @pl.when(step == 0)
    def _():
        width = w_ref.shape[0] * w_ref.shape[2]
        for k in range(w_ref.shape[1]):
            place = pl.ds(pl.multiple_of((rank_ref[0] ^ k) * width, width), width)
            all_ref[place, :] = w_ref[:, k].reshape(width, w_ref.shape[3])

    for k in range(chunks):

        @pl.when(step == k)
        def _():
            x = x_refs[k][...].astype(F32)
            scale = lax.rsqrt(jnp.mean(x * x, axis=1, keepdims=True) + 1e-05)
            normed = (x * scale * gain_ref[...]).astype(BF16)
            normed_ref[...] = normed
            total = mm(normed, all_ref[...])
            gates = gate_ref.shape[1]
            gate_ref[...] = total[:, :gates]
            logit = total[:, gates + channels :]
            high = logit.astype(BF16)
            place = slice(k * count, (k + 1) * count)
            rows_ref[place, : channels + 128] = total[:, gates:].astype(BF16)
            rows_ref[place, channels + 128 :] = (logit - high.astype(F32)).astype(BF16)

    @pl.when(step >= chunks)
    def _():
        order = lax.broadcasted_iota(jnp.int32, (proj_ref.shape[0], rows_ref.shape[0]), 1)
        picked = (col_ref[:, 4:5].astype(jnp.int32) == order).astype(F32)
        packed = mm(picked, rows_ref[...])
        proj_ref[...] = packed[:, :channels].astype(BF16)
        logit_ref[...] = packed[:, channels : channels + 128] + packed[:, channels + 128 :]


def project(rank, x_chunks, gain, weights, cols, channels, passed, tokens):
    count, width = x_chunks[0].shape
    total = count * len(x_chunks)
    gates = weights.shape[3] - channels - 128
    chunks = total // count
    block = total // 2
    first = lambda i: jnp.minimum(i, chunks - 1)
    later = lambda i: jnp.maximum(i - chunks, 0)
    outs = pl.pallas_call(
        functools.partial(project_kernel, channels, chunks, len(passed) + len(tokens)),
        grid=(chunks + total // block,),
        in_specs=[
            SCALAR,
            pl.BlockSpec((1, width), lambda i: (0, 0)),
            pl.BlockSpec(weights.shape, lambda i: (0, 0, 0, 0)),
            pl.BlockSpec((block, 128), lambda i: (later(i), 0)),
        ]
        + [pl.BlockSpec((count, width), lambda i: (0, 0))] * chunks
        + [ANYWHERE] * (len(passed) + len(tokens)),
        out_specs=[
            pl.BlockSpec((count, width), lambda i: (first(i), 0)),
            pl.BlockSpec((count, gates), lambda i: (first(i), 0)),
            pl.BlockSpec((block, channels), lambda i: (later(i), 0)),
            pl.BlockSpec((block, 128), lambda i: (later(i), 0)),
            pl.BlockSpec((width, weights.shape[3]), lambda i: (0, 0)),
        ]
        + [ANYWHERE] * len(passed),
        out_shape=[
            jax.ShapeDtypeStruct((total, width), BF16),
            jax.ShapeDtypeStruct((total, gates), F32),
            jax.ShapeDtypeStruct((total, channels), BF16),
            jax.ShapeDtypeStruct((total, 128), F32),
            jax.ShapeDtypeStruct((width, weights.shape[3]), BF16),
        ]
        + [jax.ShapeDtypeStruct(p.shape, p.dtype) for p in passed],
        input_output_aliases={4 + chunks + i: 5 + i for i in range(len(passed))},
        scratch_shapes=[pltpu.VMEM((total, channels + 256), BF16)],
        compiler_params=params(56 * MIB),
        cost_estimate=SMALL_COST,
        name="project",
    )(rank, gain, weights, cols, *x_chunks, *passed, *tokens)
    return outs[:5], outs[5:]


def gate_kernel(heads, count, first, o_ref, place_ref, gate_ref, gain_ref, *refs):
    chunks = place_ref.shape[1] // count
    dealt_ref, chunk_refs = refs[first], refs[first + 1 : first + 1 + chunks]
    for k, chunk_ref in enumerate(chunk_refs):
        order = lax.broadcasted_iota(jnp.int32, (count, o_ref.shape[0]), 0) + k * count
        picked = (place_ref[...].astype(jnp.int32) == order).astype(F32)
        rows = mm(picked, o_ref[...])
        place = pl.ds(k * count, count)
        dealt_ref[place, :] = rows.astype(BF16)
        for h in range(heads):
            lanes = slice(h * DV, (h + 1) * DV)
            value = rows[:, lanes]
            scale = lax.rsqrt(jnp.mean(value * value, axis=1, keepdims=True) + 1e-05)
            gated = value * scale * gain_ref[...] * silu(gate_ref[place, lanes])
            chunk_ref[:, lanes] = gated.astype(BF16)


def gate_rows(output, place, gate_logit, gain, count, heads, passed, tokens):
    total, cols = output.shape
    chunks = total // count
    others = len(passed) + len(tokens)
    outs = pl.pallas_call(
        functools.partial(gate_kernel, heads, count, others),
        in_specs=[WHOLE] * 4 + [ANYWHERE] * others,
        out_specs=[WHOLE] * (chunks + 1) + [ANYWHERE] * len(passed),
        out_shape=[jax.ShapeDtypeStruct((total, cols), BF16)]
        + [jax.ShapeDtypeStruct((count, cols), BF16)] * chunks
        + [jax.ShapeDtypeStruct(a.shape, a.dtype) for a in passed],
        input_output_aliases={4 + i: 1 + chunks + i for i in range(len(passed))},
        compiler_params=pltpu.CompilerParams(vmem_limit_bytes=VMEM_BYTES),
        cost_estimate=SMALL_COST,
        name="gate_rows",
    )(output, place, gate_logit, gain, *passed, *tokens)
    return outs[0], outs[1 : 1 + chunks], outs[1 + chunks :]


def ungate_kernel(heads, chunks, outs, dealt_ref, col_ref, gate_ref, gain_ref, *refs):
    grad_refs = refs[:chunks]
    gate_grad_ref, o_grad_ref, gain_grad_ref, rows_ref = *refs[outs : outs + 3], refs[-1]
    count = grad_refs[0].shape[0]
    total = dealt_ref.shape[0]
    sums = jnp.zeros((1, DV), F32)
    for k in range(chunks):
        place = pl.ds(k * count, count)
        for h in range(heads):
            lanes = slice(h * DV, (h + 1) * DV)
            value = dealt_ref[place, lanes].astype(F32)
            grad = grad_refs[k][:, lanes].astype(F32)
            logit = gate_ref[place, lanes]
            scale = lax.rsqrt(jnp.mean(value * value, axis=1, keepdims=True) + 1e-05)
            unit = value * scale
            gate = jax.nn.sigmoid(logit)
            slid = logit * gate
            sums += jnp.sum(grad * unit * slid, axis=0, keepdims=True)
            grad = grad * gain_ref[...]
            slope = gate * (1.0 + logit * (1.0 - gate))
            gate_grad_ref[place, lanes] = (grad * unit * slope).astype(BF16)
            grad = grad * slid
            inner = jnp.mean(grad * unit, axis=1, keepdims=True)
            rows_ref[place, lanes] = (scale * (grad - unit * inner)).astype(BF16)
    gain_grad_ref[...] = sums
    for k in range(chunks):
        place = pl.ds(k * count, count)
        order = lax.broadcasted_iota(jnp.int32, (count, total), 1)
        picked = (col_ref[place, 4:5].astype(jnp.int32) == order).astype(F32)
        o_grad_ref[place, :] = mm(picked, rows_ref[...]).astype(BF16)


def ungate_rows(dealt_rows, cols, gate_logit, gain, grads, heads, passed, tokens):
    total, width = dealt_rows.shape
    whole = pl.BlockSpec(memory_space=pltpu.VMEM)
    first = 4 + len(grads)
    outs = pl.pallas_call(
        functools.partial(ungate_kernel, heads, len(grads), len(grads) + len(passed) + len(tokens)),
        in_specs=[whole] * first + [ANYWHERE] * (len(passed) + len(tokens)),
        out_specs=[whole] * 3 + [ANYWHERE] * len(passed),
        out_shape=[
            jax.ShapeDtypeStruct((total, width), BF16),
            jax.ShapeDtypeStruct((total, width), BF16),
            jax.ShapeDtypeStruct((1, DV), F32),
        ]
        + [jax.ShapeDtypeStruct(p.shape, p.dtype) for p in passed],
        input_output_aliases={first + i: 3 + i for i in range(len(passed))},
        scratch_shapes=[pltpu.VMEM((total, width), BF16)],
        compiler_params=pltpu.CompilerParams(vmem_limit_bytes=VMEM_BYTES),
        cost_estimate=SMALL_COST,
        name="ungate_rows",
    )(dealt_rows, cols, gate_logit, gain, *grads, *passed, *tokens)
    return outs[:3], list(outs[3:])


def turned_sums(values):
    sums = jnp.sum(values, axis=1, keepdims=True)
    return jnp.broadcast_to(sums, (values.shape[0], 128)).T[:1]


def put_rows(total, split, core_ref, refs):
    total = total.astype(BF16)
    if split is None:
        refs[0][...] = total
        return
    halves = total.reshape(*split, 2, -1, total.shape[1])
    for core in range(2):

        @pl.when(core_ref[0] == core)
        def _():
            refs[0][...] = halves[:, :, core]
            refs[1][...] = halves[:, :, 1 - core]


def row_outputs(split, width, cols, tile):
    if split is None:
        shape, block = (width, cols), (width, tile)
        spec = pl.BlockSpec(block, lambda i: (0, i))
        return [spec], [jax.ShapeDtypeStruct(shape, BF16)]
    shape = (*split, width // (2 * split[0] * split[1]))
    spec = pl.BlockSpec((*shape, tile), lambda i: (0, 0, 0, i))
    return [spec] * 2, [jax.ShapeDtypeStruct((*shape, cols), BF16)] * 2


def unpack_kernel(split, heads, words_ref, grad_ref, gates_ref, place_ref, normed_ref, w_ref, conv_ref, gain_ref, mid_ref, o_ref, first_sums_ref, *refs):
    count = 2 if split else 1
    dealt_ref, sums_ref = refs[-4 - count], refs[-3 - count]
    row_refs, small_ref, picked_ref = refs[-2 - count : -2], refs[-2], refs[-1]
    step = pl.program_id(0)
    total = grad_ref.shape[0]
    gates = gates_ref.shape[1]
    tile = grad_ref.shape[1] // 2

    @pl.when(step == 0)
    def _():
        part = 256
        for k in range(total // part):
            order = lax.broadcasted_iota(jnp.int32, (part, total), 0) + k * part
            picked = (place_ref[...].astype(jnp.int32) == order).astype(F32)
            picked_ref[k * part : (k + 1) * part, :] = picked.astype(BF16)
        dealt_ref[:, :gates] = gates_ref[...]
        dealt_ref[:, gates : gates + tile] = mm(picked_ref[...], grad_ref[:, :tile]).astype(BF16)
        share = mm(normed_ref[...], dealt_ref[:, gates : gates + tile])
        weights = w_ref[:, gates : gates + tile].astype(F32)
        sums_ref[...] = first_sums_ref[...] + turned_sums(share * weights)
        put_rows(share, split, words_ref, row_refs)

    @pl.when(step == 1)
    def _():
        dealt_ref[:, gates + tile :] = mm(picked_ref[...], grad_ref[:, tile:]).astype(BF16)
        share = mm(normed_ref[...], dealt_ref[:, gates + tile :])
        used = w_ref.shape[1] - gates - tile
        weights = w_ref[:, gates + tile :].astype(F32)
        sums_ref[...] += turned_sums(share[:, :used] * weights)
        if split:
            devices, rows = 2 * split[0] * split[1], share.shape[0] // (2 * split[0] * split[1])
            gin = sums_ref[...] / gain_ref[...]
            small_ref[...] = jnp.zeros_like(small_ref)
            gin = jnp.concatenate([gin[:, j * 128 : (j + 1) * 128] for j in range(8)], 0)
            mid = jnp.concatenate([mid_ref[:, j * 128 : (j + 1) * 128] for j in range(8)], 0)
            for d in range(devices):
                small_ref[d * rows + 4 : d * rows + 5, :] = o_ref[:, :128]
                small_ref[d * rows + 5 : d * rows + 6, :] = o_ref[:, 128:]
                small_ref[d * rows + 8 : d * rows + 16, :] = mid
                small_ref[d * rows + 16 : d * rows + 24, :] = gin
            rank = words_ref[2]
            keys = heads * DK // 128
            vals = heads * DV // 128
            owners = [rank * keys + j for j in range(keys)]
            owners += [HEAD_COUNT * DK // 128 + rank * keys + j for j in range(keys)]
            owners += [2 * HEAD_COUNT * DK // 128 + rank * vals + j for j in range(vals)]
            for j, owner in enumerate(owners):
                place = pl.ds(pl.multiple_of(owner * rows, rows), 8)
                old = small_ref[place, :]
                taps = lax.broadcasted_iota(jnp.int32, (8, 128), 0) < 4
                small_ref[place, :] = jnp.where(taps, conv_ref[:, j * 128 : (j + 1) * 128], old)
            share = jnp.concatenate([share[:, :-128], small_ref[...]], 1)
        put_rows(share, split, words_ref, row_refs)


def unpack(split, words, grad, gate_grad, place, normed, weights, g_conv, gain, g_mid, g_o, sums, heads, tokens):
    total = grad.shape[0]
    cols = grad.shape[1] + gate_grad.shape[1]
    width = normed.shape[0]
    operands = (grad, gate_grad, place, normed, weights, g_conv, gain, g_mid, g_o, sums)
    specs, shapes = row_outputs(split, width, grad.shape[1], grad.shape[1] // 2)
    return pl.pallas_call(
        functools.partial(unpack_kernel, split, heads),
        grid=(2,),
        in_specs=[SCALAR]
        + [pl.BlockSpec(a.shape, lambda i: (0, 0)) for a in operands]
        + [ANYWHERE] * len(tokens),
        out_specs=[
            pl.BlockSpec((total, cols), lambda i: (0, 0)),
            pl.BlockSpec((1, width), lambda i: (0, 0)),
        ]
        + specs,
        out_shape=[
            jax.ShapeDtypeStruct((total, cols), BF16),
            jax.ShapeDtypeStruct((1, width), F32),
        ]
        + shapes,
        scratch_shapes=[pltpu.VMEM((width, 128), F32), pltpu.VMEM((total, total), BF16)],
        compiler_params=params(),
        cost_estimate=SMALL_COST,
        name="unpack",
    )(words, *operands, *tokens)


def unproject_kernel(chunks, first, grad_ref, w_ref, *refs):
    part_refs, turned_ref = refs[first : first + chunks], refs[-1]
    step = pl.program_id(0)

    @pl.when(step == 0)
    def _():
        turned_ref[...] = w_ref[...].T

    part = mm(grad_ref[:, : turned_ref.shape[0]], turned_ref[...])
    for k in range(chunks):

        @pl.when(step == k)
        def _():
            part_refs[k][...] = part.astype(BF16)


def unproject(grad, weights, count, passed, tokens):
    total, cols = grad.shape
    width = weights.shape[0]
    chunks = total // count
    outs = pl.pallas_call(
        functools.partial(unproject_kernel, chunks, len(passed) + len(tokens)),
        grid=(chunks,),
        in_specs=[
            pl.BlockSpec((count, cols), lambda i: (i, 0)),
            pl.BlockSpec(weights.shape, lambda i: (0, 0)),
        ]
        + [ANYWHERE] * (len(passed) + len(tokens)),
        out_specs=[pl.BlockSpec((count, width), lambda i: (0, 0))] * chunks
        + [ANYWHERE] * len(passed),
        out_shape=[jax.ShapeDtypeStruct((count, width), BF16)] * chunks
        + [jax.ShapeDtypeStruct(p.shape, p.dtype) for p in passed],
        input_output_aliases={2 + i: chunks + i for i in range(len(passed))},
        scratch_shapes=[pltpu.VMEM(weights.shape[::-1], BF16)],
        compiler_params=params(56 * MIB),
        cost_estimate=SMALL_COST,
        name="unproject",
    )(grad, weights, *passed, *tokens)
    return list(outs[:chunks]), list(outs[chunks:])


def hand_kernel(*refs):
    refs[-1][...] = jnp.zeros_like(refs[-1])


def handed(passed, tokens):
    outs = pl.pallas_call(
        hand_kernel,
        in_specs=[ANYWHERE] * (len(passed) + len(tokens)),
        out_specs=[ANYWHERE] * len(passed) + [WHOLE],
        out_shape=[jax.ShapeDtypeStruct(p.shape, p.dtype) for p in passed]
        + [jax.ShapeDtypeStruct((8, 128), F32)],
        input_output_aliases={i: i for i in range(len(passed))},
        cost_estimate=SMALL_COST,
        name="handed",
    )(*passed, *tokens)
    return outs[:-1]


def weight_grad_kernel(split, tiles, sums, words_ref, *refs):
    row_refs = refs[-2:] if split else refs[-1:]
    step = pl.program_id(0)
    for tile, pairs in enumerate(tiles):

        @pl.when(step == tile)
        def _():
            total = mm_tn(refs[pairs[0][0]][...], refs[pairs[0][1]][...])
            for left, right in pairs[1:]:
                total += mm_tn(refs[left][...], refs[right][...])
            put_rows(total, split, words_ref, row_refs)
            if sums is not None and tile == 0:
                refs[sums[1]][...] = turned_sums(total * refs[sums[0]][...].astype(F32))


def weight_grad(split, words, groups, tile, tokens, weights=None, limit=VMEM_BYTES):
    width = groups[0][0][0].shape[1]
    operands, specs, tiles = [words], [SCALAR], []
    first = 0
    for lefts, rights in groups:
        count = rights[0].shape[1] // tile
        base = len(operands) - 1
        for left in lefts:
            operands.append(left)
            specs.append(pl.BlockSpec((rights[0].shape[0], width), lambda i: (0, 0)))
        for right in rights:
            operands.append(right)
            specs.append(
                pl.BlockSpec(
                    (right.shape[0], tile),
                    lambda i, first=first, count=count: (0, jnp.clip(i - first, 0, count - 1)),
                )
            )
        tiles += [[(base + k, base + len(lefts) + k) for k in range(len(lefts))]] * count
        first += count
    sums = None
    out_specs, out_shapes = row_outputs(split, width, first * tile, tile)
    if weights is not None:
        operands.append(weights)
        specs.append(pl.BlockSpec((width, tile), lambda i: (0, 0)))
        sums = (len(operands) - 2, len(operands) - 1 + len(tokens))
        out_specs = [pl.BlockSpec((1, width), lambda i: (0, 0))] + out_specs
        out_shapes = [jax.ShapeDtypeStruct((1, width), F32)] + out_shapes
    return pl.pallas_call(
        functools.partial(weight_grad_kernel, split, tiles, sums),
        grid=(first,),
        in_specs=specs + [ANYWHERE] * len(tokens),
        out_specs=out_specs,
        out_shape=out_shapes,
        compiler_params=params(limit),
        cost_estimate=SMALL_COST,
        name="weight_grad",
    )(*operands, *tokens)


def join_kernel(pairs, *refs):
    for chip in range(refs[0].shape[1]):
        place = 0
        for k in range(pairs):
            keep_ref, got_ref = refs[2 * k], refs[2 * k + 1]
            width = keep_ref.shape[3]
            total = keep_ref[:, chip].astype(F32) + got_ref[:, chip].astype(F32)
            refs[-1][chip, :, :, place : place + width] = total.astype(BF16)
            place += width


def joined(pairs, tokens):
    seq_count, chips, rows, _ = pairs[0][0].shape
    cols = sum(keep.shape[3] for keep, _ in pairs)
    return pl.pallas_call(
        functools.partial(join_kernel, len(pairs)),
        in_specs=[WHOLE] * (2 * len(pairs)) + [ANYWHERE] * len(tokens),
        out_specs=WHOLE,
        out_shape=jax.ShapeDtypeStruct((chips, seq_count, rows, cols), BF16),
        compiler_params=pltpu.CompilerParams(vmem_limit_bytes=VMEM_BYTES),
        cost_estimate=SMALL_COST,
        name="joined",
    )(*[a for pair in pairs for a in pair], *tokens)


def layer_kernel(chunks, w_ref, low_ref, *refs):
    weights = w_ref[...].T
    count = low_ref.shape[0]
    refs[chunks][...] = mm(refs[0][...], weights).astype(BF16)
    for k in range(1, chunks):
        refs[chunks + k][:count, :] = low_ref[...]
        refs[chunks + k][count:, :] = mm(refs[k][...], weights).astype(BF16)


def layer_products(hiddens, weights, low):
    count, wide = hiddens[0].shape
    width = weights.shape[0]
    chunks = len(hiddens)
    rows = [count] + [2 * count] * (chunks - 1)
    return pl.pallas_call(
        functools.partial(layer_kernel, chunks),
        grid=(1,),
        in_specs=[
            pl.BlockSpec((width, wide), lambda i: (0, weights.shape[1] // wide - 1)),
            pl.BlockSpec((count, width), lambda i: (0, 0)),
        ]
        + [pl.BlockSpec((count, wide), lambda i: (0, 0))] * chunks,
        out_specs=[pl.BlockSpec((r, width), lambda i: (0, 0)) for r in rows],
        out_shape=[jax.ShapeDtypeStruct((r, width), BF16) for r in rows],
        compiler_params=params(),
        cost_estimate=SMALL_COST,
        name="layer_products",
    )(weights, low, *hiddens)


def position_kernel(heads, chunks, words_ref, lengths_ref, order_ref, decay_ref, *refs):
    col_ref, row_ref, place_ref, cum_ref = refs[-4:]
    total = order_ref.shape[1]
    count = total // chunks
    blocks, near = total // BLOCK, count // BLOCK
    rank = words_ref[2]
    ends = [lengths_ref[0]]
    for e in range(1, lengths_ref.shape[0]):
        ends.append(ends[-1] + lengths_ref[e])

    def segment(position):
        found = jnp.zeros(position.shape, jnp.int32)
        for end in ends:
            found += (position >= end).astype(jnp.int32)
        return jnp.where(position < 0, -1, found)

    for k in range(chunks):
        for h in range(heads):
            for b in range(near):
                value = jnp.zeros((1, BLOCK), F32)
                for part in range(3):
                    row = (part * heads + h) * near + b
                    value += decay_ref[k, row : row + 1, :].astype(F32)
                cum_ref[pl.ds(h * blocks + (rank ^ k) * near + b, 1), :] = value
    rows, cols = masks()
    upper = (rows <= cols).astype(F32)
    cums = jnp.dot(
        cum_ref[...], upper, precision=lax.Precision.HIGHEST, preferred_element_type=F32
    )
    order = order_ref[...]
    chunk = jnp.zeros_like(order)
    for k in range(1, chunks):
        chunk += (order >= k * count).astype(jnp.int32)
    place = (order + ((chunk ^ rank) - chunk) * count).astype(F32)
    place_ref[...] = place
    row_ref[...] = jnp.zeros_like(row_ref)
    lane = lax.broadcasted_iota(jnp.int32, (1, BLOCK), 1)
    for b in range(blocks):
        position = lane + b * BLOCK
        here = segment(position)
        low, high = jnp.full((1, BLOCK), b * BLOCK - 1), jnp.full((1, BLOCK), b * BLOCK + BLOCK - 1)
        keep_in = (here == segment(low)).astype(F32)
        keep_out = (here == segment(high)).astype(F32)
        found = [(segment(position - 3 + tap) == here).astype(F32) for tap in range(3)]
        found += [here.astype(F32), place[:, b * BLOCK : (b + 1) * BLOCK]]
        mine = [cums[h * blocks + b : h * blocks + b + 1, :] for h in range(heads)]
        found += mine
        found += [jnp.exp(c) * keep_in for c in mine]
        found += [jnp.exp(c[:, BLOCK - 1 :] - c) * keep_out for c in mine]
        found.append(jnp.zeros((128 - len(found), BLOCK), F32))
        col_ref[b * BLOCK : (b + 1) * BLOCK, :] = jnp.concatenate(found, 0).T
        for h in range(heads):
            row_ref[h : h + 1, b * BLOCK : (b + 1) * BLOCK] = mine[h]
        row_ref[heads : heads + 1, b * BLOCK : (b + 1) * BLOCK] = here.astype(F32)


def positions(words, lengths, order, decays, heads, tokens):
    total = order.shape[1]
    return pl.pallas_call(
        functools.partial(position_kernel, heads, decays.shape[0]),
        in_specs=[SCALAR, SCALAR, WHOLE, WHOLE] + [ANYWHERE] * len(tokens),
        out_specs=[WHOLE] * 3,
        out_shape=(
            jax.ShapeDtypeStruct((total, 128), F32),
            jax.ShapeDtypeStruct((8, total), F32),
            jax.ShapeDtypeStruct((1, total), F32),
        ),
        scratch_shapes=[pltpu.VMEM((heads * total // BLOCK, BLOCK), F32)],
        cost_estimate=SMALL_COST,
        compiler_params=pltpu.CompilerParams(vmem_limit_bytes=VMEM_BYTES),
        name="positions",
    )(words, lengths, order, decays, *tokens)


def out_rows_kernel(others, words_ref, mine_ref, normed_ref, *refs):
    out_ref, turned_ref = refs[-2:]
    core, chip = words_ref[0], words_ref[1]
    if others:
        chunks, chips, rows, _ = mine_ref.shape
        for k in range(chunks):
            for j in range(chips):
                device = k * 2 * chips + 2 * (chip ^ j)
                for ref, side in ((mine_ref, core), (refs[0], 1 - core)):
                    place = pl.ds(pl.multiple_of((device + side) * rows, rows), rows)
                    out_ref[place, :] = ref[k, j]
    else:
        out_ref[...] = mine_ref[...]
    turned_ref[...] = normed_ref[...].T


def out_rows(words, mine, others, normed, rows, tokens):
    return pl.pallas_call(
        functools.partial(out_rows_kernel, len(others)),
        in_specs=[SCALAR] + [WHOLE] * (2 + len(others)) + [ANYWHERE] * len(tokens),
        out_specs=[WHOLE] * 2,
        out_shape=(
            jax.ShapeDtypeStruct((rows, mine.shape[-1]), BF16),
            jax.ShapeDtypeStruct(normed.shape[::-1], BF16),
        ),
        compiler_params=pltpu.CompilerParams(vmem_limit_bytes=VMEM_BYTES),
        cost_estimate=SMALL_COST,
        name="out_rows",
    )(words, mine, normed, *others, *tokens)


def ffn_rows_kernel(words_ref, ffn_ref, *refs):
    width = ffn_ref.shape[0] * ffn_ref.shape[2]
    for k in range(ffn_ref.shape[1]):
        place = pl.ds(pl.multiple_of((words_ref[2] ^ k) * width, width), width)
        refs[-1][place, :] = ffn_ref[:, k].reshape(width, ffn_ref.shape[3])


def ffn_rows(words, ffn, tokens):
    return pl.pallas_call(
        ffn_rows_kernel,
        in_specs=[SCALAR, WHOLE] + [ANYWHERE] * len(tokens),
        out_specs=WHOLE,
        out_shape=jax.ShapeDtypeStruct((ffn.shape[0] * ffn.shape[1] * ffn.shape[2], ffn.shape[3]), BF16),
        compiler_params=pltpu.CompilerParams(vmem_limit_bytes=VMEM_BYTES),
        cost_estimate=SMALL_COST,
        name="ffn_rows",
    )(words, ffn, *tokens)


def out_project_kernel(chunks, rank_ref, x_ref, gain_ref, w_ref, *refs):
    residual_ref, mid_ref, all_ref = refs[-3:]
    rank = rank_ref[0]
    for k in range(chunks):
        width = refs[k].shape[1]
        all_ref[:, pl.ds(pl.multiple_of((rank ^ k) * width, width), width)] = refs[k][...]
    residual = x_ref[...].astype(F32) + mm_nt(all_ref[...], w_ref[...])
    residual_ref[...] = residual
    scale = lax.rsqrt(jnp.mean(residual * residual, axis=1, keepdims=True) + 1e-05)
    mid_ref[...] = (residual * scale * gain_ref[...]).astype(BF16)


def out_project(rank, x, gain, attn, weights):
    count, width = x.shape
    return pl.pallas_call(
        functools.partial(out_project_kernel, len(attn)),
        in_specs=[SCALAR] + [WHOLE] * (3 + len(attn)),
        out_specs=[WHOLE] * 2,
        out_shape=(
            jax.ShapeDtypeStruct((count, width), F32),
            jax.ShapeDtypeStruct((count, width), BF16),
        ),
        scratch_shapes=[pltpu.VMEM((count, weights.shape[1]), BF16)],
        compiler_params=pltpu.CompilerParams(vmem_limit_bytes=VMEM_BYTES),
        cost_estimate=SMALL_COST,
        name="out_project",
    )(rank, x, gain, weights, *attn)


def mid_back_kernel(chunks, handed, rank_ref, grad_ref, residual_ref, gain_ref, w_ref, *refs):
    parts = refs[:chunks]
    outs, all_ref = refs[chunks + handed :], refs[-1]
    res_grad_ref, low_ref, gain_grad_ref, chunk_refs = outs[0], outs[1], outs[2], outs[3 : 3 + chunks]
    rank = rank_ref[0]
    mid_grad = parts[0][...].astype(F32)
    for k in range(1, chunks):
        mid_grad += parts[k][...].astype(F32)
    residual = residual_ref[...]
    scale = lax.rsqrt(jnp.mean(residual * residual, axis=1, keepdims=True) + 1e-05)
    unit = residual * scale
    gain_grad_ref[...] = jnp.sum(mid_grad * unit, axis=0, keepdims=True)
    scaled = mid_grad * gain_ref[...]
    inner = jnp.mean(scaled * unit, axis=1, keepdims=True)
    res_grad = grad_ref[...].astype(F32) + scale * (scaled - unit * inner)
    res_grad_ref[...] = res_grad
    low = res_grad.astype(BF16)
    low_ref[...] = low
    all_ref[...] = mm(low, w_ref[...]).astype(BF16)
    for k in range(chunks):
        width = chunk_refs[k].shape[1]
        chunk_refs[k][...] = all_ref[:, pl.ds(pl.multiple_of((rank ^ k) * width, width), width)]


def mid_back(rank, grad, residual, gain, parts, weights, passed):
    count, width = residual.shape
    chunks = len(parts)
    wide = weights.shape[1]
    first = 5 + chunks
    outs = pl.pallas_call(
        functools.partial(mid_back_kernel, chunks, len(passed)),
        in_specs=[SCALAR] + [WHOLE] * (first - 1) + [ANYWHERE] * len(passed),
        out_specs=[WHOLE] * (3 + chunks) + [ANYWHERE] * len(passed),
        out_shape=[
            jax.ShapeDtypeStruct((count, width), F32),
            jax.ShapeDtypeStruct((count, width), BF16),
            jax.ShapeDtypeStruct((1, width), F32),
        ]
        + [jax.ShapeDtypeStruct((count, wide // chunks), BF16)] * chunks
        + [jax.ShapeDtypeStruct(p.shape, p.dtype) for p in passed],
        input_output_aliases={first + i: 3 + chunks + i for i in range(len(passed))},
        scratch_shapes=[pltpu.VMEM((count, wide), BF16)],
        compiler_params=pltpu.CompilerParams(vmem_limit_bytes=VMEM_BYTES),
        cost_estimate=SMALL_COST,
        name="mid_back",
    )(rank, grad, residual, gain, weights, *parts, *passed)
    return (*outs[:3], outs[3 : 3 + chunks], list(outs[3 + chunks :]))


def in_back_kernel(chunks, x_ref, res_grad_ref, gain_ref, *refs):
    x = x_ref[...].astype(F32)
    grad = refs[0][...].astype(F32)
    for k in range(1, chunks):
        grad += refs[k][...].astype(F32)
    scale = lax.rsqrt(jnp.mean(x * x, axis=1, keepdims=True) + 1e-05)
    unit = x * scale
    scaled = grad * gain_ref[...]
    inner = jnp.mean(scaled * unit, axis=1, keepdims=True)
    refs[-1][...] = (res_grad_ref[...] + scale * (scaled - unit * inner)).astype(BF16)


def in_back(x, res_grad, gain, parts, tokens):
    return pl.pallas_call(
        functools.partial(in_back_kernel, len(parts)),
        in_specs=[WHOLE] * (3 + len(parts)) + [ANYWHERE] * len(tokens),
        out_specs=WHOLE,
        out_shape=jax.ShapeDtypeStruct(x.shape, BF16),
        compiler_params=pltpu.CompilerParams(vmem_limit_bytes=VMEM_BYTES),
        cost_estimate=SMALL_COST,
        name="in_back",
    )(x, res_grad, gain, *parts, *tokens)


def swapped(value, axis, mask):
    devices = lax.axis_size(axis)
    return lax.ppermute(value, axis, [(i, i ^ mask) for i in range(devices)])


def pinned(value, other):
    return value + 0 * other[:1, :1].astype(value.dtype)


def spread(value):
    return [value] + [swapped(value, "seq", k) for k in range(1, lax.axis_size("seq"))]


def returned(chunks):
    return [chunks[0]] + [swapped(chunks[k], "seq", k) for k in range(1, len(chunks))]


class RowSum:
    def __init__(self, outs):
        self.outs = list(outs)

    def pair(self):
        if len(self.outs) == 2:
            self.got = swapped(self.outs[1], "mp", 1)

    def join(self, *tokens):
        seq_count, mp_count = lax.axis_size("seq"), lax.axis_size("mp")
        if len(self.outs) == 1:
            (grad,) = self.outs
            cols = grad.shape[1]
            parts = grad.astype(F32).reshape(seq_count, mp_count, -1, cols).transpose(1, 0, 2, 3)
            own = lax.psum_scatter(parts.reshape(-1, cols), "mp", scatter_dimension=0, tiled=True)
            self.half = grad
            self.parts = own.reshape(1, seq_count, -1, cols)
            return
        self.half = joined([(self.outs[0], self.got)], tokens)
        self.between()

    def between(self):
        mp_count = lax.axis_size("mp")
        groups = [list(range(core, mp_count, 2)) for core in range(2)]
        self.parts = lax.all_to_all(self.half, "mp", 0, 0, axis_index_groups=groups, tiled=True)

    def beside(self, other):
        if len(self.outs) == 1:
            both = RowSum([jnp.concatenate([self.outs[0], other.outs[0]], 1)])
            both.join()
            return both
        both = RowSum([])
        both.half = joined([(s.outs[0], s.got) for s in (self, other)], [])
        both.between()
        return both


def row_sums(sums, tokens):
    groups = [part.parts for part in sums]
    shape = groups[0].shape[1:3]
    cols = [group.shape[3] for group in groups]

    def kernel(*refs):
        place = 0
        for ref, width in zip(refs, cols):
            total = ref[0].astype(F32)
            for k in range(1, ref.shape[0]):
                total += ref[k].astype(F32)
            refs[-1][:, :, place : place + width] = total.astype(BF16)
            place = place + width

    return pl.pallas_call(
        kernel,
        in_specs=[WHOLE] * len(groups) + [ANYWHERE] * len(tokens),
        out_specs=WHOLE,
        out_shape=jax.ShapeDtypeStruct(shape + (sum(cols),), BF16),
        cost_estimate=SMALL_COST,
        compiler_params=pltpu.CompilerParams(vmem_limit_bytes=VMEM_BYTES),
        name="row_sums",
    )(*groups, *tokens)


def finish_kernel(heads, wide, half, rows, pieces_ref, *refs):
    qkv_ref, gate_ref, beta_ref, conv_ref, out_ref, gu_ref, down_ref, small_ref = refs
    chunks = pieces_ref.shape[0]
    keys, vals = heads * DK, heads * DV
    ffn, mix = 0, 3 * wide
    gate_first, first, out_first = mix, mix + vals, pieces_ref.shape[2] - vals

    def piece(j, start, width):
        return pieces_ref[j, :, start : start + width].astype(F32)

    for j in range(chunks):
        gate_ref[:, j * vals : (j + 1) * vals] = piece(j, gate_first, vals)
        qkv_ref[:, j * keys : (j + 1) * keys] = piece(j, first, keys)
        place = chunks * keys + j * keys
        qkv_ref[:, place : place + keys] = piece(j, first + keys, keys)
        place = 2 * chunks * keys + j * vals
        qkv_ref[:, place : place + vals] = piece(j, first + 2 * keys, vals)
        out_ref[:, j * vals : (j + 1) * vals] = piece(j, out_first, vals)
        beta = piece(j, first + 2 * keys + vals, 128)
        beta_ref[:, j * heads : (j + 1) * heads] = beta[:, :heads]
    small = piece(0, out_first - 128, 128)
    for j in range(1, chunks):
        small += piece(j, out_first - 128, 128)
    small_ref[...] = small
    conv_ref[...] = small[: conv_ref.shape[0]]
    for part in range(3):
        whole = jnp.concatenate(
            [piece(j, ffn + part * wide, wide)[:, :half] for j in range(chunks)], 1
        )
        if part < 2:
            gu_ref[:, part * chunks * half : (part + 1) * chunks * half] = whole
        else:
            down_ref[...] = whole


def finish(pieces, heads, wide, half, taps):
    chunks, rows, _ = pieces.shape
    keys, vals = HEAD_COUNT * DK, HEAD_COUNT * DV
    ffn = chunks * half
    shapes = [(rows, 2 * keys + vals), (rows, vals), (rows, HEAD_COUNT), (taps, 128)]
    shapes += [(rows, vals), (rows, 2 * ffn), (rows, ffn), (rows, 128)]
    return pl.pallas_call(
        functools.partial(finish_kernel, heads, wide, half, rows),
        in_specs=[WHOLE],
        out_specs=[WHOLE] * len(shapes),
        out_shape=[jax.ShapeDtypeStruct(shape, F32) for shape in shapes],
        compiler_params=pltpu.CompilerParams(vmem_limit_bytes=VMEM_BYTES),
        cost_estimate=SMALL_COST,
        name="finish",
    )(pieces)


def dealt(own):
    return lax.all_to_all(own, "seq", 0, 0, tiled=True)


def left_product(left, right):
    return lax.dot_general(
        left, right, (((0,), (0,)), ((), ())), preferred_element_type=jnp.float32
    )


def right_product(left, right):
    return lax.dot_general(
        left, right, (((1,), (1,)), ((), ())), preferred_element_type=jnp.float32
    )


def dot(left, right):
    return jnp.dot(left, right, preferred_element_type=jnp.float32)


def silu_slope(values):
    gate = jax.nn.sigmoid(values)
    return gate * (1.0 + values * (1.0 - gate))


def split_three(values):
    high = values.astype(BF16)
    rest = values - high.astype(F32)
    middle = rest.astype(BF16)
    return jnp.stack([high, middle, (rest - middle.astype(F32)).astype(BF16)])


def body(
    layer_in,
    out_grad,
    seq_lengths,
    dealing,
    log_decay,
    w_qkv,
    w_out_gate,
    w_beta,
    conv_w,
    gain_in,
    gain_o,
    w_out,
    gain_mid,
    w_gate_up,
    w_down,
):
    seq_count, mp_count = lax.axis_size("seq"), lax.axis_size("mp")
    rank, place_mp = lax.axis_index("seq"), lax.axis_index("mp")
    count = layer_in.shape[1]
    rows = w_qkv.shape[0]
    heads = HEAD_COUNT // seq_count
    key_cols, val_cols = heads * DK, heads * DV
    half = w_down.shape[0] // seq_count
    wide = -(-half // 256) * 256
    taps = conv_w.shape[1]
    total = dealing.shape[1]
    devices = seq_count * mp_count
    channels = 2 * key_cols + val_cols
    all_keys, ffn = HEAD_COUNT * DK, w_down.shape[0]
    split = (seq_count, mp_count // 2) if mp_count <= 8 else None
    words = jnp.stack([place_mp % 2, place_mp // 2, rank]).astype(jnp.int32)
    rank_word = rank.astype(jnp.int32).reshape(1)

    small = jnp.concatenate([conv_w.T.reshape(-1), gain_in, gain_mid, gain_o])
    small_count = small.shape[0]
    spare = 128 - heads
    filler = jnp.concatenate([small, jnp.zeros((rows * spare - small_count,), BF16)])
    filler = filler.reshape(rows, spare)
    wide_filler = jnp.zeros((rows, wide - half), BF16)
    turned_down = w_down.T
    decay_lanes = -(-3 * heads * count // (128 * rows)) * 128
    decays = split_three(log_decay[0].T)
    mix_cols = channels + 128 + val_cols
    pieces, ffn_pieces = [], []
    for j in range(seq_count):
        own_decay = decays[:, j * heads : (j + 1) * heads].reshape(-1)
        own_decay = jnp.concatenate(
            [own_decay, jnp.zeros((rows * decay_lanes - own_decay.shape[0],), BF16)]
        )
        pieces.append(
            jnp.concatenate(
                [
                    w_out_gate[:, j * val_cols : (j + 1) * val_cols],
                    w_qkv[:, j * key_cols : (j + 1) * key_cols],
                    w_qkv[:, all_keys + j * key_cols : all_keys + (j + 1) * key_cols],
                    w_qkv[:, 2 * all_keys + j * val_cols : 2 * all_keys + (j + 1) * val_cols],
                    w_beta[:, j * heads : (j + 1) * heads],
                    filler,
                    own_decay.reshape(rows, decay_lanes),
                ],
                1,
            )
        )
        ffn_pieces.append(
            jnp.concatenate(
                [
                    w_gate_up[:, j * half : (j + 1) * half],
                    wide_filler,
                    w_gate_up[:, ffn + j * half : ffn + (j + 1) * half],
                    wide_filler,
                    turned_down[:, j * half : (j + 1) * half],
                    wide_filler,
                ],
                1,
            )
        )
    def near(arrays):
        arrays = jnp.stack(arrays)
        return jnp.stack(
            returned(
                [lax.dynamic_index_in_dim(arrays, rank ^ k, 0, keepdims=False) for k in range(seq_count)]
            )
        )

    pieces, ffn_pieces = near(pieces), near(ffn_pieces)
    gathered = lax.all_gather(pieces[:, :, :mix_cols], "mp", axis=0, tiled=False)
    late = pieces[1, :1, :1] + jnp.sum(ffn_pieces[1:, :1, :1], axis=0)
    chunks_in = spread(layer_in[0] + 0 * late)

    relative = rank ^ jnp.arange(seq_count)
    smalls = gathered[:, :, :, mix_cols - spare :].transpose(1, 0, 2, 3)
    smalls = jnp.take(smalls, relative, axis=0).reshape(devices, -1)[:, :small_count]
    own_taps = conv_w.shape[0] * taps
    full_conv = smalls[:, :own_taps].reshape(-1, taps, conv_w.shape[0]).transpose(1, 0, 2)
    full_conv = full_conv.reshape(taps, -1).astype(F32)
    conv = jnp.concatenate(
        [
            lax.dynamic_slice_in_dim(full_conv, rank * key_cols, key_cols, 1),
            lax.dynamic_slice_in_dim(full_conv, all_keys + rank * key_cols, key_cols, 1),
            lax.dynamic_slice_in_dim(full_conv, 2 * all_keys + rank * val_cols, val_cols, 1),
        ],
        1,
    )
    conv = jnp.concatenate([conv, jnp.zeros((8 - taps, channels), F32)], 0)
    gains = smalls[:, own_taps:].astype(F32)
    full_gin = gains[:, :rows].reshape(1, -1)
    full_gmid = gains[:, rows : 2 * rows].reshape(1, -1)
    full_go = gains[:, 2 * rows :].reshape(1, -1)

    out_turned = w_out.T
    out_near = []
    if split:
        out_near = [out_turned] + [swapped(out_turned, "mp", 2 * j) for j in range(1, mp_count // 2)]

    out_copies = []
    if split:
        out_copies = [
            jnp.broadcast_to(jnp.stack(out_near), (seq_count, mp_count // 2, *out_turned.shape))
        ]

    decays = pieces[:, :, mix_cols:].reshape(seq_count, -1)[:, : 3 * heads * count]
    col_info, row_info, place_row = positions(
        words, seq_lengths[0], dealing, decays.reshape(seq_count, -1, BLOCK), heads, out_copies
    )

    passed = [ffn_pieces, out_grad[0] + 0 * pieces[1, :1, :1]] + out_copies
    passed = handed(passed, chunks_in[1:] + [row_info])
    ffn_all = lax.all_gather(passed[0], "mp", axis=0, tiled=False)
    chunks_grad = spread(passed[1])
    out_mine = [lax.all_to_all(passed[2], "seq", 0, 0, tiled=True)] if split else []
    (normed, gate_logit, proj, logit_parts, mix), _ = project(
        rank_word, chunks_in, full_gin, gathered, col_info, channels,
        [], [conv, full_go, full_gmid],
    )
    outs = forward_recurrence(proj, conv, col_info, row_info, logit_parts, heads, [])
    dealt_rows, attn, out_mine = gate_rows(
        outs[0], place_row, gate_logit, full_go, count, heads, out_mine, chunks_grad[1:]
    )
    if split:
        out_others = [swapped(out_mine[0], "mp", 1)]
    else:
        out_mine, out_others = [lax.all_gather(out_turned, ("seq", "mp"), axis=0, tiled=True)], []
    attn_parts = returned(attn)
    out_w, normed_t = out_rows(words, out_mine[0], out_others, normed, devices * rows, [attn[0]])

    residual, mid_own = out_project(rank_word, layer_in[0], full_gmid, attn_parts, out_w)

    ffn_w = ffn_rows(words, ffn_all, [mid_own])
    w_gu, down_turned = ffn_w[:, : 2 * wide], ffn_w[:, 2 * wide :]
    mids = spread(mid_own)
    hiddens, gu_grads, mid_parts = ([None] * seq_count for _ in range(3))
    last_part = None
    for k in (0, 1, 3, 2):
        mid_k = mids[k] if last_part is None else pinned(mids[k], last_part)
        gate_up = dot(mid_k, w_gu)
        gate, up = gate_up[:, :wide], gate_up[:, wide:]
        hiddens[k] = (silu(gate) * up).astype(BF16)
        hidden_grad = dot(chunks_grad[k], down_turned)
        gu_grads[k] = jnp.concatenate(
            [hidden_grad * up * silu_slope(gate), hidden_grad * silu(gate)], 1
        ).astype(BF16)
        mid_parts[k] = last_part = right_product(gu_grads[k], w_gu).astype(BF16)
    mid_parts = returned(mid_parts)
    ffn_sum = RowSum(
        weight_grad(
            split, words, [(mids, gu_grads), (chunks_grad, hiddens)], wide, [last_part, mid_parts[1]]
        ),
    )
    res_grad, out_proj_grad, g_mid, attn_grads, ffn_sum.outs[-1:] = mid_back(
        rank_word, out_grad[0], residual, full_gmid, mid_parts, out_w, ffn_sum.outs[-1:]
    )
    attn_grads = returned(attn_grads)
    ffn_sum.pair()
    layer_own, *both = layer_products(hiddens, ffn_w, out_proj_grad)

    (gate_grad, o_grad, g_go), both = ungate_rows(
        dealt_rows, col_info, gate_logit, full_go, attn_grads, heads, both, []
    )
    gate_sums, *gate_outs = weight_grad(
        split, words, [([normed], [gate_grad])], val_cols, [], weights=mix
    )
    gate_sum = RowSum(gate_outs)
    gate_sum.pair()
    ffn_sum = ffn_sum.beside(gate_sum)
    both = returned([None] + both)[1:]
    proj_grad, g_conv = backward_recurrence(
        proj, conv, col_info, row_info, logit_parts, outs[1:], o_grad, heads, [ffn_sum.half]
    )
    mix_grad, mix_sums, *mix_outs = unpack(
        split, words, proj_grad, gate_grad, place_row, normed_t, mix, g_conv, full_gin, g_mid, g_go,
        gate_sums, heads, [],
    )
    mix_sum = RowSum(mix_outs)
    mix_sum.pair()
    normed_parts, _ = unproject(mix_grad, mix, count, [], [])
    normed_chunks = returned(normed_parts)
    out_sum = RowSum(
        weight_grad(split, words, [([out_proj_grad] + both, attn)], val_cols,
            [normed_parts[0], ffn_sum.parts], limit=56 * MIB,
        )
    )
    out_sum.pair()
    last_sum = mix_sum.beside(out_sum)
    in_grad = in_back(layer_in[0], res_grad, full_gin, normed_chunks, [last_sum.half])
    layer_out = residual + sum(
        c.astype(F32) for c in [layer_own] + [b[count:] for b in both]
    )
    all_pieces = dealt(row_sums([ffn_sum, last_sum], [in_grad]))
    layer_out = layer_out.astype(BF16)[None]
    if split:
        g_qkv, g_gate, g_beta, g_conv, g_out, g_gu, g_down, small_sum = finish(
            all_pieces, heads, wide, half, taps
        )
        device = rank * mp_count + place_mp
        grad_go = lax.dynamic_slice_in_dim(
            small_sum[4:6].reshape(-1), device * gain_o.shape[0], gain_o.shape[0]
        )
        grad_gmid = lax.dynamic_slice_in_dim(small_sum[8:16].reshape(-1), device * rows, rows)
        grad_gin = lax.dynamic_slice_in_dim(small_sum[16:24].reshape(-1), device * rows, rows)
        return (
            layer_out, in_grad[None], g_qkv, g_gate, g_beta, g_conv.T,
            grad_gin, grad_go, g_out.T, grad_gmid, g_gu, g_down.T,
        )

    def columns(first, width):
        parts = [all_pieces[j, :, first : first + width] for j in range(seq_count)]
        return jnp.concatenate(parts, 1).astype(F32)

    everywhere = ("seq", "mp")
    conv_full = jnp.zeros((taps, conv_w.shape[0] * devices), F32)
    for first, width in ((0, key_cols), (key_cols, key_cols), (2 * key_cols, val_cols)):
        conv_full = lax.dynamic_update_slice_in_dim(
            conv_full, g_conv[:taps, first : first + width], first * seq_count + rank * width, 1
        )
    grad_conv = lax.psum_scatter(conv_full.T, everywhere, scatter_dimension=0, tiled=True)
    g_gin = mix_sums[0] / full_gin[0]
    grad_gin, grad_gmid, grad_go = (
        lax.psum_scatter(g, everywhere, scatter_dimension=0, tiled=True)
        for g in (g_gin, g_mid[0], g_go[0])
    )
    first = 3 * wide + val_cols
    last = all_pieces.shape[2] - val_cols
    return (
        layer_out,
        in_grad[None],
        jnp.concatenate(
            [
                columns(first, key_cols),
                columns(first + key_cols, key_cols),
                columns(first + 2 * key_cols, val_cols),
            ],
            1,
        ),
        columns(3 * wide, val_cols),
        columns(first + channels, heads),
        grad_conv,
        grad_gin,
        grad_go,
        columns(last, val_cols).T,
        grad_gmid,
        jnp.concatenate([columns(0, half), columns(wide, half)], 1),
        columns(2 * wide, half).T,
    )


def solution(mesh):
    in_specs = (
        P("mp", "seq", None),
        P("mp", "seq", None),
        P("mp", None),
        P("mp", None),
        P("mp", "seq", None),
        P(("seq", "mp"), None),
        P(("seq", "mp"), None),
        P(("seq", "mp"), None),
        P(("seq", "mp"), None),
        P(("seq", "mp")),
        P(("seq", "mp")),
        P(None, ("seq", "mp")),
        P(("seq", "mp")),
        P(("seq", "mp"), None),
        P(None, ("seq", "mp")),
    )
    out_specs = (
        P("mp", "seq", None),
        P("mp", "seq", None),
        P(("seq", "mp"), None),
        P(("seq", "mp"), None),
        P(("seq", "mp"), None),
        P(("seq", "mp"), None),
        P(("seq", "mp")),
        P(("seq", "mp")),
        P(None, ("seq", "mp")),
        P(("seq", "mp")),
        P(("seq", "mp"), None),
        P(None, ("seq", "mp")),
    )
    return jax.shard_map(body, mesh=mesh, in_specs=in_specs, out_specs=out_specs, check_vma=False)
```

profile of v0, /device:TPU:0, one launch (start us, length us, event | category | flops | bytes accessed | tf_op | source)
XLA Modules:
  0.0 455.4 jit_solution(13874055824429536655)
XLA Ops:
  10.5 2.8 concatenate.62
  15.2 3.0 collective-permute-start
  19.8 2.0 collective-permute-done
  21.8 2.8 collective-permute-done.1
  33.0 2.6 collective-permute-start.4
  44.9 4.4 collective-permute-done.4
  53.3 19.7 %collective-permute-done.10.refs_2_.refs_4_ = bf16[384,1024]{1,0:T(8,128)(2,1)S(1)} collective-permute-done((bf16[384,1024]{1,0:T(8,128)(2,1)S(1)}, bf16[384,1024]{1,0:T(8,128)(2,1)S(1)}, u32[]{:S(2)}, u32[]{:S(2)}) %collective-permute-start.10) | collective-permute-done | bytes 786464 | tf_op jit(solution)/shard_map/ppermute | solution.py:1071
  78.7 4.1 all-to-all-start
  87.9 20.0 %project.1 = (bf16[1536,1024]{1,0:T(8,128)(2,1)}, f32[1536,512]{1,0:T(8,128)}, bf16[1536,1024]{1,0:T(8,128)(2,1)}, f32[1536,128]{1,0:T(8,128)}, bf16[1024,1664]{1,0:T(8,128)(2,1)}) custom-call(s32[1]{0:T(128)} %bitcast.rank_ref, f32[1,1024]{1,0:T(1,128)} %reshape.124.gain_ref, bf16[8,4,32,1664]{3,2,1,0:T(8,128)(2,1)} %bitcast.134, f32[1536,128]{1,0:T(8,128)} %copy-done.5, ...), custom_call_target="tpu_custom_call" | custom-call | flops 1000000 | bytes 1000000 | tf_op jit(solution)/shard_map/project/pallas_call | solution.py:433
  108.0 24.7 %recurrence_forward.1 = (bf16[1536,512]{1,0:T(8,128)(2,1)}, bf16[12,2,128,256]{3,2,1,0:T(8,128)(2,1)}, bf16[12,2,128,256]{3,2,1,0:T(8,128)(2,1)}, bf16[12,2,128,...) custom-call(bf16[1536,1024]{1,0:T(8,128)(2,1)} %get-tuple-element.83, ...), custom_call_target="tpu_custom_call" | custom-call | flops 1000000 | bytes 1000000 | tf_op jit(solution)/shard_map/recurrence_forward/pallas_call | solution.py:335
  136.7 3.2 gate_rows.1
  148.8 4.4 collective-permute-done.16.refs_1_
  153.2 9.0 %collective-permute-done.17.refs_2_ = bf16[384,512]{1,0:T(8,128)(2,1)S(1)} collective-permute-done((bf16[384,512]{1,0:T(8,128)(2,1)S(1)}, bf16[384,512]{1,0:T(8,128)(2,1)S(1)}, u32[]{:S(2)}, u32[]{:S(2)}) %collective-permute-start.17) | collective-permute-done | bytes 393248 | tf_op jit(solution)/shard_map/ppermute | solution.py:1071
  162.2 3.0 out_project.1
  168.6 2.3 copy-done.19
  171.8 2.6 fusion.26
  178.1 7.7 %collective-permute-done.19.refs_1_ = bf16[384,1024]{1,0:T(8,128)(2,1)S(1)} collective-permute-done((bf16[384,1024]{1,0:T(8,128)(2,1)}, bf16[384,1024]{1,0:T(8,128)(2,1)S(1)}, u32[]{:S(2)}, u32[]{:S(2)}) %collective-permute-start.19) | collective-permute-done | bytes 786464 | tf_op jit(solution)/shard_map/ppermute | solution.py:1071
  187.2 2.2 multiply_convert_fusion.9
  193.3 10.4 %collective-permute-done.22.refs_3_ = bf16[384,1024]{1,0:T(8,128)(2,1)S(1)} collective-permute-done((bf16[384,1024]{1,0:T(8,128)(2,1)}, bf16[384,1024]{1,0:T(8,128)(2,1)S(1)}, u32[]{:S(2)}, u32[]{:S(2)}) %collective-permute-start.22) | collective-permute-done | bytes 786464 | tf_op jit(solution)/shard_map/ppermute | solution.py:1071
  205.3 2.2 multiply_convert_fusion.7
  211.3 2.5 fusion.13
  213.9 2.2 multiply_convert_fusion.5
  219.6 14.2 %weight_grad.3 = (bf16[4,4,32,2304]{3,2,1,0:T(8,128)(2,1)S(1)}, bf16[4,4,32,2304]{3,2,1,0:T(8,128)(2,1)S(1)}) custom-call(s32[3]{0:T(128)S(1)} %pad_add_fusion.words_ref, bf16[384,1024]{1,0:T(8,128)(2,1)} %get-tuple-element.100.refs_0_, bf16[384,1024]{1,0:T(8,128)(2,1)S(1)} %collective-permute-done.19.refs_1_, ...), custom_call_target="tpu_custom_call" | custom-call | flops 1000000 | bytes 1000000 | tf_op jit(solution)/shard_map/weight_grad/pallas_call | solution.py:776
  233.8 17.1 %collective-permute-done.23.refs_2_ = bf16[384,1024]{1,0:T(8,128)(2,1)S(1)} collective-permute-done((bf16[384,1024]{1,0:T(8,128)(2,1)S(1)}, bf16[384,1024]{1,0:T(8,128)(2,1)S(1)}, u32[]{:S(2)}, u32[]{:S(2)}) %collective-permute-start.23) | collective-permute-done | bytes 786464 | tf_op jit(solution)/shard_map/ppermute | solution.py:1071
  251.0 3.0 mid_back.1
  257.6 2.6 layer_products.1
  260.3 5.7 %collective-permute-done.25.refs_1_ = bf16[384,512]{1,0:T(8,128)(2,1)S(1)} collective-permute-done((bf16[384,512]{1,0:T(8,128)(2,1)S(1)}, bf16[384,512]{1,0:T(8,128)(2,1)S(1)}, u32[]{:S(2)}, u32[]{:S(2)}) %collective-permute-start.25) | collective-permute-done | bytes 393248 | tf_op jit(solution)/shard_map/ppermute | solution.py:1071
  266.0 8.1 %collective-permute-done.26.refs_2_ = bf16[384,512]{1,0:T(8,128)(2,1)S(1)} collective-permute-done((bf16[384,512]{1,0:T(8,128)(2,1)S(1)}, bf16[384,512]{1,0:T(8,128)(2,1)S(1)}, u32[]{:S(2)}, u32[]{:S(2)}) %collective-permute-start.26) | collective-permute-done | bytes 393248 | tf_op jit(solution)/shard_map/ppermute | solution.py:1071
  274.1 5.2 %ungate_rows.1 = (bf16[1536,512]{1,0:T(8,128)(2,1)S(1)}, bf16[1536,512]{1,0:T(8,128)(2,1)S(1)}, f32[1,256]{1,0:T(1,128)S(1)}, bf16[768,1024]{1,0:T(8,128)(2,1)S(...) custom-call(bf16[1536,512]{1,0:T(8,128)(2,1)S(1)} %copy-done.30, ...), custom_call_target="tpu_custom_call", output_to_operand_aliasing={{3}: (8, {}), {4}: (9, {}), {5}: (10, {})} | custom-call | flops 1000000 | bytes 1000000 | tf_op jit(solution)/shard_map/ungate_rows/pallas_call | solution.py:541
  279.5 2.9 weight_grad.4
  282.5 1.9 collective-permute-done.32.refs_3_
  286.6 5.0 %all-to-all-start.1 = ((bf16[4,4,32,2816]{3,2,1,0:T(8,128)(2,1)}), bf16[4,4,32,2816]{3,2,1,0:T(8,128)(2,1)}, u32[]{:S(2)}, u32[]{:S(2)}) async-start(bf16[4,4,32,2816]{3,2,1,0:T(8,128)(2,1)} %copy-done.2), calls=%async_computation.1 | async-start | bytes 5767168 | tf_op jit(solution)/shard_map/all_to_all | solution.py:1110
  295.1 29.9 %recurrence_backward.1 = (bf16[1536,1280]{1,0:T(8,128)(2,1)}, f32[8,1024]{1,0:T(8,128)}) custom-call(bf16[1536,1024]{1,0:T(8,128)(2,1)} %get-tuple-element.83.edge_ref.proj_ref, bf16[1536,1024]{1,0:T(8,128)(2,1)} %get-tuple-element.83.edge_ref.proj_ref, f32[8,1024]{1,0:T(8,128)} %select_maximum_fusion.refs_4_.conv_ref, f32[1536,128]{1,0:T(8,128)} %copy-done.5, ...), custom_call_target="tpu_custom_call" | custom-call | flops 1000000 | bytes 1000000 | tf_op jit(solution)/shard_map/recurrence_backward/pallas_call | solution.py:356
  325.0 2.1 copy-done.20
  327.9 14.9 %unpack.1 = (bf16[1536,1792]{1,0:T(8,128)(2,1)S(1)}, f32[1,1024]{1,0:T(1,128)}, bf16[4,4,32,1280]{3,2,1,0:T(8,128)(2,1)S(1)}, bf16[4,4,32,1280]{3,2,1,0:T(8,128)(2,1)}) custom-call(s32[3]{0:T(128)S(1)} %pad_add_fusion.words_ref, bf16[1536,1280]{1,0:T(8,128)(2,1)S(1)} %copy-done.20, bf16[1536,512]{1,0:T(8,128)(2,1)S(1)} %copy-done.15, ...), custom_call_target="tpu_custom_call" | custom-call | flops 1000000 | bytes 1000000 | tf_op jit(solution)/shard_map/unpack/pallas_call | solution.py:651
  342.7 2.3 copy-done.18
  346.1 12.0 %unproject.1 = (bf16[384,1024]{1,0:T(8,128)(2,1)}, bf16[384,1024]{1,0:T(8,128)(2,1)}, bf16[384,1024]{1,0:T(8,128)(2,1)}, bf16[384,1024]{1,0:T(8,128)(2,1)}) custom-call(bf16[1536,1792]{1,0:T(8,128)(2,1)} %copy-done.18, bf16[1024,1664]{1,0:T(8,128)(2,1)} %get-tuple-element.126.refs_2_.w_ref), custom_call_target="tpu_custom_call" | custom-call | flops 1000000 | bytes 1000000 | tf_op jit(solution)/shard_map/unproject/pallas_call | solution.py:694
  358.2 5.0 %collective-permute-done.29.refs_2_ = bf16[768,1024]{1,0:T(8,128)(2,1)} collective-permute-done((bf16[768,1024]{1,0:T(8,128)(2,1)}, bf16[768,1024]{1,0:T(8,128)(2,1)}, u32[]{:S(2)}, u32[]{:S(2)}) %collective-permute-start.29) | collective-permute-done | bytes 1572896 | tf_op jit(solution)/shard_map/ppermute | solution.py:1071
  363.2 5.8 %weight_grad.5 = (bf16[4,4,32,512]{3,2,1,0:T(8,128)(2,1)}, bf16[4,4,32,512]{3,2,1,0:T(8,128)(2,1)}) custom-call(s32[3]{0:T(128)} %copy-done.50, bf16[384,1024]{1,0:T(8,128)(2,1)} %copy-done.28, bf16[768,1024]{1,0:T(8,128)(2,1)} %collective-permute-done.28.refs_1_, bf16[768,1024]{1,0:T(8,128)(2,1)} %collective-permute-done.29.refs_2_, ...), custom_call_target="tpu_custom_call" | custom-call | flops 1000000 | bytes 1000000 | tf_op jit(solution)/shard_map/weight_grad/pallas_call | solution.py:776
  369.0 2.1 collective-permute-done.37.refs_3_
  373.8 5.0 %all-to-all-start.2 = ((bf16[4,4,32,1792]{3,2,1,0:T(8,128)(2,1)}), bf16[4,4,32,1792]{3,2,1,0:T(8,128)(2,1)S(1)}, u32[]{:S(2)}, u32[]{:S(2)}) async-start(bf16[4,4,32,1792]{3,2,1,0:T(8,128)(2,1)} %joined.3.refs_4_), calls=%async_computation.2 | async-start | bytes 3670016 | tf_op jit(solution)/shard_map/all_to_all | solution.py:1110
  382.3 17.1 %collective-permute-done.33.refs_1_ = bf16[384,1024]{1,0:T(8,128)(2,1)S(1)} collective-permute-done((bf16[384,1024]{1,0:T(8,128)(2,1)}, bf16[384,1024]{1,0:T(8,128)(2,1)S(1)}, u32[]{:S(2)}, u32[]{:S(2)}) %collective-permute-start.33) | collective-permute-done | bytes 786464 | tf_op jit(solution)/shard_map/ppermute | solution.py:1071
  399.5 15.9 %collective-permute-done.34.refs_2_ = bf16[384,1024]{1,0:T(8,128)(2,1)S(1)} collective-permute-done((bf16[384,1024]{1,0:T(8,128)(2,1)}, bf16[384,1024]{1,0:T(8,128)(2,1)S(1)}, u32[]{:S(2)}, u32[]{:S(2)}) %collective-permute-start.34) | collective-permute-done | bytes 786464 | tf_op jit(solution)/shard_map/ppermute | solution.py:1071
  418.6 3.1 all-to-all-done.2.refs_1_
  422.8 3.5 row_sums.1
  426.3 3.7 all-to-all-start.3
  430.0 3.2 fusion.12
  433.2 11.3 %all-to-all-done.3.pieces_ref = bf16[4,32,4608]{2,1,0:T(8,128)(2,1)S(1)} async-done(((bf16[4,32,4608]{2,1,0:T(8,128)(2,1)}), bf16[4,32,4608]{2,1,0:T(8,128)(2,1)S(1)}, u32[]{:S(2)}, u32[]{:S(2)}) %all-to-all-start.3) | async-done | bytes 1179680 | tf_op jit(solution)/shard_map/all_to_all | solution.py:1201
  (296 shorter events, 95.4 us)
Async XLA Ops:
  7.2 75.7 %all-gather.5.cloned.1.call-start = ((), (), s32[]{:S(2)}) async-start(), calls=%async_computation.4 | async-start | bytes 3833856 | tf_op jit(solution)/shard_map/all_gather | solution.py:1318
  15.2 6.6 %collective-permute-start = (bf16[32,1792]{1,0:T(8,128)(2,1)S(1)}, bf16[32,1792]{1,0:T(8,128)(2,1)S(1)}, u32[]{:S(2)}, u32[]{:S(2)}) collective-permute-start(bf16[32,1792]{1,0:T(8,128)(2,1)S(1)} %get-tuple-element.207), channel_id=1, source_target_pairs={{0,8},{8,0},{16,24},{24,16},{1,9},{9,1},{17,25},{25,17},{2,10},{10... | collective-permute-start | bytes 344072 | tf_op jit(solution)/shard_map/ppermute | solution.py:1071
  18.2 6.4 %collective-permute-start.1 = (bf16[32,1792]{1,0:T(8,128)(2,1)S(1)}, bf16[32,1792]{1,0:T(8,128)(2,1)S(1)}, u32[]{:S(2)}, u32[]{:S(2)}) collective-permute-start(bf16[32,1792]{1,0:T(8,128)(2,1)S(1)} %get-tuple-element.206), channel_id=1, source_target_pairs={{0,16},{8,24},{16,0},{24,8},{1,17},{9,25},{17,1},{25,9},{2,18},{10... | collective-permute-start | bytes 344072 | tf_op jit(solution)/shard_map/ppermute | solution.py:1071
  19.8 5.7 %collective-permute-start.2 = (bf16[32,1792]{1,0:T(8,128)(2,1)S(1)}, bf16[32,1792]{1,0:T(8,128)(2,1)S(1)}, u32[]{:S(2)}, u32[]{:S(2)}) collective-permute-start(bf16[32,1792]{1,0:T(8,128)(2,1)S(1)} %get-tuple-element.205), channel_id=1, source_target_pairs={{0,24},{8,16},{16,8},{24,0},{1,25},{9,17},{17,9},{25,1},{2,26},{10... | collective-permute-start | bytes 344072 | tf_op jit(solution)/shard_map/ppermute | solution.py:1071
  27.0 141.6 %all-gather.7.cloned.1.call-start = ((), (), s32[]{:S(2)}) async-start(), calls=%async_computation.5 | async-start | bytes 5308416 | tf_op jit(solution)/shard_map/all_gather | solution.py:1360
  27.8 9.0 %collective-permute-start.6 = (bf16[32,2304]{1,0:T(8,128)(2,1)S(1)}, bf16[32,2304]{1,0:T(8,128)(2,1)S(1)}, u32[]{:S(2)}, u32[]{:S(2)}) collective-permute-start(bf16[32,2304]{1,0:T(8,128)(2,1)S(1)} %get-tuple-element.203), channel_id=1, source_target_pairs={{0,8},{8,0},{16,24},{24,16},{1,9},{9,1},{17,25},{25,17},{2,10},{10... | collective-permute-start | bytes 442376 | tf_op jit(solution)/shard_map/ppermute | solution.py:1071
  28.9 9.2 %collective-permute-start.7 = (bf16[32,2304]{1,0:T(8,128)(2,1)S(1)}, bf16[32,2304]{1,0:T(8,128)(2,1)S(1)}, u32[]{:S(2)}, u32[]{:S(2)}) collective-permute-start(bf16[32,2304]{1,0:T(8,128)(2,1)S(1)} %get-tuple-element.202), channel_id=1, source_target_pairs={{0,16},{8,24},{16,0},{24,8},{1,17},{9,25},{17,1},{25,9},{2,18},{10... | collective-permute-start | bytes 442376 | tf_op jit(solution)/shard_map/ppermute | solution.py:1071
  29.8 8.4 %collective-permute-start.8 = (bf16[32,2304]{1,0:T(8,128)(2,1)S(1)}, bf16[32,2304]{1,0:T(8,128)(2,1)S(1)}, u32[]{:S(2)}, u32[]{:S(2)}) collective-permute-start(bf16[32,2304]{1,0:T(8,128)(2,1)S(1)} %get-tuple-element.201), channel_id=1, source_target_pairs={{0,24},{8,16},{16,8},{24,0},{1,25},{9,17},{17,9},{25,1},{2,26},{10... | collective-permute-start | bytes 442376 | tf_op jit(solution)/shard_map/ppermute | solution.py:1071
  31.4 11.2 %collective-permute-start.3 = (bf16[32,2048]{1,0:T(8,128)(2,1)}, bf16[32,2048]{1,0:T(8,128)(2,1)}, u32[]{:S(2)}, u32[]{:S(2)}) collective-permute-start(bf16[32,2048]{1,0:T(8,128)(2,1)} %bitcast.30), channel_id=1, source_target_pairs={{0,2},{1,3},{2,0},{3,1},{4,6},{5,7},{6,4},{7,5},{8,10},{9,11},{10,... | collective-permute-start | bytes 393224 | tf_op jit(solution)/shard_map/ppermute | solution.py:1071
  33.0 16.3 %collective-permute-start.4 = (bf16[32,2048]{1,0:T(8,128)(2,1)}, bf16[32,2048]{1,0:T(8,128)(2,1)}, u32[]{:S(2)}, u32[]{:S(2)}) collective-permute-start(bf16[32,2048]{1,0:T(8,128)(2,1)} %bitcast.30), channel_id=1, source_target_pairs={{0,4},{1,5},{2,6},{3,7},{4,0},{5,1},{6,2},{7,3},{8,12},{9,13},{10,... | collective-permute-start | bytes 393224 | tf_op jit(solution)/shard_map/ppermute | solution.py:1071
  35.6 289.3 %copy-start.50 = (s32[3]{0:T(128)}, s32[3]{0:T(128)S(1)}, u32[]{:S(2)}) copy-start(s32[3]{0:T(128)S(1)} %pad_add_fusion.words_ref) | copy-start | bytes 40
  36.8 12.4 %collective-permute-start.5 = (bf16[32,2048]{1,0:T(8,128)(2,1)}, bf16[32,2048]{1,0:T(8,128)(2,1)}, u32[]{:S(2)}, u32[]{:S(2)}) collective-permute-start(bf16[32,2048]{1,0:T(8,128)(2,1)} %bitcast.30), channel_id=1, source_target_pairs={{0,6},{1,7},{2,4},{3,5},{4,2},{5,3},{6,0},{7,1},{8,14},{9,15},{10,... | collective-permute-start | bytes 393224 | tf_op jit(solution)/shard_map/ppermute | solution.py:1071
  40.2 32.7 %collective-permute-start.10 = (bf16[384,1024]{1,0:T(8,128)(2,1)S(1)}, bf16[384,1024]{1,0:T(8,128)(2,1)S(1)}, u32[]{:S(2)}, u32[]{:S(2)}) collective-permute-start(bf16[384,1024]{1,0:T(8,128)(2,1)S(1)} %broadcast_add_fusion.1.refs_0_), channel_id=1, source_target_pairs={{0,16},{8,24},{16,0},{24,8},{1,17},{9,25},{17,1},{25,9},{2,18},{10... | collective-permute-start | bytes 2359304 | tf_op jit(solution)/shard_map/ppermute | solution.py:1071
  40.9 32.0 %collective-permute-start.11 = (bf16[384,1024]{1,0:T(8,128)(2,1)S(1)}, bf16[384,1024]{1,0:T(8,128)(2,1)}, u32[]{:S(2)}, u32[]{:S(2)}) collective-permute-start(bf16[384,1024]{1,0:T(8,128)(2,1)S(1)} %broadcast_add_fusion.1.refs_0_), channel_id=1, source_target_pairs={{0,24},{8,16},{16,8},{24,0},{1,25},{9,17},{17,9},{25,1},{2,26},{10... | collective-permute-start | bytes 2359304 | tf_op jit(solution)/shard_map/ppermute | solution.py:1071
  42.6 31.8 %collective-permute-start.9 = (bf16[384,1024]{1,0:T(8,128)(2,1)S(1)}, bf16[384,1024]{1,0:T(8,128)(2,1)}, u32[]{:S(2)}, u32[]{:S(2)}) collective-permute-start(bf16[384,1024]{1,0:T(8,128)(2,1)S(1)} %broadcast_add_fusion.1.refs_0_), channel_id=1, source_target_pairs={{0,8},{8,0},{16,24},{24,16},{1,9},{9,1},{17,25},{25,17},{2,10},{10... | collective-permute-start | bytes 2359304 | tf_op jit(solution)/shard_map/ppermute | solution.py:1071
  75.2 57.6 %collective-permute-start.12 = (bf16[384,1024]{1,0:T(8,128)(2,1)}, bf16[384,1024]{1,0:T(8,128)(2,1)}, u32[]{:S(2)}, u32[]{:S(2)}) collective-permute-start(bf16[384,1024]{1,0:T(8,128)(2,1)} %get-tuple-element.90.refs_8_), channel_id=1, source_target_pairs={{0,8},{8,0},{16,24},{24,16},{1,9},{9,1},{17,25},{25,17},{2,10},{10... | collective-permute-start | bytes 2359304 | tf_op jit(solution)/shard_map/ppermute | solution.py:1071
  76.3 56.4 %collective-permute-start.13 = (bf16[384,1024]{1,0:T(8,128)(2,1)}, bf16[384,1024]{1,0:T(8,128)(2,1)}, u32[]{:S(2)}, u32[]{:S(2)}) collective-permute-start(bf16[384,1024]{1,0:T(8,128)(2,1)} %get-tuple-element.90.refs_8_), channel_id=1, source_target_pairs={{0,16},{8,24},{16,0},{24,8},{1,17},{9,25},{17,1},{25,9},{2,18},{10... | collective-permute-start | bytes 2359304 | tf_op jit(solution)/shard_map/ppermute | solution.py:1071
  77.0 55.8 %collective-permute-start.14 = (bf16[384,1024]{1,0:T(8,128)(2,1)}, bf16[384,1024]{1,0:T(8,128)(2,1)}, u32[]{:S(2)}, u32[]{:S(2)}) collective-permute-start(bf16[384,1024]{1,0:T(8,128)(2,1)} %get-tuple-element.90.refs_8_), channel_id=1, source_target_pairs={{0,24},{8,16},{16,8},{24,0},{1,25},{9,17},{17,9},{25,1},{2,26},{10... | collective-permute-start | bytes 2359304 | tf_op jit(solution)/shard_map/ppermute | solution.py:1071
  78.7 54.7 %all-to-all-start = ((bf16[4,4,32,2048]{3,2,1,0:T(8,128)(2,1)}), bf16[4,4,32,2048]{3,2,1,0:T(8,128)(2,1)S(1)}, u32[]{:S(2)}, u32[]{:S(2)}) async-start(bf16[4,4,32,2048]{3,2,1,0:T(8,128)(2,1)} %get-tuple-element.89), calls=%async_computation | async-start | bytes 4194304 | tf_op jit(solution)/shard_map/all_to_all | solution.py:1362
  141.1 4.2 collective-permute-start.15
  141.2 12.0 %collective-permute-start.16 = (bf16[384,512]{1,0:T(8,128)(2,1)S(1)}, bf16[384,512]{1,0:T(8,128)(2,1)S(1)}, u32[]{:S(2)}, u32[]{:S(2)}) collective-permute-start(bf16[384,512]{1,0:T(8,128)(2,1)S(1)} %get-tuple-element.95.refs_5_), channel_id=1, source_target_pairs={{0,8},{8,0},{16,24},{24,16},{1,9},{9,1},{17,25},{25,17},{2,10},{10... | collective-permute-start | bytes 1179656 | tf_op jit(solution)/shard_map/ppermute | solution.py:1071
  142.6 19.6 %collective-permute-start.17 = (bf16[384,512]{1,0:T(8,128)(2,1)S(1)}, bf16[384,512]{1,0:T(8,128)(2,1)S(1)}, u32[]{:S(2)}, u32[]{:S(2)}) collective-permute-start(bf16[384,512]{1,0:T(8,128)(2,1)S(1)} %get-tuple-element.96.refs_6_), channel_id=1, source_target_pairs={{0,16},{8,24},{16,0},{24,8},{1,17},{9,25},{17,1},{25,9},{2,18},{10... | collective-permute-start | bytes 1179656 | tf_op jit(solution)/shard_map/ppermute | solution.py:1071
  144.1 18.1 %collective-permute-start.18 = (bf16[384,512]{1,0:T(8,128)(2,1)S(1)}, bf16[384,512]{1,0:T(8,128)(2,1)S(1)}, u32[]{:S(2)}, u32[]{:S(2)}) collective-permute-start(bf16[384,512]{1,0:T(8,128)(2,1)S(1)} %get-tuple-element.97.refs_7_), channel_id=1, source_target_pairs={{0,24},{8,16},{16,8},{24,0},{1,25},{9,17},{17,9},{25,1},{2,26},{10... | collective-permute-start | bytes 1179656 | tf_op jit(solution)/shard_map/ppermute | solution.py:1071
  165.1 85.8 %copy-start.16 = (f32[384,1024]{1,0:T(8,128)}, f32[384,1024]{1,0:T(8,128)S(1)}, u32[]{:S(2)}) copy-start(f32[384,1024]{1,0:T(8,128)S(1)} %get-tuple-element.98.residual_ref) | copy-start | bytes 4718596
  165.2 20.7 %collective-permute-start.19 = (bf16[384,1024]{1,0:T(8,128)(2,1)}, bf16[384,1024]{1,0:T(8,128)(2,1)S(1)}, u32[]{:S(2)}, u32[]{:S(2)}) collective-permute-start(bf16[384,1024]{1,0:T(8,128)(2,1)} %get-tuple-element.100.refs_0_), channel_id=1, source_target_pairs={{0,8},{8,0},{16,24},{24,16},{1,9},{9,1},{17,25},{25,17},{2,10},{10... | collective-permute-start | bytes 2359304 | tf_op jit(solution)/shard_map/ppermute | solution.py:1071
  166.4 37.3 %collective-permute-start.22 = (bf16[384,1024]{1,0:T(8,128)(2,1)}, bf16[384,1024]{1,0:T(8,128)(2,1)S(1)}, u32[]{:S(2)}, u32[]{:S(2)}) collective-permute-start(bf16[384,1024]{1,0:T(8,128)(2,1)} %get-tuple-element.100.refs_0_), channel_id=1, source_target_pairs={{0,24},{8,16},{16,8},{24,0},{1,25},{9,17},{17,9},{25,1},{2,26},{10... | collective-permute-start | bytes 2359304 | tf_op jit(solution)/shard_map/ppermute | solution.py:1071
  168.1 43.2 %collective-permute-start.21 = (bf16[384,1024]{1,0:T(8,128)(2,1)}, bf16[384,1024]{1,0:T(8,128)(2,1)}, u32[]{:S(2)}, u32[]{:S(2)}) collective-permute-start(bf16[384,1024]{1,0:T(8,128)(2,1)} %get-tuple-element.100.refs_0_), channel_id=1, source_target_pairs={{0,16},{8,24},{16,0},{24,8},{1,17},{9,25},{17,1},{25,9},{2,18},{10... | collective-permute-start | bytes 2359304 | tf_op jit(solution)/shard_map/ppermute | solution.py:1071
  191.4 28.2 %collective-permute-start.20 = (bf16[384,1024]{1,0:T(8,128)(2,1)S(1)}, bf16[384,1024]{1,0:T(8,128)(2,1)S(1)}, u32[]{:S(2)}, u32[]{:S(2)}) collective-permute-start(bf16[384,1024]{1,0:T(8,128)(2,1)S(1)} %convolution_convert_fusion.2), channel_id=1, source_target_pairs={{0,8},{8,0},{16,24},{24,16},{1,9},{9,1},{17,25},{25,17},{2,10},{10... | collective-permute-start | bytes 2359304 | tf_op jit(solution)/shard_map/ppermute | solution.py:1071
  209.4 41.5 %collective-permute-start.24 = (bf16[384,1024]{1,0:T(8,128)(2,1)S(1)}, bf16[384,1024]{1,0:T(8,128)(2,1)S(1)}, u32[]{:S(2)}, u32[]{:S(2)}) collective-permute-start(bf16[384,1024]{1,0:T(8,128)(2,1)S(1)} %convolution_convert_fusion.1), channel_id=1, source_target_pairs={{0,24},{8,16},{16,8},{24,0},{1,25},{9,17},{17,9},{25,1},{2,26},{10... | collective-permute-start | bytes 2359304 | tf_op jit(solution)/shard_map/ppermute | solution.py:1071
  217.5 33.4 %collective-permute-start.23 = (bf16[384,1024]{1,0:T(8,128)(2,1)S(1)}, bf16[384,1024]{1,0:T(8,128)(2,1)S(1)}, u32[]{:S(2)}, u32[]{:S(2)}) collective-permute-start(bf16[384,1024]{1,0:T(8,128)(2,1)S(1)} %convolution_convert_fusion.refs_16_), channel_id=1, source_target_pairs={{0,16},{8,24},{16,0},{24,8},{1,17},{9,25},{17,1},{25,9},{2,18},{10... | collective-permute-start | bytes 2359304 | tf_op jit(solution)/shard_map/ppermute | solution.py:1071
  254.0 30.4 %collective-permute-start.31 = (bf16[4,4,32,2304]{3,2,1,0:T(8,128)(2,1)S(1)}, bf16[4,4,32,2304]{3,2,1,0:T(8,128)(2,1)S(1)}, u32[]{:S(2)}, u32[]{:S(2)}) collective-permute-start(bf16[4,4,32,2304]{3,2,1,0:T(8,128)(2,1)S(1)} %get-tuple-element.124), channel_id=1, source_target_pairs={{0,1},{1,0},{2,3},{3,2},{4,5},{5,4},{6,7},{7,6},{8,9},{9,8},{10,11... | collective-permute-start | bytes 7077896 | tf_op jit(solution)/shard_map/ppermute | solution.py:1071
  254.0 12.0 %collective-permute-start.25 = (bf16[384,512]{1,0:T(8,128)(2,1)S(1)}, bf16[384,512]{1,0:T(8,128)(2,1)S(1)}, u32[]{:S(2)}, u32[]{:S(2)}) collective-permute-start(bf16[384,512]{1,0:T(8,128)(2,1)S(1)} %get-tuple-element.106), channel_id=1, source_target_pairs={{0,8},{8,0},{16,24},{24,16},{1,9},{9,1},{17,25},{25,17},{2,10},{10... | collective-permute-start | bytes 1179656 | tf_op jit(solution)/shard_map/ppermute | solution.py:1071
  254.5 19.6 %collective-permute-start.26 = (bf16[384,512]{1,0:T(8,128)(2,1)S(1)}, bf16[384,512]{1,0:T(8,128)(2,1)S(1)}, u32[]{:S(2)}, u32[]{:S(2)}) collective-permute-start(bf16[384,512]{1,0:T(8,128)(2,1)S(1)} %get-tuple-element.107), channel_id=1, source_target_pairs={{0,16},{8,24},{16,0},{24,8},{1,17},{9,25},{17,1},{25,9},{2,18},{10... | collective-permute-start | bytes 1179656 | tf_op jit(solution)/shard_map/ppermute | solution.py:1071
  255.8 18.3 %collective-permute-start.27 = (bf16[384,512]{1,0:T(8,128)(2,1)S(1)}, bf16[384,512]{1,0:T(8,128)(2,1)S(1)}, u32[]{:S(2)}, u32[]{:S(2)}) collective-permute-start(bf16[384,512]{1,0:T(8,128)(2,1)S(1)} %get-tuple-element.108), channel_id=1, source_target_pairs={{0,24},{8,16},{16,8},{24,0},{1,25},{9,17},{17,9},{25,1},{2,26},{10... | collective-permute-start | bytes 1179656 | tf_op jit(solution)/shard_map/ppermute | solution.py:1071
  282.5 1.9 collective-permute-start.32
  286.6 76.5 %all-to-all-start.1 = ((bf16[4,4,32,2816]{3,2,1,0:T(8,128)(2,1)}), bf16[4,4,32,2816]{3,2,1,0:T(8,128)(2,1)}, u32[]{:S(2)}, u32[]{:S(2)}) async-start(bf16[4,4,32,2816]{3,2,1,0:T(8,128)(2,1)} %copy-done.2), calls=%async_computation.1 | async-start | bytes 5767168 | tf_op jit(solution)/shard_map/all_to_all | solution.py:1110
  291.6 66.6 %collective-permute-start.28 = (bf16[768,1024]{1,0:T(8,128)(2,1)}, bf16[768,1024]{1,0:T(8,128)(2,1)}, u32[]{:S(2)}, u32[]{:S(2)}) collective-permute-start(bf16[768,1024]{1,0:T(8,128)(2,1)} %copy-done.34), channel_id=1, source_target_pairs={{0,8},{8,0},{16,24},{24,16},{1,9},{9,1},{17,25},{25,17},{2,10},{10... | collective-permute-start | bytes 4718600 | tf_op jit(solution)/shard_map/ppermute | solution.py:1071
  293.2 70.0 %collective-permute-start.29 = (bf16[768,1024]{1,0:T(8,128)(2,1)}, bf16[768,1024]{1,0:T(8,128)(2,1)}, u32[]{:S(2)}, u32[]{:S(2)}) collective-permute-start(bf16[768,1024]{1,0:T(8,128)(2,1)} %copy-done.35), channel_id=1, source_target_pairs={{0,16},{8,24},{16,0},{24,8},{1,17},{9,25},{17,1},{25,9},{2,18},{10... | collective-permute-start | bytes 4718600 | tf_op jit(solution)/shard_map/ppermute | solution.py:1071
  293.6 69.6 %collective-permute-start.30 = (bf16[768,1024]{1,0:T(8,128)(2,1)}, bf16[768,1024]{1,0:T(8,128)(2,1)}, u32[]{:S(2)}, u32[]{:S(2)}) collective-permute-start(bf16[768,1024]{1,0:T(8,128)(2,1)} %copy-done.36), channel_id=1, source_target_pairs={{0,24},{8,16},{16,8},{24,0},{1,25},{9,17},{17,9},{25,1},{2,26},{10... | collective-permute-start | bytes 4718600 | tf_op jit(solution)/shard_map/ppermute | solution.py:1071
  346.1 22.9 %collective-permute-start.36 = (bf16[4,4,32,1280]{3,2,1,0:T(8,128)(2,1)}, bf16[4,4,32,1280]{3,2,1,0:T(8,128)(2,1)S(1)}, u32[]{:S(2)}, u32[]{:S(2)}) collective-permute-start(bf16[4,4,32,1280]{3,2,1,0:T(8,128)(2,1)} %get-tuple-element.141), channel_id=1, source_target_pairs={{0,1},{1,0},{2,3},{3,2},{4,5},{5,4},{6,7},{7,6},{8,9},{9,8},{10,11... | collective-permute-start | bytes 3932168 | tf_op jit(solution)/shard_map/ppermute | solution.py:1071
  369.0 2.1 collective-permute-start.37
  373.8 41.5 %copy-start.13 = (bf16[1,384,1024]{2,1,0:T(8,128)(2,1)S(1)}, bf16[1,384,1024]{2,1,0:T(8,128)(2,1)}, u32[]{:S(2)}) copy-start(bf16[1,384,1024]{2,1,0:T(8,128)(2,1)} %param.15) | copy-start | bytes 2359300
  373.8 41.5 %copy-start.27 = (bf16[384,1024]{1,0:T(8,128)(2,1)S(1)}, bf16[384,1024]{1,0:T(8,128)(2,1)}, u32[]{:S(2)}) copy-start(bf16[384,1024]{1,0:T(8,128)(2,1)} %get-tuple-element.136.refs_8_.refs_0_) | copy-start | bytes 2359300
  373.8 47.9 %all-to-all-start.2 = ((bf16[4,4,32,1792]{3,2,1,0:T(8,128)(2,1)}), bf16[4,4,32,1792]{3,2,1,0:T(8,128)(2,1)S(1)}, u32[]{:S(2)}, u32[]{:S(2)}) async-start(bf16[4,4,32,1792]{3,2,1,0:T(8,128)(2,1)} %joined.3.refs_4_), calls=%async_computation.2 | async-start | bytes 3670016 | tf_op jit(solution)/shard_map/all_to_all | solution.py:1110
  378.8 20.6 %collective-permute-start.33 = (bf16[384,1024]{1,0:T(8,128)(2,1)}, bf16[384,1024]{1,0:T(8,128)(2,1)S(1)}, u32[]{:S(2)}, u32[]{:S(2)}) collective-permute-start(bf16[384,1024]{1,0:T(8,128)(2,1)} %get-tuple-element.137), channel_id=1, source_target_pairs={{0,8},{8,0},{16,24},{24,16},{1,9},{9,1},{17,25},{25,17},{2,10},{10... | collective-permute-start | bytes 2359304 | tf_op jit(solution)/shard_map/ppermute | solution.py:1071
  379.3 36.1 %collective-permute-start.34 = (bf16[384,1024]{1,0:T(8,128)(2,1)}, bf16[384,1024]{1,0:T(8,128)(2,1)S(1)}, u32[]{:S(2)}, u32[]{:S(2)}) collective-permute-start(bf16[384,1024]{1,0:T(8,128)(2,1)} %get-tuple-element.138), channel_id=1, source_target_pairs={{0,16},{8,24},{16,0},{24,8},{1,17},{9,25},{17,1},{25,9},{2,18},{10... | collective-permute-start | bytes 2359304 | tf_op jit(solution)/shard_map/ppermute | solution.py:1071
  380.6 34.8 %collective-permute-start.35 = (bf16[384,1024]{1,0:T(8,128)(2,1)}, bf16[384,1024]{1,0:T(8,128)(2,1)S(1)}, u32[]{:S(2)}, u32[]{:S(2)}) collective-permute-start(bf16[384,1024]{1,0:T(8,128)(2,1)} %get-tuple-element.139), channel_id=1, source_target_pairs={{0,24},{8,16},{16,8},{24,0},{1,25},{9,17},{17,9},{25,1},{2,26},{10... | collective-permute-start | bytes 2359304 | tf_op jit(solution)/shard_map/ppermute | solution.py:1071
  426.3 18.2 %all-to-all-start.3 = ((bf16[4,32,4608]{2,1,0:T(8,128)(2,1)}), bf16[4,32,4608]{2,1,0:T(8,128)(2,1)S(1)}, u32[]{:S(2)}, u32[]{:S(2)}) async-start(bf16[4,32,4608]{2,1,0:T(8,128)(2,1)} %row_sums.1), calls=%async_computation.3 | async-start | bytes 2359296 | tf_op jit(solution)/shard_map/all_to_all | solution.py:1201
  (64 other events, 536.9 us)
Sparse Core Ops, SparseCore 0:
  27.1 47.1 all-gather.4
  76.6 50.9 all-gather.6
where the time goes:
time: 460 us; the launch traced here: 455 us
  Pallas kernels  155 us (34%)
  waiting for transfers between devices  152 us (33%)
  starting transfers between devices  59.5 us (13%)
  local copies, waits for them, and re-layouts  38.4 us (8%)
  matrix products  21.5 us (5%)
  between operations  19.4 us (4%)
  other arithmetic  9.81 us (2%)
    ppermute x38, waiting for transfers between devices, swapped(): return lax.ppermute(value, axis, [(i, i ^ mask) for i in range(devices)])  137 us
    ppermute x38, starting transfers between devices, swapped(): return lax.ppermute(value, axis, [(i, i ^ mask) for i in range(devices)])  41.6 us
    pallas_call x1, Pallas kernels, backward_recurrence(): pl.pallas_call(functools.partial(backward_kernel, heads), grid=(count //...  29.9 us
    pallas_call x1, Pallas kernels, forward_recurrence(): pl.pallas_call(functools.partial(forward_kernel, heads), grid=(count // s...  24.7 us
    pallas_call x3, Pallas kernels, weight_grad(): pl.pallas_call(functools.partial(weight_grad_kernel, split, tiles, sums),...  22.9 us
    unnamed x139, local copies, waits for them, and re-layouts  22.1 us
    pallas_call x1, Pallas kernels, project(): pl.pallas_call(functools.partial(project_kernel, channels, chunks, len(pa...  20 us
    dot_general x8, matrix products, dot(): return jnp.dot(left, right, preferred_element_type=jnp.float32)  15.9 us
  transfers between devices with their start and end apart: 44, of which 23 were waited for; matrix products, arithmetic and copies ran while one was open for 8% of the time, Pallas kernels for 32%

commit v1 on v0

--- a/solution.py
+++ b/solution.py
@@ -1288,7 +1288,6 @@
                     w_qkv[:, 2 * all_keys + j * val_cols : 2 * all_keys + (j + 1) * val_cols],
                     w_beta[:, j * heads : (j + 1) * heads],
                     filler,
-                    own_decay.reshape(rows, decay_lanes),
                 ],
                 1,
             )
@@ -1302,6 +1301,7 @@
                     wide_filler,
                     turned_down[:, j * half : (j + 1) * half],
                     wide_filler,
+                    own_decay.reshape(rows, decay_lanes),
                 ],
                 1,
             )
@@ -1315,7 +1315,7 @@
         )
 
     pieces, ffn_pieces = near(pieces), near(ffn_pieces)
-    gathered = lax.all_gather(pieces[:, :, :mix_cols], "mp", axis=0, tiled=False)
+    gathered = lax.all_gather(pieces, "mp", axis=0, tiled=False)
     late = pieces[1, :1, :1] + jnp.sum(ffn_pieces[1:, :1, :1], axis=0)
     chunks_in = spread(layer_in[0] + 0 * late)
 
@@ -1350,12 +1350,12 @@
             jnp.broadcast_to(jnp.stack(out_near), (seq_count, mp_count // 2, *out_turned.shape))
         ]
 
-    decays = pieces[:, :, mix_cols:].reshape(seq_count, -1)[:, : 3 * heads * count]
+    decays = ffn_pieces[:, :, 3 * wide :].reshape(seq_count, -1)[:, : 3 * heads * count]
     col_info, row_info, place_row = positions(
         words, seq_lengths[0], dealing, decays.reshape(seq_count, -1, BLOCK), heads, out_copies
     )
 
-    passed = [ffn_pieces, out_grad[0] + 0 * pieces[1, :1, :1]] + out_copies
+    passed = [ffn_pieces[:, :, : 3 * wide], out_grad[0] + 0 * pieces[1, :1, :1]] + out_copies
     passed = handed(passed, chunks_in[1:] + [row_info])
     ffn_all = lax.all_gather(passed[0], "mp", axis=0, tiled=False)
     chunks_grad = spread(passed[1])

time: 460 us -> 458 us (level)
    unnamed x139 -> x141, local copies, waits for them, and re-layouts: 22.1 us -> 21.5 us
where the time goes in v1:
time: 458 us; the launch traced here: 453 us
  Pallas kernels  155 us (34%)
  waiting for transfers between devices  152 us (33%)
  starting transfers between devices  59.6 us (13%)
  local copies, waits for them, and re-layouts  37.1 us (8%)
  matrix products  21.5 us (5%)
  between operations  19.4 us (4%)
  other arithmetic  8.96 us (2%)
    ppermute x38, waiting for transfers between devices, swapped(): return lax.ppermute(value, axis, [(i, i ^ mask) for i in range(devices)])  137 us
    ppermute x38, starting transfers between devices, swapped(): return lax.ppermute(value, axis, [(i, i ^ mask) for i in range(devices)])  41.8 us
    pallas_call x1, Pallas kernels, backward_recurrence(): pl.pallas_call(functools.partial(backward_kernel, heads), grid=(count //...  29.9 us
    pallas_call x1, Pallas kernels, forward_recurrence(): pl.pallas_call(functools.partial(forward_kernel, heads), grid=(count // s...  24.7 us
    pallas_call x3, Pallas kernels, weight_grad(): pl.pallas_call(functools.partial(weight_grad_kernel, split, tiles, sums),...  22.9 us
    unnamed x141, local copies, waits for them, and re-layouts  21.5 us
    pallas_call x1, Pallas kernels, project(): pl.pallas_call(functools.partial(project_kernel, channels, chunks, len(pa...  20 us
    dot_general x8, matrix products, dot(): return jnp.dot(left, right, preferred_element_type=jnp.float32)  15.9 us
  transfers between devices with their start and end apart: 44, of which 23 were waited for; matrix products, arithmetic and copies ran while one was open for 8% of the time, Pallas kernels for 32%

profile of v1, /device:TPU:0, one launch (start us, length us, event | category | flops | bytes accessed | tf_op | source)
XLA Modules:
  0.0 453.1 jit_solution(7733109025320629248)
XLA Ops:
  9.0 2.8 concatenate.62
  13.7 3.0 collective-permute-start
  19.9 2.6 collective-permute-done.1
  30.9 2.6 collective-permute-start.7
  42.9 4.1 collective-permute-done.7
  50.9 19.7 %collective-permute-done.10.refs_2_.refs_4_ = bf16[384,1024]{1,0:T(8,128)(2,1)S(1)} collective-permute-done((bf16[384,1024]{1,0:T(8,128)(2,1)S(1)}, bf16[384,1024]{1,0:T(8,128)(2,1)S(1)}, u32[]{:S(2)}, u32[]{:S(2)}) %collective-permute-start.10) | collective-permute-done | bytes 786464 | tf_op jit(solution)/shard_map/ppermute | solution.py:1071
  76.4 4.1 all-to-all-start
  85.6 20.0 %project.1 = (bf16[1536,1024]{1,0:T(8,128)(2,1)}, f32[1536,512]{1,0:T(8,128)}, bf16[1536,1024]{1,0:T(8,128)(2,1)}, f32[1536,128]{1,0:T(8,128)}, bf16[1024,1664]{1,0:T(8,128)(2,1)}) custom-call(s32[1]{0:T(128)} %bitcast.rank_ref, f32[1,1024]{1,0:T(1,128)} %reshape.116.gain_ref, bf16[8,4,32,1664]{3,2,1,0:T(8,128)(2,1)} %bitcast.134, f32[1536,128]{1,0:T(8,128)} %copy-done.5, ...), custom_call_target="tpu_custom_call" | custom-call | flops 1000000 | bytes 1000000 | tf_op jit(solution)/shard_map/project/pallas_call | solution.py:433
  105.6 24.7 %recurrence_forward.1 = (bf16[1536,512]{1,0:T(8,128)(2,1)}, bf16[12,2,128,256]{3,2,1,0:T(8,128)(2,1)}, bf16[12,2,128,256]{3,2,1,0:T(8,128)(2,1)}, bf16[12,2,128,...) custom-call(bf16[1536,1024]{1,0:T(8,128)(2,1)} %get-tuple-element.83, ...), custom_call_target="tpu_custom_call" | custom-call | flops 1000000 | bytes 1000000 | tf_op jit(solution)/shard_map/recurrence_forward/pallas_call | solution.py:335
  130.9 1.9 copy-done.7
  134.2 3.2 gate_rows.1
  146.2 4.4 collective-permute-done.16.refs_1_
  150.6 9.3 %collective-permute-done.17.refs_2_ = bf16[384,512]{1,0:T(8,128)(2,1)S(1)} collective-permute-done((bf16[384,512]{1,0:T(8,128)(2,1)S(1)}, bf16[384,512]{1,0:T(8,128)(2,1)S(1)}, u32[]{:S(2)}, u32[]{:S(2)}) %collective-permute-start.17) | collective-permute-done | bytes 393248 | tf_op jit(solution)/shard_map/ppermute | solution.py:1071
  159.9 3.0 out_project.1
  166.3 2.3 copy-done.19
  169.5 2.6 fusion.26
  175.8 7.7 %collective-permute-done.19.refs_1_ = bf16[384,1024]{1,0:T(8,128)(2,1)S(1)} collective-permute-done((bf16[384,1024]{1,0:T(8,128)(2,1)}, bf16[384,1024]{1,0:T(8,128)(2,1)S(1)}, u32[]{:S(2)}, u32[]{:S(2)}) %collective-permute-start.19) | collective-permute-done | bytes 786464 | tf_op jit(solution)/shard_map/ppermute | solution.py:1071
  184.9 2.2 multiply_convert_fusion.9
  191.0 10.4 %collective-permute-done.22.refs_3_ = bf16[384,1024]{1,0:T(8,128)(2,1)S(1)} collective-permute-done((bf16[384,1024]{1,0:T(8,128)(2,1)}, bf16[384,1024]{1,0:T(8,128)(2,1)S(1)}, u32[]{:S(2)}, u32[]{:S(2)}) %collective-permute-start.22) | collective-permute-done | bytes 786464 | tf_op jit(solution)/shard_map/ppermute | solution.py:1071
  203.0 2.2 multiply_convert_fusion.7
  209.1 2.5 fusion.13
  211.6 2.2 multiply_convert_fusion.5
  217.3 14.2 %weight_grad.3 = (bf16[4,4,32,2304]{3,2,1,0:T(8,128)(2,1)S(1)}, bf16[4,4,32,2304]{3,2,1,0:T(8,128)(2,1)S(1)}) custom-call(s32[3]{0:T(128)S(1)} %pad_add_fusion.words_ref, bf16[384,1024]{1,0:T(8,128)(2,1)} %get-tuple-element.100.refs_0_, bf16[384,1024]{1,0:T(8,128)(2,1)S(1)} %collective-permute-done.19.refs_1_, ...), custom_call_target="tpu_custom_call" | custom-call | flops 1000000 | bytes 1000000 | tf_op jit(solution)/shard_map/weight_grad/pallas_call | solution.py:776
  231.5 17.1 %collective-permute-done.23.refs_2_ = bf16[384,1024]{1,0:T(8,128)(2,1)S(1)} collective-permute-done((bf16[384,1024]{1,0:T(8,128)(2,1)S(1)}, bf16[384,1024]{1,0:T(8,128)(2,1)S(1)}, u32[]{:S(2)}, u32[]{:S(2)}) %collective-permute-start.23) | collective-permute-done | bytes 786464 | tf_op jit(solution)/shard_map/ppermute | solution.py:1071
  248.7 3.0 mid_back.1
  255.3 2.6 layer_products.1
  258.0 5.7 %collective-permute-done.25.refs_1_ = bf16[384,512]{1,0:T(8,128)(2,1)S(1)} collective-permute-done((bf16[384,512]{1,0:T(8,128)(2,1)S(1)}, bf16[384,512]{1,0:T(8,128)(2,1)S(1)}, u32[]{:S(2)}, u32[]{:S(2)}) %collective-permute-start.25) | collective-permute-done | bytes 393248 | tf_op jit(solution)/shard_map/ppermute | solution.py:1071
  263.7 8.0 %collective-permute-done.26.refs_2_ = bf16[384,512]{1,0:T(8,128)(2,1)S(1)} collective-permute-done((bf16[384,512]{1,0:T(8,128)(2,1)S(1)}, bf16[384,512]{1,0:T(8,128)(2,1)S(1)}, u32[]{:S(2)}, u32[]{:S(2)}) %collective-permute-start.26) | collective-permute-done | bytes 393248 | tf_op jit(solution)/shard_map/ppermute | solution.py:1071
  271.8 5.3 %ungate_rows.1 = (bf16[1536,512]{1,0:T(8,128)(2,1)S(1)}, bf16[1536,512]{1,0:T(8,128)(2,1)S(1)}, f32[1,256]{1,0:T(1,128)S(1)}, bf16[768,1024]{1,0:T(8,128)(2,1)S(...) custom-call(bf16[1536,512]{1,0:T(8,128)(2,1)S(1)} %copy-done.30, ...), custom_call_target="tpu_custom_call", output_to_operand_aliasing={{3}: (8, {}), {4}: (9, {}), {5}: (10, {})} | custom-call | flops 1000000 | bytes 1000000 | tf_op jit(solution)/shard_map/ungate_rows/pallas_call | solution.py:541
  277.1 2.9 weight_grad.4
  280.1 1.9 collective-permute-done.32.refs_3_
  284.3 5.0 %all-to-all-start.1 = ((bf16[4,4,32,2816]{3,2,1,0:T(8,128)(2,1)}), bf16[4,4,32,2816]{3,2,1,0:T(8,128)(2,1)}, u32[]{:S(2)}, u32[]{:S(2)}) async-start(bf16[4,4,32,2816]{3,2,1,0:T(8,128)(2,1)} %copy-done.2), calls=%async_computation.1 | async-start | bytes 5767168 | tf_op jit(solution)/shard_map/all_to_all | solution.py:1110
  292.8 29.9 %recurrence_backward.1 = (bf16[1536,1280]{1,0:T(8,128)(2,1)}, f32[8,1024]{1,0:T(8,128)}) custom-call(bf16[1536,1024]{1,0:T(8,128)(2,1)} %get-tuple-element.83.edge_ref.proj_ref, bf16[1536,1024]{1,0:T(8,128)(2,1)} %get-tuple-element.83.edge_ref.proj_ref, f32[8,1024]{1,0:T(8,128)} %select_maximum_fusion.refs_4_.conv_ref, f32[1536,128]{1,0:T(8,128)} %copy-done.5, ...), custom_call_target="tpu_custom_call" | custom-call | flops 1000000 | bytes 1000000 | tf_op jit(solution)/shard_map/recurrence_backward/pallas_call | solution.py:356
  322.7 2.1 copy-done.20
  325.6 14.9 %unpack.1 = (bf16[1536,1792]{1,0:T(8,128)(2,1)S(1)}, f32[1,1024]{1,0:T(1,128)}, bf16[4,4,32,1280]{3,2,1,0:T(8,128)(2,1)S(1)}, bf16[4,4,32,1280]{3,2,1,0:T(8,128)(2,1)}) custom-call(s32[3]{0:T(128)S(1)} %pad_add_fusion.words_ref, bf16[1536,1280]{1,0:T(8,128)(2,1)S(1)} %copy-done.20, bf16[1536,512]{1,0:T(8,128)(2,1)S(1)} %copy-done.15, ...), custom_call_target="tpu_custom_call" | custom-call | flops 1000000 | bytes 1000000 | tf_op jit(solution)/shard_map/unpack/pallas_call | solution.py:651
  340.5 2.3 copy-done.18
  343.9 12.0 %unproject.1 = (bf16[384,1024]{1,0:T(8,128)(2,1)}, bf16[384,1024]{1,0:T(8,128)(2,1)}, bf16[384,1024]{1,0:T(8,128)(2,1)}, bf16[384,1024]{1,0:T(8,128)(2,1)}) custom-call(bf16[1536,1792]{1,0:T(8,128)(2,1)} %copy-done.18, bf16[1024,1664]{1,0:T(8,128)(2,1)} %get-tuple-element.126.refs_2_.w_ref), custom_call_target="tpu_custom_call" | custom-call | flops 1000000 | bytes 1000000 | tf_op jit(solution)/shard_map/unproject/pallas_call | solution.py:694
  355.9 5.0 %collective-permute-done.29.refs_2_ = bf16[768,1024]{1,0:T(8,128)(2,1)} collective-permute-done((bf16[768,1024]{1,0:T(8,128)(2,1)}, bf16[768,1024]{1,0:T(8,128)(2,1)}, u32[]{:S(2)}, u32[]{:S(2)}) %collective-permute-start.29) | collective-permute-done | bytes 1572896 | tf_op jit(solution)/shard_map/ppermute | solution.py:1071
  360.9 5.8 %weight_grad.5 = (bf16[4,4,32,512]{3,2,1,0:T(8,128)(2,1)}, bf16[4,4,32,512]{3,2,1,0:T(8,128)(2,1)}) custom-call(s32[3]{0:T(128)} %copy-done.50, bf16[384,1024]{1,0:T(8,128)(2,1)} %copy-done.28, bf16[768,1024]{1,0:T(8,128)(2,1)} %collective-permute-done.28.refs_1_, bf16[768,1024]{1,0:T(8,128)(2,1)} %collective-permute-done.29.refs_2_, ...), custom_call_target="tpu_custom_call" | custom-call | flops 1000000 | bytes 1000000 | tf_op jit(solution)/shard_map/weight_grad/pallas_call | solution.py:776
  366.8 2.1 collective-permute-done.37.refs_3_
  371.6 5.0 %all-to-all-start.2 = ((bf16[4,4,32,1792]{3,2,1,0:T(8,128)(2,1)}), bf16[4,4,32,1792]{3,2,1,0:T(8,128)(2,1)S(1)}, u32[]{:S(2)}, u32[]{:S(2)}) async-start(bf16[4,4,32,1792]{3,2,1,0:T(8,128)(2,1)} %joined.3.refs_4_), calls=%async_computation.2 | async-start | bytes 3670016 | tf_op jit(solution)/shard_map/all_to_all | solution.py:1110
  380.0 17.1 %collective-permute-done.33.refs_1_ = bf16[384,1024]{1,0:T(8,128)(2,1)S(1)} collective-permute-done((bf16[384,1024]{1,0:T(8,128)(2,1)}, bf16[384,1024]{1,0:T(8,128)(2,1)S(1)}, u32[]{:S(2)}, u32[]{:S(2)}) %collective-permute-start.33) | collective-permute-done | bytes 786464 | tf_op jit(solution)/shard_map/ppermute | solution.py:1071
  397.2 15.9 %collective-permute-done.34.refs_2_ = bf16[384,1024]{1,0:T(8,128)(2,1)S(1)} collective-permute-done((bf16[384,1024]{1,0:T(8,128)(2,1)}, bf16[384,1024]{1,0:T(8,128)(2,1)S(1)}, u32[]{:S(2)}, u32[]{:S(2)}) %collective-permute-start.34) | collective-permute-done | bytes 786464 | tf_op jit(solution)/shard_map/ppermute | solution.py:1071
  416.3 3.1 all-to-all-done.2.refs_1_
  420.5 3.4 row_sums.1
  424.0 3.7 all-to-all-start.3
  427.7 3.2 fusion.12
  430.9 11.3 %all-to-all-done.3.pieces_ref = bf16[4,32,4608]{2,1,0:T(8,128)(2,1)S(1)} async-done(((bf16[4,32,4608]{2,1,0:T(8,128)(2,1)}), bf16[4,32,4608]{2,1,0:T(8,128)(2,1)S(1)}, u32[]{:S(2)}, u32[]{:S(2)}) %all-to-all-start.3) | async-done | bytes 1179680 | tf_op jit(solution)/shard_map/all_to_all | solution.py:1201
  (297 shorter events, 93.6 us)
Async XLA Ops:
  7.2 73.3 %all-gather.5.cloned.1.call-start = ((), (), s32[]{:S(2)}) async-start(), calls=%async_computation.4 | async-start | bytes 3833856 | tf_op jit(solution)/shard_map/all_gather | solution.py:1318
  13.7 6.3 %collective-permute-start = (bf16[32,1664]{1,0:T(8,128)(2,1)S(1)}, bf16[32,1664]{1,0:T(8,128)(2,1)S(1)}, u32[]{:S(2)}, u32[]{:S(2)}) collective-permute-start(bf16[32,1664]{1,0:T(8,128)(2,1)S(1)} %get-tuple-element.207), channel_id=1, source_target_pairs={{0,8},{8,0},{16,24},{24,16},{1,9},{9,1},{17,25},{25,17},{2,10},{10... | collective-permute-start | bytes 319496 | tf_op jit(solution)/shard_map/ppermute | solution.py:1071
  16.7 5.8 %collective-permute-start.1 = (bf16[32,1664]{1,0:T(8,128)(2,1)S(1)}, bf16[32,1664]{1,0:T(8,128)(2,1)S(1)}, u32[]{:S(2)}, u32[]{:S(2)}) collective-permute-start(bf16[32,1664]{1,0:T(8,128)(2,1)S(1)} %get-tuple-element.206), channel_id=1, source_target_pairs={{0,16},{8,24},{16,0},{24,8},{1,17},{9,25},{17,1},{25,9},{2,18},{10... | collective-permute-start | bytes 319496 | tf_op jit(solution)/shard_map/ppermute | solution.py:1071
  18.2 5.6 %collective-permute-start.2 = (bf16[32,1664]{1,0:T(8,128)(2,1)S(1)}, bf16[32,1664]{1,0:T(8,128)(2,1)S(1)}, u32[]{:S(2)}, u32[]{:S(2)}) collective-permute-start(bf16[32,1664]{1,0:T(8,128)(2,1)S(1)} %get-tuple-element.205), channel_id=1, source_target_pairs={{0,24},{8,16},{16,8},{24,0},{1,25},{9,17},{17,9},{25,1},{2,26},{10... | collective-permute-start | bytes 319496 | tf_op jit(solution)/shard_map/ppermute | solution.py:1071
  24.7 141.7 %all-gather.7.cloned.1.call-start = ((), (), s32[]{:S(2)}) async-start(), calls=%async_computation.5 | async-start | bytes 5308416 | tf_op jit(solution)/shard_map/all_gather | solution.py:1360
  25.7 9.0 %collective-permute-start.3 = (bf16[32,2432]{1,0:T(8,128)(2,1)S(1)}, bf16[32,2432]{1,0:T(8,128)(2,1)S(1)}, u32[]{:S(2)}, u32[]{:S(2)}) collective-permute-start(bf16[32,2432]{1,0:T(8,128)(2,1)S(1)} %get-tuple-element.203), channel_id=1, source_target_pairs={{0,8},{8,0},{16,24},{24,16},{1,9},{9,1},{17,25},{25,17},{2,10},{10... | collective-permute-start | bytes 466952 | tf_op jit(solution)/shard_map/ppermute | solution.py:1071
  26.6 9.6 %collective-permute-start.4 = (bf16[32,2432]{1,0:T(8,128)(2,1)S(1)}, bf16[32,2432]{1,0:T(8,128)(2,1)S(1)}, u32[]{:S(2)}, u32[]{:S(2)}) collective-permute-start(bf16[32,2432]{1,0:T(8,128)(2,1)S(1)} %get-tuple-element.202), channel_id=1, source_target_pairs={{0,16},{8,24},{16,0},{24,8},{1,17},{9,25},{17,1},{25,9},{2,18},{10... | collective-permute-start | bytes 466952 | tf_op jit(solution)/shard_map/ppermute | solution.py:1071
  27.5 8.8 %collective-permute-start.5 = (bf16[32,2432]{1,0:T(8,128)(2,1)S(1)}, bf16[32,2432]{1,0:T(8,128)(2,1)S(1)}, u32[]{:S(2)}, u32[]{:S(2)}) collective-permute-start(bf16[32,2432]{1,0:T(8,128)(2,1)S(1)} %get-tuple-element.201), channel_id=1, source_target_pairs={{0,24},{8,16},{16,8},{24,0},{1,25},{9,17},{17,9},{25,1},{2,26},{10... | collective-permute-start | bytes 466952 | tf_op jit(solution)/shard_map/ppermute | solution.py:1071
  29.3 11.4 %collective-permute-start.6 = (bf16[32,2048]{1,0:T(8,128)(2,1)S(1)}, bf16[32,2048]{1,0:T(8,128)(2,1)}, u32[]{:S(2)}, u32[]{:S(2)}) collective-permute-start(bf16[32,2048]{1,0:T(8,128)(2,1)S(1)} %bitcast.153), channel_id=1, source_target_pairs={{0,2},{1,3},{2,0},{3,1},{4,6},{5,7},{6,4},{7,5},{8,10},{9,11},{10,... | collective-permute-start | bytes 393224 | tf_op jit(solution)/shard_map/ppermute | solution.py:1071
  30.9 16.1 %collective-permute-start.7 = (bf16[32,2048]{1,0:T(8,128)(2,1)S(1)}, bf16[32,2048]{1,0:T(8,128)(2,1)}, u32[]{:S(2)}, u32[]{:S(2)}) collective-permute-start(bf16[32,2048]{1,0:T(8,128)(2,1)S(1)} %bitcast.154), channel_id=1, source_target_pairs={{0,4},{1,5},{2,6},{3,7},{4,0},{5,1},{6,2},{7,3},{8,12},{9,13},{10,... | collective-permute-start | bytes 393224 | tf_op jit(solution)/shard_map/ppermute | solution.py:1071
  33.5 289.1 %copy-start.50 = (s32[3]{0:T(128)}, s32[3]{0:T(128)S(1)}, u32[]{:S(2)}) copy-start(s32[3]{0:T(128)S(1)} %pad_add_fusion.words_ref) | copy-start | bytes 40
  34.7 12.2 %collective-permute-start.8 = (bf16[32,2048]{1,0:T(8,128)(2,1)S(1)}, bf16[32,2048]{1,0:T(8,128)(2,1)S(1)}, u32[]{:S(2)}, u32[]{:S(2)}) collective-permute-start(bf16[32,2048]{1,0:T(8,128)(2,1)S(1)} %bitcast.155), channel_id=1, source_target_pairs={{0,6},{1,7},{2,4},{3,5},{4,2},{5,3},{6,0},{7,1},{8,14},{9,15},{10,... | collective-permute-start | bytes 393224 | tf_op jit(solution)/shard_map/ppermute | solution.py:1071
  38.3 32.2 %collective-permute-start.10 = (bf16[384,1024]{1,0:T(8,128)(2,1)S(1)}, bf16[384,1024]{1,0:T(8,128)(2,1)S(1)}, u32[]{:S(2)}, u32[]{:S(2)}) collective-permute-start(bf16[384,1024]{1,0:T(8,128)(2,1)S(1)} %broadcast_add_fusion.1.refs_0_), channel_id=1, source_target_pairs={{0,16},{8,24},{16,0},{24,8},{1,17},{9,25},{17,1},{25,9},{2,18},{10... | collective-permute-start | bytes 2359304 | tf_op jit(solution)/shard_map/ppermute | solution.py:1071
  38.9 31.7 %collective-permute-start.11 = (bf16[384,1024]{1,0:T(8,128)(2,1)S(1)}, bf16[384,1024]{1,0:T(8,128)(2,1)}, u32[]{:S(2)}, u32[]{:S(2)}) collective-permute-start(bf16[384,1024]{1,0:T(8,128)(2,1)S(1)} %broadcast_add_fusion.1.refs_0_), channel_id=1, source_target_pairs={{0,24},{8,16},{16,8},{24,0},{1,25},{9,17},{17,9},{25,1},{2,26},{10... | collective-permute-start | bytes 2359304 | tf_op jit(solution)/shard_map/ppermute | solution.py:1071
  40.6 31.4 %collective-permute-start.9 = (bf16[384,1024]{1,0:T(8,128)(2,1)S(1)}, bf16[384,1024]{1,0:T(8,128)(2,1)}, u32[]{:S(2)}, u32[]{:S(2)}) collective-permute-start(bf16[384,1024]{1,0:T(8,128)(2,1)S(1)} %broadcast_add_fusion.1.refs_0_), channel_id=1, source_target_pairs={{0,8},{8,0},{16,24},{24,16},{1,9},{9,1},{17,25},{25,17},{2,10},{10... | collective-permute-start | bytes 2359304 | tf_op jit(solution)/shard_map/ppermute | solution.py:1071
  72.8 57.6 %collective-permute-start.12 = (bf16[384,1024]{1,0:T(8,128)(2,1)}, bf16[384,1024]{1,0:T(8,128)(2,1)}, u32[]{:S(2)}, u32[]{:S(2)}) collective-permute-start(bf16[384,1024]{1,0:T(8,128)(2,1)} %get-tuple-element.90.refs_8_), channel_id=1, source_target_pairs={{0,8},{8,0},{16,24},{24,16},{1,9},{9,1},{17,25},{25,17},{2,10},{10... | collective-permute-start | bytes 2359304 | tf_op jit(solution)/shard_map/ppermute | solution.py:1071
  74.1 56.3 %collective-permute-start.13 = (bf16[384,1024]{1,0:T(8,128)(2,1)}, bf16[384,1024]{1,0:T(8,128)(2,1)}, u32[]{:S(2)}, u32[]{:S(2)}) collective-permute-start(bf16[384,1024]{1,0:T(8,128)(2,1)} %get-tuple-element.90.refs_8_), channel_id=1, source_target_pairs={{0,16},{8,24},{16,0},{24,8},{1,17},{9,25},{17,1},{25,9},{2,18},{10... | collective-permute-start | bytes 2359304 | tf_op jit(solution)/shard_map/ppermute | solution.py:1071
  75.2 55.2 %collective-permute-start.14 = (bf16[384,1024]{1,0:T(8,128)(2,1)}, bf16[384,1024]{1,0:T(8,128)(2,1)}, u32[]{:S(2)}, u32[]{:S(2)}) collective-permute-start(bf16[384,1024]{1,0:T(8,128)(2,1)} %get-tuple-element.90.refs_8_), channel_id=1, source_target_pairs={{0,24},{8,16},{16,8},{24,0},{1,25},{9,17},{17,9},{25,1},{2,26},{10... | collective-permute-start | bytes 2359304 | tf_op jit(solution)/shard_map/ppermute | solution.py:1071
  76.4 54.5 %all-to-all-start = ((bf16[4,4,32,2048]{3,2,1,0:T(8,128)(2,1)}), bf16[4,4,32,2048]{3,2,1,0:T(8,128)(2,1)S(1)}, u32[]{:S(2)}, u32[]{:S(2)}) async-start(bf16[4,4,32,2048]{3,2,1,0:T(8,128)(2,1)} %get-tuple-element.89), calls=%async_computation | async-start | bytes 4194304 | tf_op jit(solution)/shard_map/all_to_all | solution.py:1362
  138.6 4.2 collective-permute-start.15
  138.6 12.0 %collective-permute-start.16 = (bf16[384,512]{1,0:T(8,128)(2,1)S(1)}, bf16[384,512]{1,0:T(8,128)(2,1)S(1)}, u32[]{:S(2)}, u32[]{:S(2)}) collective-permute-start(bf16[384,512]{1,0:T(8,128)(2,1)S(1)} %get-tuple-element.95.refs_5_), channel_id=1, source_target_pairs={{0,8},{8,0},{16,24},{24,16},{1,9},{9,1},{17,25},{25,17},{2,10},{10... | collective-permute-start | bytes 1179656 | tf_op jit(solution)/shard_map/ppermute | solution.py:1071
  140.3 19.6 %collective-permute-start.17 = (bf16[384,512]{1,0:T(8,128)(2,1)S(1)}, bf16[384,512]{1,0:T(8,128)(2,1)S(1)}, u32[]{:S(2)}, u32[]{:S(2)}) collective-permute-start(bf16[384,512]{1,0:T(8,128)(2,1)S(1)} %get-tuple-element.96.refs_6_), channel_id=1, source_target_pairs={{0,16},{8,24},{16,0},{24,8},{1,17},{9,25},{17,1},{25,9},{2,18},{10... | collective-permute-start | bytes 1179656 | tf_op jit(solution)/shard_map/ppermute | solution.py:1071
  141.8 18.1 %collective-permute-start.18 = (bf16[384,512]{1,0:T(8,128)(2,1)S(1)}, bf16[384,512]{1,0:T(8,128)(2,1)S(1)}, u32[]{:S(2)}, u32[]{:S(2)}) collective-permute-start(bf16[384,512]{1,0:T(8,128)(2,1)S(1)} %get-tuple-element.97.refs_7_), channel_id=1, source_target_pairs={{0,24},{8,16},{16,8},{24,0},{1,25},{9,17},{17,9},{25,1},{2,26},{10... | collective-permute-start | bytes 1179656 | tf_op jit(solution)/shard_map/ppermute | solution.py:1071
  162.8 85.8 %copy-start.16 = (f32[384,1024]{1,0:T(8,128)}, f32[384,1024]{1,0:T(8,128)S(1)}, u32[]{:S(2)}) copy-start(f32[384,1024]{1,0:T(8,128)S(1)} %get-tuple-element.98.residual_ref) | copy-start | bytes 4718596
  162.8 20.7 %collective-permute-start.19 = (bf16[384,1024]{1,0:T(8,128)(2,1)}, bf16[384,1024]{1,0:T(8,128)(2,1)S(1)}, u32[]{:S(2)}, u32[]{:S(2)}) collective-permute-start(bf16[384,1024]{1,0:T(8,128)(2,1)} %get-tuple-element.100.refs_0_), channel_id=1, source_target_pairs={{0,8},{8,0},{16,24},{24,16},{1,9},{9,1},{17,25},{25,17},{2,10},{10... | collective-permute-start | bytes 2359304 | tf_op jit(solution)/shard_map/ppermute | solution.py:1071
  164.1 37.3 %collective-permute-start.22 = (bf16[384,1024]{1,0:T(8,128)(2,1)}, bf16[384,1024]{1,0:T(8,128)(2,1)S(1)}, u32[]{:S(2)}, u32[]{:S(2)}) collective-permute-start(bf16[384,1024]{1,0:T(8,128)(2,1)} %get-tuple-element.100.refs_0_), channel_id=1, source_target_pairs={{0,24},{8,16},{16,8},{24,0},{1,25},{9,17},{17,9},{25,1},{2,26},{10... | collective-permute-start | bytes 2359304 | tf_op jit(solution)/shard_map/ppermute | solution.py:1071
  165.8 43.2 %collective-permute-start.21 = (bf16[384,1024]{1,0:T(8,128)(2,1)}, bf16[384,1024]{1,0:T(8,128)(2,1)}, u32[]{:S(2)}, u32[]{:S(2)}) collective-permute-start(bf16[384,1024]{1,0:T(8,128)(2,1)} %get-tuple-element.100.refs_0_), channel_id=1, source_target_pairs={{0,16},{8,24},{16,0},{24,8},{1,17},{9,25},{17,1},{25,9},{2,18},{10... | collective-permute-start | bytes 2359304 | tf_op jit(solution)/shard_map/ppermute | solution.py:1071
  189.1 28.2 %collective-permute-start.20 = (bf16[384,1024]{1,0:T(8,128)(2,1)S(1)}, bf16[384,1024]{1,0:T(8,128)(2,1)S(1)}, u32[]{:S(2)}, u32[]{:S(2)}) collective-permute-start(bf16[384,1024]{1,0:T(8,128)(2,1)S(1)} %convolution_convert_fusion.2), channel_id=1, source_target_pairs={{0,8},{8,0},{16,24},{24,16},{1,9},{9,1},{17,25},{25,17},{2,10},{10... | collective-permute-start | bytes 2359304 | tf_op jit(solution)/shard_map/ppermute | solution.py:1071
  207.2 41.5 %collective-permute-start.24 = (bf16[384,1024]{1,0:T(8,128)(2,1)S(1)}, bf16[384,1024]{1,0:T(8,128)(2,1)S(1)}, u32[]{:S(2)}, u32[]{:S(2)}) collective-permute-start(bf16[384,1024]{1,0:T(8,128)(2,1)S(1)} %convolution_convert_fusion.1), channel_id=1, source_target_pairs={{0,24},{8,16},{16,8},{24,0},{1,25},{9,17},{17,9},{25,1},{2,26},{10... | collective-permute-start | bytes 2359304 | tf_op jit(solution)/shard_map/ppermute | solution.py:1071
  215.3 33.4 %collective-permute-start.23 = (bf16[384,1024]{1,0:T(8,128)(2,1)S(1)}, bf16[384,1024]{1,0:T(8,128)(2,1)S(1)}, u32[]{:S(2)}, u32[]{:S(2)}) collective-permute-start(bf16[384,1024]{1,0:T(8,128)(2,1)S(1)} %convolution_convert_fusion.refs_16_), channel_id=1, source_target_pairs={{0,16},{8,24},{16,0},{24,8},{1,17},{9,25},{17,1},{25,9},{2,18},{10... | collective-permute-start | bytes 2359304 | tf_op jit(solution)/shard_map/ppermute | solution.py:1071
  251.7 30.4 %collective-permute-start.31 = (bf16[4,4,32,2304]{3,2,1,0:T(8,128)(2,1)S(1)}, bf16[4,4,32,2304]{3,2,1,0:T(8,128)(2,1)S(1)}, u32[]{:S(2)}, u32[]{:S(2)}) collective-permute-start(bf16[4,4,32,2304]{3,2,1,0:T(8,128)(2,1)S(1)} %get-tuple-element.124), channel_id=1, source_target_pairs={{0,1},{1,0},{2,3},{3,2},{4,5},{5,4},{6,7},{7,6},{8,9},{9,8},{10,11... | collective-permute-start | bytes 7077896 | tf_op jit(solution)/shard_map/ppermute | solution.py:1071
  251.8 12.0 %collective-permute-start.25 = (bf16[384,512]{1,0:T(8,128)(2,1)S(1)}, bf16[384,512]{1,0:T(8,128)(2,1)S(1)}, u32[]{:S(2)}, u32[]{:S(2)}) collective-permute-start(bf16[384,512]{1,0:T(8,128)(2,1)S(1)} %get-tuple-element.106), channel_id=1, source_target_pairs={{0,8},{8,0},{16,24},{24,16},{1,9},{9,1},{17,25},{25,17},{2,10},{10... | collective-permute-start | bytes 1179656 | tf_op jit(solution)/shard_map/ppermute | solution.py:1071
  252.1 19.6 %collective-permute-start.26 = (bf16[384,512]{1,0:T(8,128)(2,1)S(1)}, bf16[384,512]{1,0:T(8,128)(2,1)S(1)}, u32[]{:S(2)}, u32[]{:S(2)}) collective-permute-start(bf16[384,512]{1,0:T(8,128)(2,1)S(1)} %get-tuple-element.107), channel_id=1, source_target_pairs={{0,16},{8,24},{16,0},{24,8},{1,17},{9,25},{17,1},{25,9},{2,18},{10... | collective-permute-start | bytes 1179656 | tf_op jit(solution)/shard_map/ppermute | solution.py:1071
  253.6 18.2 %collective-permute-start.27 = (bf16[384,512]{1,0:T(8,128)(2,1)S(1)}, bf16[384,512]{1,0:T(8,128)(2,1)S(1)}, u32[]{:S(2)}, u32[]{:S(2)}) collective-permute-start(bf16[384,512]{1,0:T(8,128)(2,1)S(1)} %get-tuple-element.108), channel_id=1, source_target_pairs={{0,24},{8,16},{16,8},{24,0},{1,25},{9,17},{17,9},{25,1},{2,26},{10... | collective-permute-start | bytes 1179656 | tf_op jit(solution)/shard_map/ppermute | solution.py:1071
  280.1 1.9 collective-permute-start.32
  284.3 76.6 %all-to-all-start.1 = ((bf16[4,4,32,2816]{3,2,1,0:T(8,128)(2,1)}), bf16[4,4,32,2816]{3,2,1,0:T(8,128)(2,1)}, u32[]{:S(2)}, u32[]{:S(2)}) async-start(bf16[4,4,32,2816]{3,2,1,0:T(8,128)(2,1)} %copy-done.2), calls=%async_computation.1 | async-start | bytes 5767168 | tf_op jit(solution)/shard_map/all_to_all | solution.py:1110
  289.3 66.6 %collective-permute-start.28 = (bf16[768,1024]{1,0:T(8,128)(2,1)}, bf16[768,1024]{1,0:T(8,128)(2,1)}, u32[]{:S(2)}, u32[]{:S(2)}) collective-permute-start(bf16[768,1024]{1,0:T(8,128)(2,1)} %copy-done.34), channel_id=1, source_target_pairs={{0,8},{8,0},{16,24},{24,16},{1,9},{9,1},{17,25},{25,17},{2,10},{10... | collective-permute-start | bytes 4718600 | tf_op jit(solution)/shard_map/ppermute | solution.py:1071
  290.9 70.0 %collective-permute-start.29 = (bf16[768,1024]{1,0:T(8,128)(2,1)}, bf16[768,1024]{1,0:T(8,128)(2,1)}, u32[]{:S(2)}, u32[]{:S(2)}) collective-permute-start(bf16[768,1024]{1,0:T(8,128)(2,1)} %copy-done.35), channel_id=1, source_target_pairs={{0,16},{8,24},{16,0},{24,8},{1,17},{9,25},{17,1},{25,9},{2,18},{10... | collective-permute-start | bytes 4718600 | tf_op jit(solution)/shard_map/ppermute | solution.py:1071
  291.3 69.6 %collective-permute-start.30 = (bf16[768,1024]{1,0:T(8,128)(2,1)}, bf16[768,1024]{1,0:T(8,128)(2,1)}, u32[]{:S(2)}, u32[]{:S(2)}) collective-permute-start(bf16[768,1024]{1,0:T(8,128)(2,1)} %copy-done.36), channel_id=1, source_target_pairs={{0,24},{8,16},{16,8},{24,0},{1,25},{9,17},{17,9},{25,1},{2,26},{10... | collective-permute-start | bytes 4718600 | tf_op jit(solution)/shard_map/ppermute | solution.py:1071
  343.9 22.9 %collective-permute-start.36 = (bf16[4,4,32,1280]{3,2,1,0:T(8,128)(2,1)}, bf16[4,4,32,1280]{3,2,1,0:T(8,128)(2,1)S(1)}, u32[]{:S(2)}, u32[]{:S(2)}) collective-permute-start(bf16[4,4,32,1280]{3,2,1,0:T(8,128)(2,1)} %get-tuple-element.141), channel_id=1, source_target_pairs={{0,1},{1,0},{2,3},{3,2},{4,5},{5,4},{6,7},{7,6},{8,9},{9,8},{10,11... | collective-permute-start | bytes 3932168 | tf_op jit(solution)/shard_map/ppermute | solution.py:1071
  366.7 2.1 collective-permute-start.37
  371.6 41.5 %copy-start.13 = (bf16[1,384,1024]{2,1,0:T(8,128)(2,1)S(1)}, bf16[1,384,1024]{2,1,0:T(8,128)(2,1)}, u32[]{:S(2)}) copy-start(bf16[1,384,1024]{2,1,0:T(8,128)(2,1)} %param.15) | copy-start | bytes 2359300
  371.6 41.5 %copy-start.27 = (bf16[384,1024]{1,0:T(8,128)(2,1)S(1)}, bf16[384,1024]{1,0:T(8,128)(2,1)}, u32[]{:S(2)}) copy-start(bf16[384,1024]{1,0:T(8,128)(2,1)} %get-tuple-element.136.refs_8_.refs_0_) | copy-start | bytes 2359300
  371.6 47.8 %all-to-all-start.2 = ((bf16[4,4,32,1792]{3,2,1,0:T(8,128)(2,1)}), bf16[4,4,32,1792]{3,2,1,0:T(8,128)(2,1)S(1)}, u32[]{:S(2)}, u32[]{:S(2)}) async-start(bf16[4,4,32,1792]{3,2,1,0:T(8,128)(2,1)} %joined.3.refs_4_), calls=%async_computation.2 | async-start | bytes 3670016 | tf_op jit(solution)/shard_map/all_to_all | solution.py:1110
  376.5 20.6 %collective-permute-start.33 = (bf16[384,1024]{1,0:T(8,128)(2,1)}, bf16[384,1024]{1,0:T(8,128)(2,1)S(1)}, u32[]{:S(2)}, u32[]{:S(2)}) collective-permute-start(bf16[384,1024]{1,0:T(8,128)(2,1)} %get-tuple-element.137), channel_id=1, source_target_pairs={{0,8},{8,0},{16,24},{24,16},{1,9},{9,1},{17,25},{25,17},{2,10},{10... | collective-permute-start | bytes 2359304 | tf_op jit(solution)/shard_map/ppermute | solution.py:1071
  377.0 36.1 %collective-permute-start.34 = (bf16[384,1024]{1,0:T(8,128)(2,1)}, bf16[384,1024]{1,0:T(8,128)(2,1)S(1)}, u32[]{:S(2)}, u32[]{:S(2)}) collective-permute-start(bf16[384,1024]{1,0:T(8,128)(2,1)} %get-tuple-element.138), channel_id=1, source_target_pairs={{0,16},{8,24},{16,0},{24,8},{1,17},{9,25},{17,1},{25,9},{2,18},{10... | collective-permute-start | bytes 2359304 | tf_op jit(solution)/shard_map/ppermute | solution.py:1071
  378.3 34.8 %collective-permute-start.35 = (bf16[384,1024]{1,0:T(8,128)(2,1)}, bf16[384,1024]{1,0:T(8,128)(2,1)S(1)}, u32[]{:S(2)}, u32[]{:S(2)}) collective-permute-start(bf16[384,1024]{1,0:T(8,128)(2,1)} %get-tuple-element.139), channel_id=1, source_target_pairs={{0,24},{8,16},{16,8},{24,0},{1,25},{9,17},{17,9},{25,1},{2,26},{10... | collective-permute-start | bytes 2359304 | tf_op jit(solution)/shard_map/ppermute | solution.py:1071
  424.0 18.2 %all-to-all-start.3 = ((bf16[4,32,4608]{2,1,0:T(8,128)(2,1)}), bf16[4,32,4608]{2,1,0:T(8,128)(2,1)S(1)}, u32[]{:S(2)}, u32[]{:S(2)}) async-start(bf16[4,32,4608]{2,1,0:T(8,128)(2,1)} %row_sums.1), calls=%async_computation.3 | async-start | bytes 2359296 | tf_op jit(solution)/shard_map/all_to_all | solution.py:1201
  (65 other events, 567.4 us)
Sparse Core Ops, SparseCore 0:
  24.8 47.0 all-gather.4
  74.1 50.9 all-gather.6

commit v2 on v1

--- a/solution.py
+++ b/solution.py
@@ -1433,7 +1433,9 @@
     )
     out_sum.pair()
     last_sum = mix_sum.beside(out_sum)
-    in_grad = in_back(layer_in[0], res_grad, full_gin, normed_chunks, [last_sum.half])
+    ffn_total = row_sums([ffn_sum], [last_sum.half])
+    in_grad = in_back(layer_in[0], res_grad, full_gin, normed_chunks, [ffn_total])
+    ffn_sum.parts = ffn_total[None]
     layer_out = residual + sum(
         c.astype(F32) for c in [layer_own] + [b[count:] for b in both]
     )

time: 458 us -> 457 us (level)
    unnamed x141 -> x145, local copies, waits for them, and re-layouts: 21.5 us -> 22.4 us
  transfers between devices with their start and end apart: 44 -> 44, of which waited for: 23 -> 22; matrix products, arithmetic and copies ran while one was open for 8% -> 8% of each run, Pallas kernels for 32% -> 32%
where the time goes in v2:
time: 457 us; the launch traced here: 452 us
  Pallas kernels  153 us (33%)
  waiting for transfers between devices  152 us (33%)
  starting transfers between devices  59.6 us (13%)
  local copies, waits for them, and re-layouts  37.9 us (8%)
  matrix products  21.4 us (5%)
  between operations  19.5 us (4%)
  other arithmetic  8.98 us (2%)
    ppermute x38, waiting for transfers between devices, swapped(): return lax.ppermute(value, axis, [(i, i ^ mask) for i in range(devices)])  135 us
    ppermute x38, starting transfers between devices, swapped(): return lax.ppermute(value, axis, [(i, i ^ mask) for i in range(devices)])  41.8 us
    pallas_call x1, Pallas kernels, backward_recurrence(): pl.pallas_call(functools.partial(backward_kernel, heads), grid=(count //...  29.9 us
    pallas_call x1, Pallas kernels, forward_recurrence(): pl.pallas_call(functools.partial(forward_kernel, heads), grid=(count // s...  24.7 us
    pallas_call x3, Pallas kernels, weight_grad(): pl.pallas_call(functools.partial(weight_grad_kernel, split, tiles, sums),...  22.9 us
    unnamed x145, local copies, waits for them, and re-layouts  22.4 us
    pallas_call x1, Pallas kernels, project(): pl.pallas_call(functools.partial(project_kernel, channels, chunks, len(pa...  20 us
    dot_general x8, matrix products, dot(): return jnp.dot(left, right, preferred_element_type=jnp.float32)  15.8 us
  transfers between devices with their start and end apart: 44, of which 22 were waited for; matrix products, arithmetic and copies ran while one was open for 8% of the time, Pallas kernels for 32%

profile of v2, /device:TPU:0, one launch (start us, length us, event | category | flops | bytes accessed | tf_op | source)
XLA Modules:
  0.0 451.8 jit_solution(2901187946592604065)
XLA Ops:
  9.0 2.8 concatenate.62
  13.7 3.0 collective-permute-start
  19.9 2.6 collective-permute-done.1
  30.9 2.6 collective-permute-start.7
  42.9 4.0 collective-permute-done.7
  50.9 19.7 %collective-permute-done.10.refs_2_.refs_4_ = bf16[384,1024]{1,0:T(8,128)(2,1)S(1)} collective-permute-done((bf16[384,1024]{1,0:T(8,128)(2,1)S(1)}, bf16[384,1024]{1,0:T(8,128)(2,1)S(1)}, u32[]{:S(2)}, u32[]{:S(2)}) %collective-permute-start.10) | collective-permute-done | bytes 786464 | tf_op jit(solution)/shard_map/ppermute | solution.py:1071
  76.4 4.1 all-to-all-start
  85.6 20.0 %project.1 = (bf16[1536,1024]{1,0:T(8,128)(2,1)}, f32[1536,512]{1,0:T(8,128)}, bf16[1536,1024]{1,0:T(8,128)(2,1)}, f32[1536,128]{1,0:T(8,128)}, bf16[1024,1664]{1,0:T(8,128)(2,1)}) custom-call(s32[1]{0:T(128)} %bitcast.rank_ref, f32[1,1024]{1,0:T(1,128)} %reshape.116.gain_ref, bf16[8,4,32,1664]{3,2,1,0:T(8,128)(2,1)} %bitcast.136, f32[1536,128]{1,0:T(8,128)} %copy-done.5, ...), custom_call_target="tpu_custom_call" | custom-call | flops 1000000 | bytes 1000000 | tf_op jit(solution)/shard_map/project/pallas_call | solution.py:433
  105.6 24.7 %recurrence_forward.1 = (bf16[1536,512]{1,0:T(8,128)(2,1)}, bf16[12,2,128,256]{3,2,1,0:T(8,128)(2,1)}, bf16[12,2,128,256]{3,2,1,0:T(8,128)(2,1)}, bf16[12,2,128,...) custom-call(bf16[1536,1024]{1,0:T(8,128)(2,1)} %get-tuple-element.83, ...), custom_call_target="tpu_custom_call" | custom-call | flops 1000000 | bytes 1000000 | tf_op jit(solution)/shard_map/recurrence_forward/pallas_call | solution.py:335
  130.8 1.9 copy-done.7
  134.1 3.2 gate_rows.1
  146.0 4.5 %collective-permute-done.16.refs_1_ = bf16[384,512]{1,0:T(8,128)(2,1)S(1)} collective-permute-done((bf16[384,512]{1,0:T(8,128)(2,1)S(1)}, bf16[384,512]{1,0:T(8,128)(2,1)S(1)}, u32[]{:S(2)}, u32[]{:S(2)}) %collective-permute-start.16) | collective-permute-done | bytes 393248 | tf_op jit(solution)/shard_map/ppermute | solution.py:1071
  150.6 9.3 %collective-permute-done.17.refs_2_ = bf16[384,512]{1,0:T(8,128)(2,1)S(1)} collective-permute-done((bf16[384,512]{1,0:T(8,128)(2,1)S(1)}, bf16[384,512]{1,0:T(8,128)(2,1)S(1)}, u32[]{:S(2)}, u32[]{:S(2)}) %collective-permute-start.17) | collective-permute-done | bytes 393248 | tf_op jit(solution)/shard_map/ppermute | solution.py:1071
  159.8 2.1 out_project.1
  165.5 2.3 copy-done.19
  173.8 8.7 %collective-permute-done.19.refs_1_ = bf16[384,1024]{1,0:T(8,128)(2,1)S(1)} collective-permute-done((bf16[384,1024]{1,0:T(8,128)(2,1)S(1)}, bf16[384,1024]{1,0:T(8,128)(2,1)S(1)}, u32[]{:S(2)}, u32[]{:S(2)}) %collective-permute-start.19) | collective-permute-done | bytes 786464 | tf_op jit(solution)/shard_map/ppermute | solution.py:1071
  183.9 2.2 multiply_convert_fusion.9
  189.9 10.5 %collective-permute-done.22.refs_3_ = bf16[384,1024]{1,0:T(8,128)(2,1)} collective-permute-done((bf16[384,1024]{1,0:T(8,128)(2,1)S(1)}, bf16[384,1024]{1,0:T(8,128)(2,1)}, u32[]{:S(2)}, u32[]{:S(2)}) %collective-permute-start.22) | collective-permute-done | bytes 786464 | tf_op jit(solution)/shard_map/ppermute | solution.py:1071
  200.4 2.7 fusion.15
  203.2 2.2 multiply_convert_fusion.7
  209.2 2.5 fusion.13
  211.8 2.2 multiply_convert_fusion.5
  216.6 14.3 %weight_grad.3 = (bf16[4,4,32,2304]{3,2,1,0:T(8,128)(2,1)S(1)}, bf16[4,4,32,2304]{3,2,1,0:T(8,128)(2,1)S(1)}) custom-call(s32[3]{0:T(128)S(1)} %pad_add_fusion.words_ref, bf16[384,1024]{1,0:T(8,128)(2,1)S(1)} %get-tuple-element.100.refs_0_, bf16[384,1024]{1,0:T(8,128)(2,1)S(1)} %collective-permute-done.19.refs_1_, ...), custom_call_target="tpu_custom_call" | custom-call | flops 1000000 | bytes 1000000 | tf_op jit(solution)/shard_map/weight_grad/pallas_call | solution.py:776
  230.9 17.3 %collective-permute-done.23.refs_2_ = bf16[384,1024]{1,0:T(8,128)(2,1)S(1)} collective-permute-done((bf16[384,1024]{1,0:T(8,128)(2,1)S(1)}, bf16[384,1024]{1,0:T(8,128)(2,1)S(1)}, u32[]{:S(2)}, u32[]{:S(2)}) %collective-permute-start.23) | collective-permute-done | bytes 786464 | tf_op jit(solution)/shard_map/ppermute | solution.py:1071
  248.2 3.0 mid_back.1
  255.8 2.6 layer_products.1
  258.5 5.8 %collective-permute-done.25.refs_1_ = bf16[384,512]{1,0:T(8,128)(2,1)S(1)} collective-permute-done((bf16[384,512]{1,0:T(8,128)(2,1)S(1)}, bf16[384,512]{1,0:T(8,128)(2,1)S(1)}, u32[]{:S(2)}, u32[]{:S(2)}) %collective-permute-start.25) | collective-permute-done | bytes 393248 | tf_op jit(solution)/shard_map/ppermute | solution.py:1071
  264.2 8.2 %collective-permute-done.26.refs_2_ = bf16[384,512]{1,0:T(8,128)(2,1)S(1)} collective-permute-done((bf16[384,512]{1,0:T(8,128)(2,1)S(1)}, bf16[384,512]{1,0:T(8,128)(2,1)S(1)}, u32[]{:S(2)}, u32[]{:S(2)}) %collective-permute-start.26) | collective-permute-done | bytes 393248 | tf_op jit(solution)/shard_map/ppermute | solution.py:1071
  272.5 5.3 %ungate_rows.1 = (bf16[1536,512]{1,0:T(8,128)(2,1)S(1)}, bf16[1536,512]{1,0:T(8,128)(2,1)S(1)}, f32[1,256]{1,0:T(1,128)S(1)}, bf16[768,1024]{1,0:T(8,128)(2,1)S(...) custom-call(bf16[1536,512]{1,0:T(8,128)(2,1)S(1)} %copy-done.31, ...), custom_call_target="tpu_custom_call", output_to_operand_aliasing={{3}: (8, {}), {4}: (9, {}), {5}: (10, {})} | custom-call | flops 1000000 | bytes 1000000 | tf_op jit(solution)/shard_map/ungate_rows/pallas_call | solution.py:541
  277.9 2.8 weight_grad.4
  280.9 1.9 collective-permute-done.32.refs_3_
  285.0 4.9 %all-to-all-start.1 = ((bf16[4,4,32,2816]{3,2,1,0:T(8,128)(2,1)}), bf16[4,4,32,2816]{3,2,1,0:T(8,128)(2,1)}, u32[]{:S(2)}, u32[]{:S(2)}) async-start(bf16[4,4,32,2816]{3,2,1,0:T(8,128)(2,1)} %copy-done.2), calls=%async_computation.1 | async-start | bytes 5767168 | tf_op jit(solution)/shard_map/all_to_all | solution.py:1110
  293.4 29.9 %recurrence_backward.1 = (bf16[1536,1280]{1,0:T(8,128)(2,1)}, f32[8,1024]{1,0:T(8,128)}) custom-call(bf16[1536,1024]{1,0:T(8,128)(2,1)} %get-tuple-element.83.edge_ref.proj_ref, bf16[1536,1024]{1,0:T(8,128)(2,1)} %get-tuple-element.83.edge_ref.proj_ref, f32[8,1024]{1,0:T(8,128)} %select_maximum_fusion.refs_4_.conv_ref, f32[1536,128]{1,0:T(8,128)} %copy-done.5, ...), custom_call_target="tpu_custom_call" | custom-call | flops 1000000 | bytes 1000000 | tf_op jit(solution)/shard_map/recurrence_backward/pallas_call | solution.py:356
  323.4 2.1 copy-done.21
  326.2 14.9 %unpack.1 = (bf16[1536,1792]{1,0:T(8,128)(2,1)S(1)}, f32[1,1024]{1,0:T(1,128)}, bf16[4,4,32,1280]{3,2,1,0:T(8,128)(2,1)S(1)}, bf16[4,4,32,1280]{3,2,1,0:T(8,128)(2,1)}) custom-call(s32[3]{0:T(128)S(1)} %pad_add_fusion.words_ref, bf16[1536,1280]{1,0:T(8,128)(2,1)S(1)} %copy-done.21, bf16[1536,512]{1,0:T(8,128)(2,1)S(1)} %copy-done.15, ...), custom_call_target="tpu_custom_call" | custom-call | flops 1000000 | bytes 1000000 | tf_op jit(solution)/shard_map/unpack/pallas_call | solution.py:651
  341.1 2.4 copy-done.18
  344.6 12.0 %unproject.1 = (bf16[384,1024]{1,0:T(8,128)(2,1)}, bf16[384,1024]{1,0:T(8,128)(2,1)}, bf16[384,1024]{1,0:T(8,128)(2,1)}, bf16[384,1024]{1,0:T(8,128)(2,1)}) custom-call(bf16[1536,1792]{1,0:T(8,128)(2,1)} %copy-done.18, bf16[1024,1664]{1,0:T(8,128)(2,1)} %get-tuple-element.126.refs_2_.w_ref), custom_call_target="tpu_custom_call" | custom-call | flops 1000000 | bytes 1000000 | tf_op jit(solution)/shard_map/unproject/pallas_call | solution.py:694
  356.7 4.8 %collective-permute-done.29.refs_2_ = bf16[768,1024]{1,0:T(8,128)(2,1)} collective-permute-done((bf16[768,1024]{1,0:T(8,128)(2,1)}, bf16[768,1024]{1,0:T(8,128)(2,1)}, u32[]{:S(2)}, u32[]{:S(2)}) %collective-permute-start.29) | collective-permute-done | bytes 1572896 | tf_op jit(solution)/shard_map/ppermute | solution.py:1071
  361.5 5.8 %weight_grad.5 = (bf16[4,4,32,512]{3,2,1,0:T(8,128)(2,1)}, bf16[4,4,32,512]{3,2,1,0:T(8,128)(2,1)}) custom-call(s32[3]{0:T(128)} %copy-done.51, bf16[384,1024]{1,0:T(8,128)(2,1)} %copy-done.29, bf16[768,1024]{1,0:T(8,128)(2,1)} %collective-permute-done.28.refs_1_, bf16[768,1024]{1,0:T(8,128)(2,1)} %collective-permute-done.29.refs_2_, ...), custom_call_target="tpu_custom_call" | custom-call | flops 1000000 | bytes 1000000 | tf_op jit(solution)/shard_map/weight_grad/pallas_call | solution.py:776
  367.3 2.1 collective-permute-done.37.refs_3_
  372.2 5.0 %all-to-all-start.2 = ((bf16[4,4,32,1792]{3,2,1,0:T(8,128)(2,1)}), bf16[4,4,32,1792]{3,2,1,0:T(8,128)(2,1)S(1)}, u32[]{:S(2)}, u32[]{:S(2)}) async-start(bf16[4,4,32,1792]{3,2,1,0:T(8,128)(2,1)} %joined.3.refs_1_), calls=%async_computation.2 | async-start | bytes 3670016 | tf_op jit(solution)/shard_map/all_to_all | solution.py:1110
  380.8 2.2 row_sums.2.refs_4_
  383.0 14.9 %collective-permute-done.33.refs_1_ = bf16[384,1024]{1,0:T(8,128)(2,1)S(1)} collective-permute-done((bf16[384,1024]{1,0:T(8,128)(2,1)}, bf16[384,1024]{1,0:T(8,128)(2,1)S(1)}, u32[]{:S(2)}, u32[]{:S(2)}) %collective-permute-start.33) | collective-permute-done | bytes 786464 | tf_op jit(solution)/shard_map/ppermute | solution.py:1071
  397.9 16.0 %collective-permute-done.34.refs_2_ = bf16[384,1024]{1,0:T(8,128)(2,1)S(1)} collective-permute-done((bf16[384,1024]{1,0:T(8,128)(2,1)}, bf16[384,1024]{1,0:T(8,128)(2,1)S(1)}, u32[]{:S(2)}, u32[]{:S(2)}) %collective-permute-start.34) | collective-permute-done | bytes 786464 | tf_op jit(solution)/shard_map/ppermute | solution.py:1071
  415.7 4.4 all-to-all-done.2.refs_1_
  422.7 3.7 all-to-all-start.3
  426.3 3.2 fusion.12
  429.5 11.3 %all-to-all-done.3.pieces_ref = bf16[4,32,4608]{2,1,0:T(8,128)(2,1)S(1)} async-done(((bf16[4,32,4608]{2,1,0:T(8,128)(2,1)}), bf16[4,32,4608]{2,1,0:T(8,128)(2,1)S(1)}, u32[]{:S(2)}, u32[]{:S(2)}) %all-to-all-start.3) | async-done | bytes 1179680 | tf_op jit(solution)/shard_map/all_to_all | solution.py:1201
  (302 shorter events, 93.7 us)
Async XLA Ops:
  7.2 73.3 %all-gather.5.cloned.1.call-start = ((), (), s32[]{:S(2)}) async-start(), calls=%async_computation.4 | async-start | bytes 3833856 | tf_op jit(solution)/shard_map/all_gather | solution.py:1318
  13.7 6.3 %collective-permute-start = (bf16[32,1664]{1,0:T(8,128)(2,1)S(1)}, bf16[32,1664]{1,0:T(8,128)(2,1)S(1)}, u32[]{:S(2)}, u32[]{:S(2)}) collective-permute-start(bf16[32,1664]{1,0:T(8,128)(2,1)S(1)} %get-tuple-element.207), channel_id=1, source_target_pairs={{0,8},{8,0},{16,24},{24,16},{1,9},{9,1},{17,25},{25,17},{2,10},{10... | collective-permute-start | bytes 319496 | tf_op jit(solution)/shard_map/ppermute | solution.py:1071
  16.7 5.8 %collective-permute-start.1 = (bf16[32,1664]{1,0:T(8,128)(2,1)S(1)}, bf16[32,1664]{1,0:T(8,128)(2,1)S(1)}, u32[]{:S(2)}, u32[]{:S(2)}) collective-permute-start(bf16[32,1664]{1,0:T(8,128)(2,1)S(1)} %get-tuple-element.206), channel_id=1, source_target_pairs={{0,16},{8,24},{16,0},{24,8},{1,17},{9,25},{17,1},{25,9},{2,18},{10... | collective-permute-start | bytes 319496 | tf_op jit(solution)/shard_map/ppermute | solution.py:1071
  18.2 5.6 %collective-permute-start.2 = (bf16[32,1664]{1,0:T(8,128)(2,1)S(1)}, bf16[32,1664]{1,0:T(8,128)(2,1)S(1)}, u32[]{:S(2)}, u32[]{:S(2)}) collective-permute-start(bf16[32,1664]{1,0:T(8,128)(2,1)S(1)} %get-tuple-element.205), channel_id=1, source_target_pairs={{0,24},{8,16},{16,8},{24,0},{1,25},{9,17},{17,9},{25,1},{2,26},{10... | collective-permute-start | bytes 319496 | tf_op jit(solution)/shard_map/ppermute | solution.py:1071
  24.7 140.8 %all-gather.7.cloned.1.call-start = ((), (), s32[]{:S(2)}) async-start(), calls=%async_computation.5 | async-start | bytes 5308416 | tf_op jit(solution)/shard_map/all_gather | solution.py:1360
  25.7 9.0 %collective-permute-start.3 = (bf16[32,2432]{1,0:T(8,128)(2,1)S(1)}, bf16[32,2432]{1,0:T(8,128)(2,1)S(1)}, u32[]{:S(2)}, u32[]{:S(2)}) collective-permute-start(bf16[32,2432]{1,0:T(8,128)(2,1)S(1)} %get-tuple-element.203), channel_id=1, source_target_pairs={{0,8},{8,0},{16,24},{24,16},{1,9},{9,1},{17,25},{25,17},{2,10},{10... | collective-permute-start | bytes 466952 | tf_op jit(solution)/shard_map/ppermute | solution.py:1071
  26.6 9.6 %collective-permute-start.4 = (bf16[32,2432]{1,0:T(8,128)(2,1)S(1)}, bf16[32,2432]{1,0:T(8,128)(2,1)S(1)}, u32[]{:S(2)}, u32[]{:S(2)}) collective-permute-start(bf16[32,2432]{1,0:T(8,128)(2,1)S(1)} %get-tuple-element.202), channel_id=1, source_target_pairs={{0,16},{8,24},{16,0},{24,8},{1,17},{9,25},{17,1},{25,9},{2,18},{10... | collective-permute-start | bytes 466952 | tf_op jit(solution)/shard_map/ppermute | solution.py:1071
  27.5 8.8 %collective-permute-start.5 = (bf16[32,2432]{1,0:T(8,128)(2,1)S(1)}, bf16[32,2432]{1,0:T(8,128)(2,1)S(1)}, u32[]{:S(2)}, u32[]{:S(2)}) collective-permute-start(bf16[32,2432]{1,0:T(8,128)(2,1)S(1)} %get-tuple-element.201), channel_id=1, source_target_pairs={{0,24},{8,16},{16,8},{24,0},{1,25},{9,17},{17,9},{25,1},{2,26},{10... | collective-permute-start | bytes 466952 | tf_op jit(solution)/shard_map/ppermute | solution.py:1071
  29.3 11.4 %collective-permute-start.6 = (bf16[32,2048]{1,0:T(8,128)(2,1)S(1)}, bf16[32,2048]{1,0:T(8,128)(2,1)}, u32[]{:S(2)}, u32[]{:S(2)}) collective-permute-start(bf16[32,2048]{1,0:T(8,128)(2,1)S(1)} %bitcast.155), channel_id=1, source_target_pairs={{0,2},{1,3},{2,0},{3,1},{4,6},{5,7},{6,4},{7,5},{8,10},{9,11},{10,... | collective-permute-start | bytes 393224 | tf_op jit(solution)/shard_map/ppermute | solution.py:1071
  30.9 16.1 %collective-permute-start.7 = (bf16[32,2048]{1,0:T(8,128)(2,1)S(1)}, bf16[32,2048]{1,0:T(8,128)(2,1)}, u32[]{:S(2)}, u32[]{:S(2)}) collective-permute-start(bf16[32,2048]{1,0:T(8,128)(2,1)S(1)} %bitcast.156), channel_id=1, source_target_pairs={{0,4},{1,5},{2,6},{3,7},{4,0},{5,1},{6,2},{7,3},{8,12},{9,13},{10,... | collective-permute-start | bytes 393224 | tf_op jit(solution)/shard_map/ppermute | solution.py:1071
  33.5 289.8 %copy-start.51 = (s32[3]{0:T(128)}, s32[3]{0:T(128)S(1)}, u32[]{:S(2)}) copy-start(s32[3]{0:T(128)S(1)} %pad_add_fusion.words_ref) | copy-start | bytes 40
  34.7 12.2 %collective-permute-start.8 = (bf16[32,2048]{1,0:T(8,128)(2,1)S(1)}, bf16[32,2048]{1,0:T(8,128)(2,1)S(1)}, u32[]{:S(2)}, u32[]{:S(2)}) collective-permute-start(bf16[32,2048]{1,0:T(8,128)(2,1)S(1)} %bitcast.157), channel_id=1, source_target_pairs={{0,6},{1,7},{2,4},{3,5},{4,2},{5,3},{6,0},{7,1},{8,14},{9,15},{10,... | collective-permute-start | bytes 393224 | tf_op jit(solution)/shard_map/ppermute | solution.py:1071
  38.3 32.2 %collective-permute-start.10 = (bf16[384,1024]{1,0:T(8,128)(2,1)S(1)}, bf16[384,1024]{1,0:T(8,128)(2,1)S(1)}, u32[]{:S(2)}, u32[]{:S(2)}) collective-permute-start(bf16[384,1024]{1,0:T(8,128)(2,1)S(1)} %broadcast_add_fusion.1.refs_0_), channel_id=1, source_target_pairs={{0,16},{8,24},{16,0},{24,8},{1,17},{9,25},{17,1},{25,9},{2,18},{10... | collective-permute-start | bytes 2359304 | tf_op jit(solution)/shard_map/ppermute | solution.py:1071
  38.9 31.7 %collective-permute-start.11 = (bf16[384,1024]{1,0:T(8,128)(2,1)S(1)}, bf16[384,1024]{1,0:T(8,128)(2,1)}, u32[]{:S(2)}, u32[]{:S(2)}) collective-permute-start(bf16[384,1024]{1,0:T(8,128)(2,1)S(1)} %broadcast_add_fusion.1.refs_0_), channel_id=1, source_target_pairs={{0,24},{8,16},{16,8},{24,0},{1,25},{9,17},{17,9},{25,1},{2,26},{10... | collective-permute-start | bytes 2359304 | tf_op jit(solution)/shard_map/ppermute | solution.py:1071
  40.6 31.4 %collective-permute-start.9 = (bf16[384,1024]{1,0:T(8,128)(2,1)S(1)}, bf16[384,1024]{1,0:T(8,128)(2,1)}, u32[]{:S(2)}, u32[]{:S(2)}) collective-permute-start(bf16[384,1024]{1,0:T(8,128)(2,1)S(1)} %broadcast_add_fusion.1.refs_0_), channel_id=1, source_target_pairs={{0,8},{8,0},{16,24},{24,16},{1,9},{9,1},{17,25},{25,17},{2,10},{10... | collective-permute-start | bytes 2359304 | tf_op jit(solution)/shard_map/ppermute | solution.py:1071
  72.8 57.5 %collective-permute-start.12 = (bf16[384,1024]{1,0:T(8,128)(2,1)}, bf16[384,1024]{1,0:T(8,128)(2,1)}, u32[]{:S(2)}, u32[]{:S(2)}) collective-permute-start(bf16[384,1024]{1,0:T(8,128)(2,1)} %get-tuple-element.90.refs_8_), channel_id=1, source_target_pairs={{0,8},{8,0},{16,24},{24,16},{1,9},{9,1},{17,25},{25,17},{2,10},{10... | collective-permute-start | bytes 2359304 | tf_op jit(solution)/shard_map/ppermute | solution.py:1071
  74.1 56.2 %collective-permute-start.13 = (bf16[384,1024]{1,0:T(8,128)(2,1)}, bf16[384,1024]{1,0:T(8,128)(2,1)}, u32[]{:S(2)}, u32[]{:S(2)}) collective-permute-start(bf16[384,1024]{1,0:T(8,128)(2,1)} %get-tuple-element.90.refs_8_), channel_id=1, source_target_pairs={{0,16},{8,24},{16,0},{24,8},{1,17},{9,25},{17,1},{25,9},{2,18},{10... | collective-permute-start | bytes 2359304 | tf_op jit(solution)/shard_map/ppermute | solution.py:1071
  75.2 55.2 %collective-permute-start.14 = (bf16[384,1024]{1,0:T(8,128)(2,1)}, bf16[384,1024]{1,0:T(8,128)(2,1)}, u32[]{:S(2)}, u32[]{:S(2)}) collective-permute-start(bf16[384,1024]{1,0:T(8,128)(2,1)} %get-tuple-element.90.refs_8_), channel_id=1, source_target_pairs={{0,24},{8,16},{16,8},{24,0},{1,25},{9,17},{17,9},{25,1},{2,26},{10... | collective-permute-start | bytes 2359304 | tf_op jit(solution)/shard_map/ppermute | solution.py:1071
  76.4 54.4 %all-to-all-start = ((bf16[4,4,32,2048]{3,2,1,0:T(8,128)(2,1)}), bf16[4,4,32,2048]{3,2,1,0:T(8,128)(2,1)S(1)}, u32[]{:S(2)}, u32[]{:S(2)}) async-start(bf16[4,4,32,2048]{3,2,1,0:T(8,128)(2,1)} %get-tuple-element.89), calls=%async_computation | async-start | bytes 4194304 | tf_op jit(solution)/shard_map/all_to_all | solution.py:1362
  138.5 4.2 collective-permute-start.15
  138.6 12.0 %collective-permute-start.16 = (bf16[384,512]{1,0:T(8,128)(2,1)S(1)}, bf16[384,512]{1,0:T(8,128)(2,1)S(1)}, u32[]{:S(2)}, u32[]{:S(2)}) collective-permute-start(bf16[384,512]{1,0:T(8,128)(2,1)S(1)} %get-tuple-element.95.refs_5_), channel_id=1, source_target_pairs={{0,8},{8,0},{16,24},{24,16},{1,9},{9,1},{17,25},{25,17},{2,10},{10... | collective-permute-start | bytes 1179656 | tf_op jit(solution)/shard_map/ppermute | solution.py:1071
  140.2 19.6 %collective-permute-start.17 = (bf16[384,512]{1,0:T(8,128)(2,1)S(1)}, bf16[384,512]{1,0:T(8,128)(2,1)S(1)}, u32[]{:S(2)}, u32[]{:S(2)}) collective-permute-start(bf16[384,512]{1,0:T(8,128)(2,1)S(1)} %get-tuple-element.96.refs_6_), channel_id=1, source_target_pairs={{0,16},{8,24},{16,0},{24,8},{1,17},{9,25},{17,1},{25,9},{2,18},{10... | collective-permute-start | bytes 1179656 | tf_op jit(solution)/shard_map/ppermute | solution.py:1071
  141.7 18.1 %collective-permute-start.18 = (bf16[384,512]{1,0:T(8,128)(2,1)S(1)}, bf16[384,512]{1,0:T(8,128)(2,1)S(1)}, u32[]{:S(2)}, u32[]{:S(2)}) collective-permute-start(bf16[384,512]{1,0:T(8,128)(2,1)S(1)} %get-tuple-element.97.refs_7_), channel_id=1, source_target_pairs={{0,24},{8,16},{16,8},{24,0},{1,25},{9,17},{17,9},{25,1},{2,26},{10... | collective-permute-start | bytes 1179656 | tf_op jit(solution)/shard_map/ppermute | solution.py:1071
  161.9 86.3 %copy-start.16 = (f32[384,1024]{1,0:T(8,128)}, f32[384,1024]{1,0:T(8,128)S(1)}, u32[]{:S(2)}) copy-start(f32[384,1024]{1,0:T(8,128)S(1)} %get-tuple-element.98.residual_ref) | copy-start | bytes 4718596
  161.9 20.5 %collective-permute-start.19 = (bf16[384,1024]{1,0:T(8,128)(2,1)S(1)}, bf16[384,1024]{1,0:T(8,128)(2,1)S(1)}, u32[]{:S(2)}, u32[]{:S(2)}) collective-permute-start(bf16[384,1024]{1,0:T(8,128)(2,1)S(1)} %get-tuple-element.100.refs_0_), channel_id=1, source_target_pairs={{0,8},{8,0},{16,24},{24,16},{1,9},{9,1},{17,25},{25,17},{2,10},{10... | collective-permute-start | bytes 2359304 | tf_op jit(solution)/shard_map/ppermute | solution.py:1071
  163.2 37.2 %collective-permute-start.22 = (bf16[384,1024]{1,0:T(8,128)(2,1)S(1)}, bf16[384,1024]{1,0:T(8,128)(2,1)}, u32[]{:S(2)}, u32[]{:S(2)}) collective-permute-start(bf16[384,1024]{1,0:T(8,128)(2,1)S(1)} %get-tuple-element.100.refs_0_), channel_id=1, source_target_pairs={{0,24},{8,16},{16,8},{24,0},{1,25},{9,17},{17,9},{25,1},{2,26},{10... | collective-permute-start | bytes 2359304 | tf_op jit(solution)/shard_map/ppermute | solution.py:1071
  165.0 44.3 %collective-permute-start.21 = (bf16[384,1024]{1,0:T(8,128)(2,1)S(1)}, bf16[384,1024]{1,0:T(8,128)(2,1)}, u32[]{:S(2)}, u32[]{:S(2)}) collective-permute-start(bf16[384,1024]{1,0:T(8,128)(2,1)S(1)} %get-tuple-element.100.refs_0_), channel_id=1, source_target_pairs={{0,16},{8,24},{16,0},{24,8},{1,17},{9,25},{17,1},{25,9},{2,18},{10... | collective-permute-start | bytes 2359304 | tf_op jit(solution)/shard_map/ppermute | solution.py:1071
  188.0 28.5 %collective-permute-start.20 = (bf16[384,1024]{1,0:T(8,128)(2,1)S(1)}, bf16[384,1024]{1,0:T(8,128)(2,1)S(1)}, u32[]{:S(2)}, u32[]{:S(2)}) collective-permute-start(bf16[384,1024]{1,0:T(8,128)(2,1)S(1)} %convolution_convert_fusion.2), channel_id=1, source_target_pairs={{0,8},{8,0},{16,24},{24,16},{1,9},{9,1},{17,25},{25,17},{2,10},{10... | collective-permute-start | bytes 2359304 | tf_op jit(solution)/shard_map/ppermute | solution.py:1071
  207.3 40.9 %collective-permute-start.24 = (bf16[384,1024]{1,0:T(8,128)(2,1)S(1)}, bf16[384,1024]{1,0:T(8,128)(2,1)S(1)}, u32[]{:S(2)}, u32[]{:S(2)}) collective-permute-start(bf16[384,1024]{1,0:T(8,128)(2,1)S(1)} %convolution_convert_fusion.1), channel_id=1, source_target_pairs={{0,24},{8,16},{16,8},{24,0},{1,25},{9,17},{17,9},{25,1},{2,26},{10... | collective-permute-start | bytes 2359304 | tf_op jit(solution)/shard_map/ppermute | solution.py:1071
  215.4 32.8 %collective-permute-start.23 = (bf16[384,1024]{1,0:T(8,128)(2,1)S(1)}, bf16[384,1024]{1,0:T(8,128)(2,1)S(1)}, u32[]{:S(2)}, u32[]{:S(2)}) collective-permute-start(bf16[384,1024]{1,0:T(8,128)(2,1)S(1)} %convolution_convert_fusion.refs_16_), channel_id=1, source_target_pairs={{0,16},{8,24},{16,0},{24,8},{1,17},{9,25},{17,1},{25,9},{2,18},{10... | collective-permute-start | bytes 2359304 | tf_op jit(solution)/shard_map/ppermute | solution.py:1071
  252.3 30.5 %collective-permute-start.31 = (bf16[4,4,32,2304]{3,2,1,0:T(8,128)(2,1)S(1)}, bf16[4,4,32,2304]{3,2,1,0:T(8,128)(2,1)S(1)}, u32[]{:S(2)}, u32[]{:S(2)}) collective-permute-start(bf16[4,4,32,2304]{3,2,1,0:T(8,128)(2,1)S(1)} %get-tuple-element.124), channel_id=1, source_target_pairs={{0,1},{1,0},{2,3},{3,2},{4,5},{5,4},{6,7},{7,6},{8,9},{9,8},{10,11... | collective-permute-start | bytes 7077896 | tf_op jit(solution)/shard_map/ppermute | solution.py:1071
  252.3 11.9 %collective-permute-start.25 = (bf16[384,512]{1,0:T(8,128)(2,1)S(1)}, bf16[384,512]{1,0:T(8,128)(2,1)S(1)}, u32[]{:S(2)}, u32[]{:S(2)}) collective-permute-start(bf16[384,512]{1,0:T(8,128)(2,1)S(1)} %get-tuple-element.106), channel_id=1, source_target_pairs={{0,8},{8,0},{16,24},{24,16},{1,9},{9,1},{17,25},{25,17},{2,10},{10... | collective-permute-start | bytes 1179656 | tf_op jit(solution)/shard_map/ppermute | solution.py:1071
  252.8 19.7 %collective-permute-start.26 = (bf16[384,512]{1,0:T(8,128)(2,1)S(1)}, bf16[384,512]{1,0:T(8,128)(2,1)S(1)}, u32[]{:S(2)}, u32[]{:S(2)}) collective-permute-start(bf16[384,512]{1,0:T(8,128)(2,1)S(1)} %get-tuple-element.107), channel_id=1, source_target_pairs={{0,16},{8,24},{16,0},{24,8},{1,17},{9,25},{17,1},{25,9},{2,18},{10... | collective-permute-start | bytes 1179656 | tf_op jit(solution)/shard_map/ppermute | solution.py:1071
  254.4 18.1 %collective-permute-start.27 = (bf16[384,512]{1,0:T(8,128)(2,1)S(1)}, bf16[384,512]{1,0:T(8,128)(2,1)S(1)}, u32[]{:S(2)}, u32[]{:S(2)}) collective-permute-start(bf16[384,512]{1,0:T(8,128)(2,1)S(1)} %get-tuple-element.108), channel_id=1, source_target_pairs={{0,24},{8,16},{16,8},{24,0},{1,25},{9,17},{17,9},{25,1},{2,26},{10... | collective-permute-start | bytes 1179656 | tf_op jit(solution)/shard_map/ppermute | solution.py:1071
  280.9 1.9 collective-permute-start.32
  285.0 76.4 %all-to-all-start.1 = ((bf16[4,4,32,2816]{3,2,1,0:T(8,128)(2,1)}), bf16[4,4,32,2816]{3,2,1,0:T(8,128)(2,1)}, u32[]{:S(2)}, u32[]{:S(2)}) async-start(bf16[4,4,32,2816]{3,2,1,0:T(8,128)(2,1)} %copy-done.2), calls=%async_computation.1 | async-start | bytes 5767168 | tf_op jit(solution)/shard_map/all_to_all | solution.py:1110
  289.9 66.7 %collective-permute-start.28 = (bf16[768,1024]{1,0:T(8,128)(2,1)}, bf16[768,1024]{1,0:T(8,128)(2,1)}, u32[]{:S(2)}, u32[]{:S(2)}) collective-permute-start(bf16[768,1024]{1,0:T(8,128)(2,1)} %copy-done.33), channel_id=1, source_target_pairs={{0,8},{8,0},{16,24},{24,16},{1,9},{9,1},{17,25},{25,17},{2,10},{10... | collective-permute-start | bytes 4718600 | tf_op jit(solution)/shard_map/ppermute | solution.py:1071
  291.5 70.0 %collective-permute-start.29 = (bf16[768,1024]{1,0:T(8,128)(2,1)}, bf16[768,1024]{1,0:T(8,128)(2,1)}, u32[]{:S(2)}, u32[]{:S(2)}) collective-permute-start(bf16[768,1024]{1,0:T(8,128)(2,1)} %copy-done.34), channel_id=1, source_target_pairs={{0,16},{8,24},{16,0},{24,8},{1,17},{9,25},{17,1},{25,9},{2,18},{10... | collective-permute-start | bytes 4718600 | tf_op jit(solution)/shard_map/ppermute | solution.py:1071
  292.0 69.5 %collective-permute-start.30 = (bf16[768,1024]{1,0:T(8,128)(2,1)}, bf16[768,1024]{1,0:T(8,128)(2,1)}, u32[]{:S(2)}, u32[]{:S(2)}) collective-permute-start(bf16[768,1024]{1,0:T(8,128)(2,1)} %copy-done.35), channel_id=1, source_target_pairs={{0,24},{8,16},{16,8},{24,0},{1,25},{9,17},{17,9},{25,1},{2,26},{10... | collective-permute-start | bytes 4718600 | tf_op jit(solution)/shard_map/ppermute | solution.py:1071
  344.6 22.7 %collective-permute-start.36 = (bf16[4,4,32,1280]{3,2,1,0:T(8,128)(2,1)}, bf16[4,4,32,1280]{3,2,1,0:T(8,128)(2,1)S(1)}, u32[]{:S(2)}, u32[]{:S(2)}) collective-permute-start(bf16[4,4,32,1280]{3,2,1,0:T(8,128)(2,1)} %get-tuple-element.141), channel_id=1, source_target_pairs={{0,1},{1,0},{2,3},{3,2},{4,5},{5,4},{6,7},{7,6},{8,9},{9,8},{10,11... | collective-permute-start | bytes 3932168 | tf_op jit(solution)/shard_map/ppermute | solution.py:1071
  367.3 2.1 collective-permute-start.37
  372.2 47.9 %all-to-all-start.2 = ((bf16[4,4,32,1792]{3,2,1,0:T(8,128)(2,1)}), bf16[4,4,32,1792]{3,2,1,0:T(8,128)(2,1)S(1)}, u32[]{:S(2)}, u32[]{:S(2)}) async-start(bf16[4,4,32,1792]{3,2,1,0:T(8,128)(2,1)} %joined.3.refs_1_), calls=%async_computation.2 | async-start | bytes 3670016 | tf_op jit(solution)/shard_map/all_to_all | solution.py:1110
  377.2 20.6 %collective-permute-start.33 = (bf16[384,1024]{1,0:T(8,128)(2,1)}, bf16[384,1024]{1,0:T(8,128)(2,1)S(1)}, u32[]{:S(2)}, u32[]{:S(2)}) collective-permute-start(bf16[384,1024]{1,0:T(8,128)(2,1)} %get-tuple-element.137), channel_id=1, source_target_pairs={{0,8},{8,0},{16,24},{24,16},{1,9},{9,1},{17,25},{25,17},{2,10},{10... | collective-permute-start | bytes 2359304 | tf_op jit(solution)/shard_map/ppermute | solution.py:1071
  377.8 36.1 %collective-permute-start.34 = (bf16[384,1024]{1,0:T(8,128)(2,1)}, bf16[384,1024]{1,0:T(8,128)(2,1)S(1)}, u32[]{:S(2)}, u32[]{:S(2)}) collective-permute-start(bf16[384,1024]{1,0:T(8,128)(2,1)} %get-tuple-element.138), channel_id=1, source_target_pairs={{0,16},{8,24},{16,0},{24,8},{1,17},{9,25},{17,1},{25,9},{2,18},{10... | collective-permute-start | bytes 2359304 | tf_op jit(solution)/shard_map/ppermute | solution.py:1071
  379.3 34.6 %copy-start.28 = (bf16[384,1024]{1,0:T(8,128)(2,1)S(1)}, bf16[384,1024]{1,0:T(8,128)(2,1)}, u32[]{:S(2)}) copy-start(bf16[384,1024]{1,0:T(8,128)(2,1)} %get-tuple-element.136.refs_8_.refs_0_) | copy-start | bytes 2359300
  379.3 34.6 %copy-start.38 = (f32[384,1024]{1,0:T(8,128)S(1)}, f32[384,1024]{1,0:T(8,128)}, u32[]{:S(2)}) copy-start(f32[384,1024]{1,0:T(8,128)} %copy-done.37) | copy-start | bytes 4718596
  379.3 34.6 %collective-permute-start.35 = (bf16[384,1024]{1,0:T(8,128)(2,1)S(1)}, bf16[384,1024]{1,0:T(8,128)(2,1)S(1)}, u32[]{:S(2)}, u32[]{:S(2)}) collective-permute-start(bf16[384,1024]{1,0:T(8,128)(2,1)S(1)} %copy-done.70), channel_id=1, source_target_pairs={{0,24},{8,16},{16,8},{24,0},{1,25},{9,17},{17,9},{25,1},{2,26},{10... | collective-permute-start | bytes 2359304 | tf_op jit(solution)/shard_map/ppermute | solution.py:1071
  422.7 18.2 %all-to-all-start.3 = ((bf16[4,32,4608]{2,1,0:T(8,128)(2,1)}), bf16[4,32,4608]{2,1,0:T(8,128)(2,1)S(1)}, u32[]{:S(2)}, u32[]{:S(2)}) async-start(bf16[4,32,4608]{2,1,0:T(8,128)(2,1)} %copy-done.20), calls=%async_computation.3 | async-start | bytes 2359296 | tf_op jit(solution)/shard_map/all_to_all | solution.py:1201
  (67 other events, 602.7 us)
Sparse Core Ops, SparseCore 0:
  24.8 47.0 all-gather.4
  74.1 50.9 all-gather.6

commit v3 on v2

--- a/solution.py
+++ b/solution.py
@@ -1449,8 +1449,9 @@
         grad_go = lax.dynamic_slice_in_dim(
             small_sum[4:6].reshape(-1), device * gain_o.shape[0], gain_o.shape[0]
         )
-        grad_gmid = lax.dynamic_slice_in_dim(small_sum[8:16].reshape(-1), device * rows, rows)
-        grad_gin = lax.dynamic_slice_in_dim(small_sum[16:24].reshape(-1), device * rows, rows)
+        grad_gmid, grad_gin = lax.dynamic_slice_in_dim(
+            small_sum[8:24].reshape(2, -1), device * rows, rows, 1
+        )
         return (
             layer_out, in_grad[None], g_qkv, g_gate, g_beta, g_conv.T,
             grad_gin, grad_go, g_out.T, grad_gmid, g_gu, g_down.T,

time: 457 us -> 456 us (level)
  no operation moved by 1% of the time
where the time goes in v3:
time: 456 us; the launch traced here: 451 us
  Pallas kernels  153 us (34%)
  waiting for transfers between devices  152 us (33%)
  starting transfers between devices  59.6 us (13%)
  local copies, waits for them, and re-layouts  37.4 us (8%)
  matrix products  21.4 us (5%)
  between operations  19.5 us (4%)
  other arithmetic  8.98 us (2%)
    ppermute x38, waiting for transfers between devices, swapped(): return lax.ppermute(value, axis, [(i, i ^ mask) for i in range(devices)])  135 us
    ppermute x38, starting transfers between devices, swapped(): return lax.ppermute(value, axis, [(i, i ^ mask) for i in range(devices)])  41.8 us
    pallas_call x1, Pallas kernels, backward_recurrence(): pl.pallas_call(functools.partial(backward_kernel, heads), grid=(count //...  29.9 us
    pallas_call x1, Pallas kernels, forward_recurrence(): pl.pallas_call(functools.partial(forward_kernel, heads), grid=(count // s...  24.7 us
    pallas_call x3, Pallas kernels, weight_grad(): pl.pallas_call(functools.partial(weight_grad_kernel, split, tiles, sums),...  22.9 us
    unnamed x145, local copies, waits for them, and re-layouts  22.4 us
    pallas_call x1, Pallas kernels, project(): pl.pallas_call(functools.partial(project_kernel, channels, chunks, len(pa...  20 us
    dot_general x8, matrix products, dot(): return jnp.dot(left, right, preferred_element_type=jnp.float32)  15.8 us
  transfers between devices with their start and end apart: 44, of which 22 were waited for; matrix products, arithmetic and copies ran while one was open for 8% of the time, Pallas kernels for 32%

profile of v3, /device:TPU:0, one launch (start us, length us, event | category | flops | bytes accessed | tf_op | source)
XLA Modules:
  0.0 451.2 jit_solution(12204967226863919537)
XLA Ops:
  9.0 2.8 concatenate.62
  13.7 3.0 collective-permute-start
  19.9 2.6 collective-permute-done.1
  30.9 2.6 collective-permute-start.7
  42.9 4.0 collective-permute-done.7
  50.9 19.7 %collective-permute-done.10.refs_2_.refs_4_ = bf16[384,1024]{1,0:T(8,128)(2,1)S(1)} collective-permute-done((bf16[384,1024]{1,0:T(8,128)(2,1)S(1)}, bf16[384,1024]{1,0:T(8,128)(2,1)S(1)}, u32[]{:S(2)}, u32[]{:S(2)}) %collective-permute-start.10) | collective-permute-done | bytes 786464 | tf_op jit(solution)/shard_map/ppermute | solution.py:1071
  76.4 4.1 all-to-all-start
  85.6 20.0 %project.1 = (bf16[1536,1024]{1,0:T(8,128)(2,1)}, f32[1536,512]{1,0:T(8,128)}, bf16[1536,1024]{1,0:T(8,128)(2,1)}, f32[1536,128]{1,0:T(8,128)}, bf16[1024,1664]{1,0:T(8,128)(2,1)}) custom-call(s32[1]{0:T(128)} %bitcast.rank_ref, f32[1,1024]{1,0:T(1,128)} %reshape.113.gain_ref, bf16[8,4,32,1664]{3,2,1,0:T(8,128)(2,1)} %bitcast.136, f32[1536,128]{1,0:T(8,128)} %copy-done.5, ...), custom_call_target="tpu_custom_call" | custom-call | flops 1000000 | bytes 1000000 | tf_op jit(solution)/shard_map/project/pallas_call | solution.py:433
  105.6 24.7 %recurrence_forward.1 = (bf16[1536,512]{1,0:T(8,128)(2,1)}, bf16[12,2,128,256]{3,2,1,0:T(8,128)(2,1)}, bf16[12,2,128,256]{3,2,1,0:T(8,128)(2,1)}, bf16[12,2,128,...) custom-call(bf16[1536,1024]{1,0:T(8,128)(2,1)} %get-tuple-element.83, ...), custom_call_target="tpu_custom_call" | custom-call | flops 1000000 | bytes 1000000 | tf_op jit(solution)/shard_map/recurrence_forward/pallas_call | solution.py:335
  130.8 1.9 copy-done.7
  134.1 3.2 gate_rows.1
  146.0 4.5 %collective-permute-done.16.refs_1_ = bf16[384,512]{1,0:T(8,128)(2,1)S(1)} collective-permute-done((bf16[384,512]{1,0:T(8,128)(2,1)S(1)}, bf16[384,512]{1,0:T(8,128)(2,1)S(1)}, u32[]{:S(2)}, u32[]{:S(2)}) %collective-permute-start.16) | collective-permute-done | bytes 393248 | tf_op jit(solution)/shard_map/ppermute | solution.py:1071
  150.6 9.3 %collective-permute-done.17.refs_2_ = bf16[384,512]{1,0:T(8,128)(2,1)S(1)} collective-permute-done((bf16[384,512]{1,0:T(8,128)(2,1)S(1)}, bf16[384,512]{1,0:T(8,128)(2,1)S(1)}, u32[]{:S(2)}, u32[]{:S(2)}) %collective-permute-start.17) | collective-permute-done | bytes 393248 | tf_op jit(solution)/shard_map/ppermute | solution.py:1071
  159.8 2.1 out_project.1
  165.5 2.3 copy-done.19
  173.8 8.7 %collective-permute-done.19.refs_1_ = bf16[384,1024]{1,0:T(8,128)(2,1)S(1)} collective-permute-done((bf16[384,1024]{1,0:T(8,128)(2,1)S(1)}, bf16[384,1024]{1,0:T(8,128)(2,1)S(1)}, u32[]{:S(2)}, u32[]{:S(2)}) %collective-permute-start.19) | collective-permute-done | bytes 786464 | tf_op jit(solution)/shard_map/ppermute | solution.py:1071
  183.9 2.2 multiply_convert_fusion.9
  189.9 10.5 %collective-permute-done.22.refs_3_ = bf16[384,1024]{1,0:T(8,128)(2,1)} collective-permute-done((bf16[384,1024]{1,0:T(8,128)(2,1)S(1)}, bf16[384,1024]{1,0:T(8,128)(2,1)}, u32[]{:S(2)}, u32[]{:S(2)}) %collective-permute-start.22) | collective-permute-done | bytes 786464 | tf_op jit(solution)/shard_map/ppermute | solution.py:1071
  200.4 2.7 fusion.15
  203.2 2.2 multiply_convert_fusion.7
  209.2 2.5 fusion.13
  211.8 2.2 multiply_convert_fusion.5
  216.6 14.3 %weight_grad.3 = (bf16[4,4,32,2304]{3,2,1,0:T(8,128)(2,1)S(1)}, bf16[4,4,32,2304]{3,2,1,0:T(8,128)(2,1)S(1)}) custom-call(s32[3]{0:T(128)S(1)} %pad_add_fusion.words_ref, bf16[384,1024]{1,0:T(8,128)(2,1)S(1)} %get-tuple-element.100.refs_0_, bf16[384,1024]{1,0:T(8,128)(2,1)S(1)} %collective-permute-done.19.refs_1_, ...), custom_call_target="tpu_custom_call" | custom-call | flops 1000000 | bytes 1000000 | tf_op jit(solution)/shard_map/weight_grad/pallas_call | solution.py:776
  230.9 17.3 %collective-permute-done.23.refs_2_ = bf16[384,1024]{1,0:T(8,128)(2,1)S(1)} collective-permute-done((bf16[384,1024]{1,0:T(8,128)(2,1)S(1)}, bf16[384,1024]{1,0:T(8,128)(2,1)S(1)}, u32[]{:S(2)}, u32[]{:S(2)}) %collective-permute-start.23) | collective-permute-done | bytes 786464 | tf_op jit(solution)/shard_map/ppermute | solution.py:1071
  248.2 3.0 mid_back.1
  255.8 2.6 layer_products.1
  258.5 5.8 %collective-permute-done.25.refs_1_ = bf16[384,512]{1,0:T(8,128)(2,1)S(1)} collective-permute-done((bf16[384,512]{1,0:T(8,128)(2,1)S(1)}, bf16[384,512]{1,0:T(8,128)(2,1)S(1)}, u32[]{:S(2)}, u32[]{:S(2)}) %collective-permute-start.25) | collective-permute-done | bytes 393248 | tf_op jit(solution)/shard_map/ppermute | solution.py:1071
  264.2 8.2 %collective-permute-done.26.refs_2_ = bf16[384,512]{1,0:T(8,128)(2,1)S(1)} collective-permute-done((bf16[384,512]{1,0:T(8,128)(2,1)S(1)}, bf16[384,512]{1,0:T(8,128)(2,1)S(1)}, u32[]{:S(2)}, u32[]{:S(2)}) %collective-permute-start.26) | collective-permute-done | bytes 393248 | tf_op jit(solution)/shard_map/ppermute | solution.py:1071
  272.5 5.3 %ungate_rows.1 = (bf16[1536,512]{1,0:T(8,128)(2,1)S(1)}, bf16[1536,512]{1,0:T(8,128)(2,1)S(1)}, f32[1,256]{1,0:T(1,128)S(1)}, bf16[768,1024]{1,0:T(8,128)(2,1)S(...) custom-call(bf16[1536,512]{1,0:T(8,128)(2,1)S(1)} %copy-done.31, ...), custom_call_target="tpu_custom_call", output_to_operand_aliasing={{3}: (8, {}), {4}: (9, {}), {5}: (10, {})} | custom-call | flops 1000000 | bytes 1000000 | tf_op jit(solution)/shard_map/ungate_rows/pallas_call | solution.py:541
  277.9 2.8 weight_grad.4
  280.9 1.9 collective-permute-done.32.refs_3_
  285.0 4.9 %all-to-all-start.1 = ((bf16[4,4,32,2816]{3,2,1,0:T(8,128)(2,1)}), bf16[4,4,32,2816]{3,2,1,0:T(8,128)(2,1)}, u32[]{:S(2)}, u32[]{:S(2)}) async-start(bf16[4,4,32,2816]{3,2,1,0:T(8,128)(2,1)} %copy-done.2), calls=%async_computation.1 | async-start | bytes 5767168 | tf_op jit(solution)/shard_map/all_to_all | solution.py:1110
  293.4 29.9 %recurrence_backward.1 = (bf16[1536,1280]{1,0:T(8,128)(2,1)}, f32[8,1024]{1,0:T(8,128)}) custom-call(bf16[1536,1024]{1,0:T(8,128)(2,1)} %get-tuple-element.83.edge_ref.proj_ref, bf16[1536,1024]{1,0:T(8,128)(2,1)} %get-tuple-element.83.edge_ref.proj_ref, f32[8,1024]{1,0:T(8,128)} %select_maximum_fusion.refs_4_.conv_ref, f32[1536,128]{1,0:T(8,128)} %copy-done.5, ...), custom_call_target="tpu_custom_call" | custom-call | flops 1000000 | bytes 1000000 | tf_op jit(solution)/shard_map/recurrence_backward/pallas_call | solution.py:356
  323.4 2.1 copy-done.21
  326.2 14.9 %unpack.1 = (bf16[1536,1792]{1,0:T(8,128)(2,1)S(1)}, f32[1,1024]{1,0:T(1,128)}, bf16[4,4,32,1280]{3,2,1,0:T(8,128)(2,1)S(1)}, bf16[4,4,32,1280]{3,2,1,0:T(8,128)(2,1)}) custom-call(s32[3]{0:T(128)S(1)} %pad_add_fusion.words_ref, bf16[1536,1280]{1,0:T(8,128)(2,1)S(1)} %copy-done.21, bf16[1536,512]{1,0:T(8,128)(2,1)S(1)} %copy-done.15, ...), custom_call_target="tpu_custom_call" | custom-call | flops 1000000 | bytes 1000000 | tf_op jit(solution)/shard_map/unpack/pallas_call | solution.py:651
  341.1 2.4 copy-done.18
  344.6 12.0 %unproject.1 = (bf16[384,1024]{1,0:T(8,128)(2,1)}, bf16[384,1024]{1,0:T(8,128)(2,1)}, bf16[384,1024]{1,0:T(8,128)(2,1)}, bf16[384,1024]{1,0:T(8,128)(2,1)}) custom-call(bf16[1536,1792]{1,0:T(8,128)(2,1)} %copy-done.18, bf16[1024,1664]{1,0:T(8,128)(2,1)} %get-tuple-element.126.refs_2_.w_ref), custom_call_target="tpu_custom_call" | custom-call | flops 1000000 | bytes 1000000 | tf_op jit(solution)/shard_map/unproject/pallas_call | solution.py:694
  356.7 4.8 %collective-permute-done.29.refs_2_ = bf16[768,1024]{1,0:T(8,128)(2,1)} collective-permute-done((bf16[768,1024]{1,0:T(8,128)(2,1)}, bf16[768,1024]{1,0:T(8,128)(2,1)}, u32[]{:S(2)}, u32[]{:S(2)}) %collective-permute-start.29) | collective-permute-done | bytes 1572896 | tf_op jit(solution)/shard_map/ppermute | solution.py:1071
  361.5 5.8 %weight_grad.5 = (bf16[4,4,32,512]{3,2,1,0:T(8,128)(2,1)}, bf16[4,4,32,512]{3,2,1,0:T(8,128)(2,1)}) custom-call(s32[3]{0:T(128)} %copy-done.51, bf16[384,1024]{1,0:T(8,128)(2,1)} %copy-done.29, bf16[768,1024]{1,0:T(8,128)(2,1)} %collective-permute-done.28.refs_1_, bf16[768,1024]{1,0:T(8,128)(2,1)} %collective-permute-done.29.refs_2_, ...), custom_call_target="tpu_custom_call" | custom-call | flops 1000000 | bytes 1000000 | tf_op jit(solution)/shard_map/weight_grad/pallas_call | solution.py:776
  367.3 2.1 collective-permute-done.37.refs_3_
  372.2 5.0 %all-to-all-start.2 = ((bf16[4,4,32,1792]{3,2,1,0:T(8,128)(2,1)}), bf16[4,4,32,1792]{3,2,1,0:T(8,128)(2,1)S(1)}, u32[]{:S(2)}, u32[]{:S(2)}) async-start(bf16[4,4,32,1792]{3,2,1,0:T(8,128)(2,1)} %joined.3.refs_1_), calls=%async_computation.2 | async-start | bytes 3670016 | tf_op jit(solution)/shard_map/all_to_all | solution.py:1110
  380.8 2.2 row_sums.2.refs_4_
  383.0 14.9 %collective-permute-done.33.refs_1_ = bf16[384,1024]{1,0:T(8,128)(2,1)S(1)} collective-permute-done((bf16[384,1024]{1,0:T(8,128)(2,1)}, bf16[384,1024]{1,0:T(8,128)(2,1)S(1)}, u32[]{:S(2)}, u32[]{:S(2)}) %collective-permute-start.33) | collective-permute-done | bytes 786464 | tf_op jit(solution)/shard_map/ppermute | solution.py:1071
  397.9 16.0 %collective-permute-done.34.refs_2_ = bf16[384,1024]{1,0:T(8,128)(2,1)S(1)} collective-permute-done((bf16[384,1024]{1,0:T(8,128)(2,1)}, bf16[384,1024]{1,0:T(8,128)(2,1)S(1)}, u32[]{:S(2)}, u32[]{:S(2)}) %collective-permute-start.34) | collective-permute-done | bytes 786464 | tf_op jit(solution)/shard_map/ppermute | solution.py:1071
  415.7 4.4 all-to-all-done.2.refs_1_
  422.7 3.7 all-to-all-start.3
  426.3 3.2 fusion.12
  429.5 11.3 %all-to-all-done.3.pieces_ref = bf16[4,32,4608]{2,1,0:T(8,128)(2,1)S(1)} async-done(((bf16[4,32,4608]{2,1,0:T(8,128)(2,1)}), bf16[4,32,4608]{2,1,0:T(8,128)(2,1)S(1)}, u32[]{:S(2)}, u32[]{:S(2)}) %all-to-all-start.3) | async-done | bytes 1179680 | tf_op jit(solution)/shard_map/all_to_all | solution.py:1201
  (303 shorter events, 93.1 us)
Async XLA Ops:
  7.2 73.3 %all-gather.5.cloned.1.call-start = ((), (), s32[]{:S(2)}) async-start(), calls=%async_computation.4 | async-start | bytes 3833856 | tf_op jit(solution)/shard_map/all_gather | solution.py:1318
  13.7 6.3 %collective-permute-start = (bf16[32,1664]{1,0:T(8,128)(2,1)S(1)}, bf16[32,1664]{1,0:T(8,128)(2,1)S(1)}, u32[]{:S(2)}, u32[]{:S(2)}) collective-permute-start(bf16[32,1664]{1,0:T(8,128)(2,1)S(1)} %get-tuple-element.207), channel_id=1, source_target_pairs={{0,8},{8,0},{16,24},{24,16},{1,9},{9,1},{17,25},{25,17},{2,10},{10... | collective-permute-start | bytes 319496 | tf_op jit(solution)/shard_map/ppermute | solution.py:1071
  16.7 5.8 %collective-permute-start.1 = (bf16[32,1664]{1,0:T(8,128)(2,1)S(1)}, bf16[32,1664]{1,0:T(8,128)(2,1)S(1)}, u32[]{:S(2)}, u32[]{:S(2)}) collective-permute-start(bf16[32,1664]{1,0:T(8,128)(2,1)S(1)} %get-tuple-element.206), channel_id=1, source_target_pairs={{0,16},{8,24},{16,0},{24,8},{1,17},{9,25},{17,1},{25,9},{2,18},{10... | collective-permute-start | bytes 319496 | tf_op jit(solution)/shard_map/ppermute | solution.py:1071
  18.2 5.6 %collective-permute-start.2 = (bf16[32,1664]{1,0:T(8,128)(2,1)S(1)}, bf16[32,1664]{1,0:T(8,128)(2,1)S(1)}, u32[]{:S(2)}, u32[]{:S(2)}) collective-permute-start(bf16[32,1664]{1,0:T(8,128)(2,1)S(1)} %get-tuple-element.205), channel_id=1, source_target_pairs={{0,24},{8,16},{16,8},{24,0},{1,25},{9,17},{17,9},{25,1},{2,26},{10... | collective-permute-start | bytes 319496 | tf_op jit(solution)/shard_map/ppermute | solution.py:1071
  24.7 140.8 %all-gather.7.cloned.1.call-start = ((), (), s32[]{:S(2)}) async-start(), calls=%async_computation.5 | async-start | bytes 5308416 | tf_op jit(solution)/shard_map/all_gather | solution.py:1360
  25.7 9.0 %collective-permute-start.3 = (bf16[32,2432]{1,0:T(8,128)(2,1)S(1)}, bf16[32,2432]{1,0:T(8,128)(2,1)S(1)}, u32[]{:S(2)}, u32[]{:S(2)}) collective-permute-start(bf16[32,2432]{1,0:T(8,128)(2,1)S(1)} %get-tuple-element.203), channel_id=1, source_target_pairs={{0,8},{8,0},{16,24},{24,16},{1,9},{9,1},{17,25},{25,17},{2,10},{10... | collective-permute-start | bytes 466952 | tf_op jit(solution)/shard_map/ppermute | solution.py:1071
  26.6 9.6 %collective-permute-start.4 = (bf16[32,2432]{1,0:T(8,128)(2,1)S(1)}, bf16[32,2432]{1,0:T(8,128)(2,1)S(1)}, u32[]{:S(2)}, u32[]{:S(2)}) collective-permute-start(bf16[32,2432]{1,0:T(8,128)(2,1)S(1)} %get-tuple-element.202), channel_id=1, source_target_pairs={{0,16},{8,24},{16,0},{24,8},{1,17},{9,25},{17,1},{25,9},{2,18},{10... | collective-permute-start | bytes 466952 | tf_op jit(solution)/shard_map/ppermute | solution.py:1071
  27.5 8.8 %collective-permute-start.5 = (bf16[32,2432]{1,0:T(8,128)(2,1)S(1)}, bf16[32,2432]{1,0:T(8,128)(2,1)S(1)}, u32[]{:S(2)}, u32[]{:S(2)}) collective-permute-start(bf16[32,2432]{1,0:T(8,128)(2,1)S(1)} %get-tuple-element.201), channel_id=1, source_target_pairs={{0,24},{8,16},{16,8},{24,0},{1,25},{9,17},{17,9},{25,1},{2,26},{10... | collective-permute-start | bytes 466952 | tf_op jit(solution)/shard_map/ppermute | solution.py:1071
  29.3 11.4 %collective-permute-start.6 = (bf16[32,2048]{1,0:T(8,128)(2,1)S(1)}, bf16[32,2048]{1,0:T(8,128)(2,1)}, u32[]{:S(2)}, u32[]{:S(2)}) collective-permute-start(bf16[32,2048]{1,0:T(8,128)(2,1)S(1)} %bitcast.155), channel_id=1, source_target_pairs={{0,2},{1,3},{2,0},{3,1},{4,6},{5,7},{6,4},{7,5},{8,10},{9,11},{10,... | collective-permute-start | bytes 393224 | tf_op jit(solution)/shard_map/ppermute | solution.py:1071
  30.9 16.1 %collective-permute-start.7 = (bf16[32,2048]{1,0:T(8,128)(2,1)S(1)}, bf16[32,2048]{1,0:T(8,128)(2,1)}, u32[]{:S(2)}, u32[]{:S(2)}) collective-permute-start(bf16[32,2048]{1,0:T(8,128)(2,1)S(1)} %bitcast.156), channel_id=1, source_target_pairs={{0,4},{1,5},{2,6},{3,7},{4,0},{5,1},{6,2},{7,3},{8,12},{9,13},{10,... | collective-permute-start | bytes 393224 | tf_op jit(solution)/shard_map/ppermute | solution.py:1071
  33.5 289.8 %copy-start.51 = (s32[3]{0:T(128)}, s32[3]{0:T(128)S(1)}, u32[]{:S(2)}) copy-start(s32[3]{0:T(128)S(1)} %pad_add_fusion.words_ref) | copy-start | bytes 40
  34.7 12.2 %collective-permute-start.8 = (bf16[32,2048]{1,0:T(8,128)(2,1)S(1)}, bf16[32,2048]{1,0:T(8,128)(2,1)S(1)}, u32[]{:S(2)}, u32[]{:S(2)}) collective-permute-start(bf16[32,2048]{1,0:T(8,128)(2,1)S(1)} %bitcast.157), channel_id=1, source_target_pairs={{0,6},{1,7},{2,4},{3,5},{4,2},{5,3},{6,0},{7,1},{8,14},{9,15},{10,... | collective-permute-start | bytes 393224 | tf_op jit(solution)/shard_map/ppermute | solution.py:1071
  38.4 32.2 %collective-permute-start.10 = (bf16[384,1024]{1,0:T(8,128)(2,1)S(1)}, bf16[384,1024]{1,0:T(8,128)(2,1)S(1)}, u32[]{:S(2)}, u32[]{:S(2)}) collective-permute-start(bf16[384,1024]{1,0:T(8,128)(2,1)S(1)} %broadcast_add_fusion.1.refs_0_), channel_id=1, source_target_pairs={{0,16},{8,24},{16,0},{24,8},{1,17},{9,25},{17,1},{25,9},{2,18},{10... | collective-permute-start | bytes 2359304 | tf_op jit(solution)/shard_map/ppermute | solution.py:1071
  38.9 31.7 %collective-permute-start.11 = (bf16[384,1024]{1,0:T(8,128)(2,1)S(1)}, bf16[384,1024]{1,0:T(8,128)(2,1)}, u32[]{:S(2)}, u32[]{:S(2)}) collective-permute-start(bf16[384,1024]{1,0:T(8,128)(2,1)S(1)} %broadcast_add_fusion.1.refs_0_), channel_id=1, source_target_pairs={{0,24},{8,16},{16,8},{24,0},{1,25},{9,17},{17,9},{25,1},{2,26},{10... | collective-permute-start | bytes 2359304 | tf_op jit(solution)/shard_map/ppermute | solution.py:1071
  40.6 31.4 %collective-permute-start.9 = (bf16[384,1024]{1,0:T(8,128)(2,1)S(1)}, bf16[384,1024]{1,0:T(8,128)(2,1)}, u32[]{:S(2)}, u32[]{:S(2)}) collective-permute-start(bf16[384,1024]{1,0:T(8,128)(2,1)S(1)} %broadcast_add_fusion.1.refs_0_), channel_id=1, source_target_pairs={{0,8},{8,0},{16,24},{24,16},{1,9},{9,1},{17,25},{25,17},{2,10},{10... | collective-permute-start | bytes 2359304 | tf_op jit(solution)/shard_map/ppermute | solution.py:1071
  72.8 57.5 %collective-permute-start.12 = (bf16[384,1024]{1,0:T(8,128)(2,1)}, bf16[384,1024]{1,0:T(8,128)(2,1)}, u32[]{:S(2)}, u32[]{:S(2)}) collective-permute-start(bf16[384,1024]{1,0:T(8,128)(2,1)} %get-tuple-element.90.refs_8_), channel_id=1, source_target_pairs={{0,8},{8,0},{16,24},{24,16},{1,9},{9,1},{17,25},{25,17},{2,10},{10... | collective-permute-start | bytes 2359304 | tf_op jit(solution)/shard_map/ppermute | solution.py:1071
  74.1 56.2 %collective-permute-start.13 = (bf16[384,1024]{1,0:T(8,128)(2,1)}, bf16[384,1024]{1,0:T(8,128)(2,1)}, u32[]{:S(2)}, u32[]{:S(2)}) collective-permute-start(bf16[384,1024]{1,0:T(8,128)(2,1)} %get-tuple-element.90.refs_8_), channel_id=1, source_target_pairs={{0,16},{8,24},{16,0},{24,8},{1,17},{9,25},{17,1},{25,9},{2,18},{10... | collective-permute-start | bytes 2359304 | tf_op jit(solution)/shard_map/ppermute | solution.py:1071
  75.2 55.2 %collective-permute-start.14 = (bf16[384,1024]{1,0:T(8,128)(2,1)}, bf16[384,1024]{1,0:T(8,128)(2,1)}, u32[]{:S(2)}, u32[]{:S(2)}) collective-permute-start(bf16[384,1024]{1,0:T(8,128)(2,1)} %get-tuple-element.90.refs_8_), channel_id=1, source_target_pairs={{0,24},{8,16},{16,8},{24,0},{1,25},{9,17},{17,9},{25,1},{2,26},{10... | collective-permute-start | bytes 2359304 | tf_op jit(solution)/shard_map/ppermute | solution.py:1071
  76.4 54.4 %all-to-all-start = ((bf16[4,4,32,2048]{3,2,1,0:T(8,128)(2,1)}), bf16[4,4,32,2048]{3,2,1,0:T(8,128)(2,1)S(1)}, u32[]{:S(2)}, u32[]{:S(2)}) async-start(bf16[4,4,32,2048]{3,2,1,0:T(8,128)(2,1)} %get-tuple-element.89), calls=%async_computation | async-start | bytes 4194304 | tf_op jit(solution)/shard_map/all_to_all | solution.py:1362
  138.5 4.2 collective-permute-start.15
  138.6 12.0 %collective-permute-start.16 = (bf16[384,512]{1,0:T(8,128)(2,1)S(1)}, bf16[384,512]{1,0:T(8,128)(2,1)S(1)}, u32[]{:S(2)}, u32[]{:S(2)}) collective-permute-start(bf16[384,512]{1,0:T(8,128)(2,1)S(1)} %get-tuple-element.95.refs_5_), channel_id=1, source_target_pairs={{0,8},{8,0},{16,24},{24,16},{1,9},{9,1},{17,25},{25,17},{2,10},{10... | collective-permute-start | bytes 1179656 | tf_op jit(solution)/shard_map/ppermute | solution.py:1071
  140.2 19.6 %collective-permute-start.17 = (bf16[384,512]{1,0:T(8,128)(2,1)S(1)}, bf16[384,512]{1,0:T(8,128)(2,1)S(1)}, u32[]{:S(2)}, u32[]{:S(2)}) collective-permute-start(bf16[384,512]{1,0:T(8,128)(2,1)S(1)} %get-tuple-element.96.refs_6_), channel_id=1, source_target_pairs={{0,16},{8,24},{16,0},{24,8},{1,17},{9,25},{17,1},{25,9},{2,18},{10... | collective-permute-start | bytes 1179656 | tf_op jit(solution)/shard_map/ppermute | solution.py:1071
  141.7 18.1 %collective-permute-start.18 = (bf16[384,512]{1,0:T(8,128)(2,1)S(1)}, bf16[384,512]{1,0:T(8,128)(2,1)S(1)}, u32[]{:S(2)}, u32[]{:S(2)}) collective-permute-start(bf16[384,512]{1,0:T(8,128)(2,1)S(1)} %get-tuple-element.97.refs_7_), channel_id=1, source_target_pairs={{0,24},{8,16},{16,8},{24,0},{1,25},{9,17},{17,9},{25,1},{2,26},{10... | collective-permute-start | bytes 1179656 | tf_op jit(solution)/shard_map/ppermute | solution.py:1071
  161.9 86.3 %copy-start.16 = (f32[384,1024]{1,0:T(8,128)}, f32[384,1024]{1,0:T(8,128)S(1)}, u32[]{:S(2)}) copy-start(f32[384,1024]{1,0:T(8,128)S(1)} %get-tuple-element.98.residual_ref) | copy-start | bytes 4718596
  161.9 20.5 %collective-permute-start.19 = (bf16[384,1024]{1,0:T(8,128)(2,1)S(1)}, bf16[384,1024]{1,0:T(8,128)(2,1)S(1)}, u32[]{:S(2)}, u32[]{:S(2)}) collective-permute-start(bf16[384,1024]{1,0:T(8,128)(2,1)S(1)} %get-tuple-element.100.refs_0_), channel_id=1, source_target_pairs={{0,8},{8,0},{16,24},{24,16},{1,9},{9,1},{17,25},{25,17},{2,10},{10... | collective-permute-start | bytes 2359304 | tf_op jit(solution)/shard_map/ppermute | solution.py:1071
  163.2 37.2 %collective-permute-start.22 = (bf16[384,1024]{1,0:T(8,128)(2,1)S(1)}, bf16[384,1024]{1,0:T(8,128)(2,1)}, u32[]{:S(2)}, u32[]{:S(2)}) collective-permute-start(bf16[384,1024]{1,0:T(8,128)(2,1)S(1)} %get-tuple-element.100.refs_0_), channel_id=1, source_target_pairs={{0,24},{8,16},{16,8},{24,0},{1,25},{9,17},{17,9},{25,1},{2,26},{10... | collective-permute-start | bytes 2359304 | tf_op jit(solution)/shard_map/ppermute | solution.py:1071
  165.0 44.3 %collective-permute-start.21 = (bf16[384,1024]{1,0:T(8,128)(2,1)S(1)}, bf16[384,1024]{1,0:T(8,128)(2,1)}, u32[]{:S(2)}, u32[]{:S(2)}) collective-permute-start(bf16[384,1024]{1,0:T(8,128)(2,1)S(1)} %get-tuple-element.100.refs_0_), channel_id=1, source_target_pairs={{0,16},{8,24},{16,0},{24,8},{1,17},{9,25},{17,1},{25,9},{2,18},{10... | collective-permute-start | bytes 2359304 | tf_op jit(solution)/shard_map/ppermute | solution.py:1071
  188.0 28.5 %collective-permute-start.20 = (bf16[384,1024]{1,0:T(8,128)(2,1)S(1)}, bf16[384,1024]{1,0:T(8,128)(2,1)S(1)}, u32[]{:S(2)}, u32[]{:S(2)}) collective-permute-start(bf16[384,1024]{1,0:T(8,128)(2,1)S(1)} %convolution_convert_fusion.2), channel_id=1, source_target_pairs={{0,8},{8,0},{16,24},{24,16},{1,9},{9,1},{17,25},{25,17},{2,10},{10... | collective-permute-start | bytes 2359304 | tf_op jit(solution)/shard_map/ppermute | solution.py:1071
  207.3 40.9 %collective-permute-start.24 = (bf16[384,1024]{1,0:T(8,128)(2,1)S(1)}, bf16[384,1024]{1,0:T(8,128)(2,1)S(1)}, u32[]{:S(2)}, u32[]{:S(2)}) collective-permute-start(bf16[384,1024]{1,0:T(8,128)(2,1)S(1)} %convolution_convert_fusion.1), channel_id=1, source_target_pairs={{0,24},{8,16},{16,8},{24,0},{1,25},{9,17},{17,9},{25,1},{2,26},{10... | collective-permute-start | bytes 2359304 | tf_op jit(solution)/shard_map/ppermute | solution.py:1071
  215.4 32.8 %collective-permute-start.23 = (bf16[384,1024]{1,0:T(8,128)(2,1)S(1)}, bf16[384,1024]{1,0:T(8,128)(2,1)S(1)}, u32[]{:S(2)}, u32[]{:S(2)}) collective-permute-start(bf16[384,1024]{1,0:T(8,128)(2,1)S(1)} %convolution_convert_fusion.refs_16_), channel_id=1, source_target_pairs={{0,16},{8,24},{16,0},{24,8},{1,17},{9,25},{17,1},{25,9},{2,18},{10... | collective-permute-start | bytes 2359304 | tf_op jit(solution)/shard_map/ppermute | solution.py:1071
  252.3 30.5 %collective-permute-start.31 = (bf16[4,4,32,2304]{3,2,1,0:T(8,128)(2,1)S(1)}, bf16[4,4,32,2304]{3,2,1,0:T(8,128)(2,1)S(1)}, u32[]{:S(2)}, u32[]{:S(2)}) collective-permute-start(bf16[4,4,32,2304]{3,2,1,0:T(8,128)(2,1)S(1)} %get-tuple-element.124), channel_id=1, source_target_pairs={{0,1},{1,0},{2,3},{3,2},{4,5},{5,4},{6,7},{7,6},{8,9},{9,8},{10,11... | collective-permute-start | bytes 7077896 | tf_op jit(solution)/shard_map/ppermute | solution.py:1071
  252.3 11.9 %collective-permute-start.25 = (bf16[384,512]{1,0:T(8,128)(2,1)S(1)}, bf16[384,512]{1,0:T(8,128)(2,1)S(1)}, u32[]{:S(2)}, u32[]{:S(2)}) collective-permute-start(bf16[384,512]{1,0:T(8,128)(2,1)S(1)} %get-tuple-element.106), channel_id=1, source_target_pairs={{0,8},{8,0},{16,24},{24,16},{1,9},{9,1},{17,25},{25,17},{2,10},{10... | collective-permute-start | bytes 1179656 | tf_op jit(solution)/shard_map/ppermute | solution.py:1071
  252.8 19.7 %collective-permute-start.26 = (bf16[384,512]{1,0:T(8,128)(2,1)S(1)}, bf16[384,512]{1,0:T(8,128)(2,1)S(1)}, u32[]{:S(2)}, u32[]{:S(2)}) collective-permute-start(bf16[384,512]{1,0:T(8,128)(2,1)S(1)} %get-tuple-element.107), channel_id=1, source_target_pairs={{0,16},{8,24},{16,0},{24,8},{1,17},{9,25},{17,1},{25,9},{2,18},{10... | collective-permute-start | bytes 1179656 | tf_op jit(solution)/shard_map/ppermute | solution.py:1071
  254.4 18.1 %collective-permute-start.27 = (bf16[384,512]{1,0:T(8,128)(2,1)S(1)}, bf16[384,512]{1,0:T(8,128)(2,1)S(1)}, u32[]{:S(2)}, u32[]{:S(2)}) collective-permute-start(bf16[384,512]{1,0:T(8,128)(2,1)S(1)} %get-tuple-element.108), channel_id=1, source_target_pairs={{0,24},{8,16},{16,8},{24,0},{1,25},{9,17},{17,9},{25,1},{2,26},{10... | collective-permute-start | bytes 1179656 | tf_op jit(solution)/shard_map/ppermute | solution.py:1071
  280.9 1.9 collective-permute-start.32
  285.0 76.4 %all-to-all-start.1 = ((bf16[4,4,32,2816]{3,2,1,0:T(8,128)(2,1)}), bf16[4,4,32,2816]{3,2,1,0:T(8,128)(2,1)}, u32[]{:S(2)}, u32[]{:S(2)}) async-start(bf16[4,4,32,2816]{3,2,1,0:T(8,128)(2,1)} %copy-done.2), calls=%async_computation.1 | async-start | bytes 5767168 | tf_op jit(solution)/shard_map/all_to_all | solution.py:1110
  289.9 66.7 %collective-permute-start.28 = (bf16[768,1024]{1,0:T(8,128)(2,1)}, bf16[768,1024]{1,0:T(8,128)(2,1)}, u32[]{:S(2)}, u32[]{:S(2)}) collective-permute-start(bf16[768,1024]{1,0:T(8,128)(2,1)} %copy-done.33), channel_id=1, source_target_pairs={{0,8},{8,0},{16,24},{24,16},{1,9},{9,1},{17,25},{25,17},{2,10},{10... | collective-permute-start | bytes 4718600 | tf_op jit(solution)/shard_map/ppermute | solution.py:1071
  291.5 70.0 %collective-permute-start.29 = (bf16[768,1024]{1,0:T(8,128)(2,1)}, bf16[768,1024]{1,0:T(8,128)(2,1)}, u32[]{:S(2)}, u32[]{:S(2)}) collective-permute-start(bf16[768,1024]{1,0:T(8,128)(2,1)} %copy-done.34), channel_id=1, source_target_pairs={{0,16},{8,24},{16,0},{24,8},{1,17},{9,25},{17,1},{25,9},{2,18},{10... | collective-permute-start | bytes 4718600 | tf_op jit(solution)/shard_map/ppermute | solution.py:1071
  292.0 69.5 %collective-permute-start.30 = (bf16[768,1024]{1,0:T(8,128)(2,1)}, bf16[768,1024]{1,0:T(8,128)(2,1)}, u32[]{:S(2)}, u32[]{:S(2)}) collective-permute-start(bf16[768,1024]{1,0:T(8,128)(2,1)} %copy-done.35), channel_id=1, source_target_pairs={{0,24},{8,16},{16,8},{24,0},{1,25},{9,17},{17,9},{25,1},{2,26},{10... | collective-permute-start | bytes 4718600 | tf_op jit(solution)/shard_map/ppermute | solution.py:1071
  344.6 22.7 %collective-permute-start.36 = (bf16[4,4,32,1280]{3,2,1,0:T(8,128)(2,1)}, bf16[4,4,32,1280]{3,2,1,0:T(8,128)(2,1)S(1)}, u32[]{:S(2)}, u32[]{:S(2)}) collective-permute-start(bf16[4,4,32,1280]{3,2,1,0:T(8,128)(2,1)} %get-tuple-element.141), channel_id=1, source_target_pairs={{0,1},{1,0},{2,3},{3,2},{4,5},{5,4},{6,7},{7,6},{8,9},{9,8},{10,11... | collective-permute-start | bytes 3932168 | tf_op jit(solution)/shard_map/ppermute | solution.py:1071
  367.3 2.1 collective-permute-start.37
  372.2 47.9 %all-to-all-start.2 = ((bf16[4,4,32,1792]{3,2,1,0:T(8,128)(2,1)}), bf16[4,4,32,1792]{3,2,1,0:T(8,128)(2,1)S(1)}, u32[]{:S(2)}, u32[]{:S(2)}) async-start(bf16[4,4,32,1792]{3,2,1,0:T(8,128)(2,1)} %joined.3.refs_1_), calls=%async_computation.2 | async-start | bytes 3670016 | tf_op jit(solution)/shard_map/all_to_all | solution.py:1110
  377.2 20.6 %collective-permute-start.33 = (bf16[384,1024]{1,0:T(8,128)(2,1)}, bf16[384,1024]{1,0:T(8,128)(2,1)S(1)}, u32[]{:S(2)}, u32[]{:S(2)}) collective-permute-start(bf16[384,1024]{1,0:T(8,128)(2,1)} %get-tuple-element.137), channel_id=1, source_target_pairs={{0,8},{8,0},{16,24},{24,16},{1,9},{9,1},{17,25},{25,17},{2,10},{10... | collective-permute-start | bytes 2359304 | tf_op jit(solution)/shard_map/ppermute | solution.py:1071
  377.8 36.1 %collective-permute-start.34 = (bf16[384,1024]{1,0:T(8,128)(2,1)}, bf16[384,1024]{1,0:T(8,128)(2,1)S(1)}, u32[]{:S(2)}, u32[]{:S(2)}) collective-permute-start(bf16[384,1024]{1,0:T(8,128)(2,1)} %get-tuple-element.138), channel_id=1, source_target_pairs={{0,16},{8,24},{16,0},{24,8},{1,17},{9,25},{17,1},{25,9},{2,18},{10... | collective-permute-start | bytes 2359304 | tf_op jit(solution)/shard_map/ppermute | solution.py:1071
  379.3 34.6 %copy-start.28 = (bf16[384,1024]{1,0:T(8,128)(2,1)S(1)}, bf16[384,1024]{1,0:T(8,128)(2,1)}, u32[]{:S(2)}) copy-start(bf16[384,1024]{1,0:T(8,128)(2,1)} %get-tuple-element.136.refs_8_.refs_0_) | copy-start | bytes 2359300
  379.3 34.6 %copy-start.38 = (f32[384,1024]{1,0:T(8,128)S(1)}, f32[384,1024]{1,0:T(8,128)}, u32[]{:S(2)}) copy-start(f32[384,1024]{1,0:T(8,128)} %copy-done.37) | copy-start | bytes 4718596
  379.3 34.6 %collective-permute-start.35 = (bf16[384,1024]{1,0:T(8,128)(2,1)S(1)}, bf16[384,1024]{1,0:T(8,128)(2,1)S(1)}, u32[]{:S(2)}, u32[]{:S(2)}) collective-permute-start(bf16[384,1024]{1,0:T(8,128)(2,1)S(1)} %copy-done.70), channel_id=1, source_target_pairs={{0,24},{8,16},{16,8},{24,0},{1,25},{9,17},{17,9},{25,1},{2,26},{10... | collective-permute-start | bytes 2359304 | tf_op jit(solution)/shard_map/ppermute | solution.py:1071
  422.7 18.2 %all-to-all-start.3 = ((bf16[4,32,4608]{2,1,0:T(8,128)(2,1)}), bf16[4,32,4608]{2,1,0:T(8,128)(2,1)S(1)}, u32[]{:S(2)}, u32[]{:S(2)}) async-start(bf16[4,32,4608]{2,1,0:T(8,128)(2,1)} %copy-done.20), calls=%async_computation.3 | async-start | bytes 2359296 | tf_op jit(solution)/shard_map/all_to_all | solution.py:1201
  (67 other events, 602.7 us)
Sparse Core Ops, SparseCore 0:
  24.8 47.0 all-gather.4
  74.1 50.9 all-gather.6
